TPU v7x, 32 devices: a whole 2x2x4 slice. The times are simulated.
32 devices in a mesh: gx: 4 (over x, core), gy: 8 (over z, y).
Axes of the slice: x: 2, y: 2, z: 4, core: 2. Of those that a mesh axis runs over, the one named last changes fastest.
Arguments:
- stem_first: float32 [4, 1024, 1024], P('gx', 'gy'), may hold values from -6 to 6
- cotangent: float32 [4, 1024, 1024], P('gx', 'gy'), may hold values from -6 to 6
- branch_first: float32 [1024, 1024], P(('gx', 'gy')), may hold values from -0.1875 to 0.1875
- branch_second: float32 [1024, 1024], P(('gx', 'gy')), may hold values from -0.1875 to 0.1875
- bond_first: int32 [1024], replicated, may hold values from 0 to 1023, each once
- bond_second: int32 [1024], replicated, may hold values from 0 to 1023, each once
Outputs:
- grad_stem: float32 [4, 1024, 1024], P('gx', 'gy')
- grad_first: float32 [1024, 1024], P(('gx', 'gy'))
- grad_second: float32 [1024, 1024], P(('gx', 'gy'))
Inputs may be any that keep to these rules, and one draw needn't show every extreme that they name: `bond_first`: each a permutation of the numbers below 1024. `bond_second`: each a permutation of the numbers below 1024.
All inputs are finite; a program needn't handle non-finite values.
Results may differ from a plain program's by a relative error of at most 0.000098.
Values sent between devices are 32-bit elements; how exact they have to be, the bound alone decides.
No kernel may reach another device: no remote copies, remote signals or barrier semaphores. Data moves between devices by JAX's collectives and lax.ppermute only.
A program may use at most 64 MiB of HBM per device.

v0:
```python
import jax
import jax.numpy as jnp
from jax import lax
from jax.sharding import PartitionSpec as P


def inverse(ordering):
    return jnp.zeros_like(ordering).at[ordering].set(jnp.arange(ordering.shape[0], dtype=jnp.int32))


def product(left, right):
    return jnp.dot(left, right, precision=lax.Precision.HIGHEST, preferred_element_type=jnp.float32)


def column_product(picked, other):
    return lax.dot_general(
        picked,
        other,
        (((0,), (0,)), ((), ())),
        precision=lax.Precision.HIGHEST,
        preferred_element_type=jnp.float32,
    )


def gradient_rows(columns, ordering, other):
    picked = jnp.take(columns, ordering, axis=1)
    return column_product(picked, other)


def on_device(stem_first, cotangent, branch_first, branch_second, bond_first, bond_second):
    full_first, full_second = (
        lax.all_gather(branch_first, ("gx", "gy"), axis=0, tiled=True),
        lax.all_gather(branch_second, ("gx", "gy"), axis=0, tiled=True),
    )
    groups = lax.axis_size("gx")
    devices = groups * lax.axis_size("gy")
    height = stem_first.shape[1]
    width = stem_first.shape[2]
    factor = 1.0 / jnp.sqrt(jnp.float32(height * devices))
    placed_first = full_first[inverse(bond_first)]
    placed_second = full_second[inverse(bond_second)]
    stem_rows = stem_first.reshape(height, width)
    cotan_rows = cotangent.reshape(height, width)
    stem_mid = product(stem_rows, placed_first)
    regrouped = lax.all_to_all(
        stem_mid.reshape(height, groups, width // groups),
        "gx",
        split_axis=1,
        concat_axis=1,
        tiled=True,
    ).reshape(height, width)
    back_regrouped = product(cotan_rows, placed_second.T)
    outer_second = lax.psum_scatter(
        gradient_rows(regrouped, bond_second, cotan_rows), "gx", scatter_dimension=0, tiled=True
    )
    grad_second = lax.psum_scatter(outer_second, "gy", scatter_dimension=0, tiled=True)
    back_mid = lax.all_to_all(
        back_regrouped.reshape(height, groups, width // groups),
        "gx",
        split_axis=1,
        concat_axis=1,
        tiled=True,
    ).reshape(height, width)
    outer_first = lax.psum_scatter(
        gradient_rows(stem_rows, bond_first, back_mid), "gx", scatter_dimension=0, tiled=True
    )
    grad_first = lax.psum_scatter(outer_first, "gy", scatter_dimension=0, tiled=True)
    grad_stem = product(back_mid, placed_first.T).reshape(1, height, width)
    return (grad_stem, grad_first * factor, grad_second * factor)


def solution(mesh):
    return jax.shard_map(
        on_device,
        mesh=mesh,
        in_specs=(
            P("gx", "gy", None),
            P("gx", "gy", None),
            P(("gx", "gy"), None),
            P(("gx", "gy"), None),
            P(),
            P(),
        ),
        out_specs=(P("gx", "gy", None), P(("gx", "gy"), None), P(("gx", "gy"), None)),
        check_vma=False,
    )
```

profile of v0, /device:TPU:0, one launch (start us, length us, event | category | flops | bytes accessed | tf_op | source)
XLA Modules:
  0.0 379.1 jit_solution(7321081563209456585)
XLA Ops:
  7.2 0.0 copy-start
  7.2 0.0 all-gather.3.cloned.1.call-start
  7.2 0.7 all-gather.3.cloned.1.call-update
  7.9 0.0 all-gather.5.cloned.1.call-start
  8.0 0.7 all-gather.5.cloned.1.call-update
  8.7 1.2 copy.9
  9.9 0.7 broadcast_clamp_fusion
  10.6 4.3 %scatter_custom_fusion = s32[1024]{0:T(1024)S(1)} fusion(s32[1024]{0:T(1024)S(1)} %get-tuple-element.5, s32[1024]{0:T(1024)S(1)} %iota.6, s32[]{:T(128)} %constant.1.clone.1), kind=kCustom, calls=%fused_computation.36 | custom fusion | bytes 4100 | tf_op jit(solution)/shard_map/scatter | solution.py:8
  14.9 61.0 %all-gather.3.cloned.1.call-done = f32[1024,1024]{1,0:T(8,128)} async-done(((f32[32,1024]{1,0:T(8,128)}), f32[1024,1024]{1,0:T(8,128)}) %all-gather.3.cloned.1.call-update) | async-done | bytes 4194320 | tf_op jit(solution)/shard_map/all_gather | solution.py:33
  75.9 8.6 %gather_fusion = f32[1024,1024]{1,0:T(8,128)} fusion(f32[1024,1024]{1,0:T(8,128)} %all-gather.3.cloned.1.call-done, s32[1024]{0:T(1024)S(1)} %fusion.15), kind=kCustom, calls=%fused_computation.2 | custom fusion | bytes 8392704 | tf_op jit(solution)/shard_map/gather | solution.py:41
  84.5 0.0 copy-done
  84.5 0.0 copy-start.2
  84.5 6.5 %fusion.7 = f32[1024,128]{1,0:T(8,128)} fusion(f32[1024,1024]{1,0:T(8,128)} %gather_fusion, f32[1,128,1024]{2,1,0:T(8,128)S(1)} %copy-done), kind=kOutput, calls=%fused_computation.14 | convolution fusion | flops 1610612736 | bytes 5242880 | tf_op jit(solution)/shard_map/dot_general | solution.py:12
  91.0 3.5 all-to-all-start
  94.5 0.0 reduce-scatter.5.cloned.1.call-start
  94.5 0.0 copy-done.2
  94.5 2.8 gather_fusion.2
  97.4 5.9 %all-to-all-done = f32[128,4,256]{0,2,1:T(8,128)S(1)} async-done(((f32[128,4,256]{0,2,1:T(8,128)}), f32[128,4,256]{0,2,1:T(8,128)S(1)}, u32[]{:S(2)}, u32[]{:S(2)}) %all-to-all-start) | async-done | bytes 524320 | tf_op jit(solution)/shard_map/all_to_all | solution.py:57
  103.3 5.1 %fusion.4 = f32[1024,1024]{1,0:T(8,128)} fusion(f32[128,1024]{0,1:T(8,128)S(1)} %bitcast.32, f32[1024,128]{1,0:T(8,128)S(1)} %gather_fusion.2, pred[1024]{0:T(1024)(128)(4,1)S(1)} %compare_and_fusion.1), kind=kOutput, calls=%fused_computation.11 | convolution fusion | flops 1610743808 | bytes 5243904 | tf_op jit(solution)/shard_map/dot_general | solution.py:16
  108.4 0.0 reduce-scatter.5.cloned.1.call-update
  108.4 4.5 %scatter_custom_fusion.1 = s32[1024]{0:T(1024)S(1)} fusion(s32[1024]{0:T(1024)S(1)} %get-tuple-element.7, s32[1024]{0:T(1024)S(1)} %iota.7, s32[]{:T(128)} %constant.1.clone.1), kind=kCustom, calls=%fused_computation.34 | custom fusion | bytes 4100 | tf_op jit(solution)/shard_map/scatter | solution.py:8
  112.9 0.0 copy-start.1
  112.9 26.7 %all-gather.5.cloned.1.call-done = f32[1024,1024]{1,0:T(8,128)} async-done(((f32[32,1024]{1,0:T(8,128)}), f32[1024,1024]{1,0:T(8,128)}) %all-gather.5.cloned.1.call-update) | async-done | bytes 4194320 | tf_op jit(solution)/shard_map/all_gather | solution.py:32
  139.6 8.6 %gather_fusion.1 = f32[1024,1024]{1,0:T(8,128)} fusion(f32[1024,1024]{1,0:T(8,128)} %all-gather.5.cloned.1.call-done, s32[1024]{0:T(1024)S(1)} %fusion.16), kind=kCustom, calls=%fused_computation.3 | custom fusion | bytes 8392704 | tf_op jit(solution)/shard_map/gather | solution.py:40
  148.2 0.0 copy-done.1
  148.2 0.0 copy-start.3
  148.2 10.5 %fusion = f32[1024,128]{1,0:T(8,128)} fusion(f32[1024,1024]{1,0:T(8,128)} %gather_fusion.1, f32[1,128,1024]{2,1,0:T(8,128)S(1)} %copy-done.1), kind=kOutput, calls=%fused_computation.7 | convolution fusion | flops 1610612736 | bytes 5242880 | tf_op jit(solution)/shard_map/dot_general | solution.py:12
  158.7 3.5 all-to-all-start.1
  162.2 0.0 reduce-scatter.9.cloned.1.call-start
  162.2 0.0 copy-done.3
  162.2 14.7 %all-to-all-done.1 = f32[128,4,256]{0,2,1:T(8,128)S(1)} async-done(((f32[128,4,256]{0,2,1:T(8,128)}), f32[128,4,256]{0,2,1:T(8,128)S(1)}, u32[]{:S(2)}, u32[]{:S(2)}) %all-to-all-start.1) | async-done | bytes 524320 | tf_op jit(solution)/shard_map/all_to_all | solution.py:45
  176.9 2.8 gather_fusion.3
  179.7 5.1 %fusion.2 = f32[1024,1024]{1,0:T(8,128)} fusion(f32[1,128,1024]{2,1,0:T(8,128)S(1)} %copy-done, f32[1024,128]{1,0:T(8,128)S(1)} %gather_fusion.3, pred[1024]{0:T(1024)(128)(4,1)S(1)} %compare_and_fusion), kind=kOutput, calls=%fused_computation.9 | convolution fusion | flops 1610743808 | bytes 5243904 | tf_op jit(solution)/shard_map/dot_general | solution.py:16
  184.8 0.0 reduce-scatter.9.cloned.1.call-update
  184.8 0.0 reduce-scatter.7.cloned.1.call-start
  184.9 6.0 %reduce-scatter.5.cloned.1.call-done = f32[256,1024]{1,0:T(8,128)} async-done(((f32[1024,1024]{1,0:T(8,128)}), f32[256,1024]{1,0:T(8,128)}) %reduce-scatter.5.cloned.1.call-update) | async-done | bytes 1048592 | tf_op jit(solution)/shard_map/reduce_scatter | solution.py:64
  190.9 0.0 reduce-scatter.7.cloned.1.call-update
  190.9 0.3 reduce-scatter.11.cloned.1.call-start
  191.2 46.8 %reduce-scatter.9.cloned.1.call-done = f32[256,1024]{1,0:T(8,128)} async-done(((f32[1024,1024]{1,0:T(8,128)}), f32[256,1024]{1,0:T(8,128)}) %reduce-scatter.9.cloned.1.call-update) | async-done | bytes 1048592 | tf_op jit(solution)/shard_map/reduce_scatter | solution.py:53
  237.9 0.0 reduce-scatter.11.cloned.1.call-update
  238.0 7.5 %convolution_bitcast_fusion = f32[1,128,1024]{2,1,0:T(8,128)} fusion(f32[128,1024]{0,1:T(8,128)S(1)} %bitcast.33, f32[1024,1024]{1,0:T(8,128)} %gather_fusion.1), kind=kOutput, calls=%fused_computation.6 | convolution fusion | flops 1610612736 | bytes 5242880 | tf_op jit(solution)/shard_map/dot_general | solution.py:12
  245.4 59.3 %reduce-scatter.7.cloned.1.call-done = f32[32,1024]{1,0:T(8,128)} async-done(((f32[256,1024]{1,0:T(8,128)}), f32[32,1024]{1,0:T(8,128)}) %reduce-scatter.7.cloned.1.call-update) | async-done | bytes 131088 | tf_op jit(solution)/shard_map/reduce_scatter | solution.py:67
  304.7 1.6 broadcast_multiply_fusion.1
  306.3 64.5 %reduce-scatter.11.cloned.1.call-done = f32[32,1024]{1,0:T(8,128)} async-done(((f32[256,1024]{1,0:T(8,128)}), f32[32,1024]{1,0:T(8,128)}) %reduce-scatter.11.cloned.1.call-update) | async-done | bytes 131088 | tf_op jit(solution)/shard_map/reduce_scatter | solution.py:56
  370.7 1.6 broadcast_multiply_fusion
  (7 shorter events, 0.0 us)
Async XLA Ops:
  7.2 77.3 %copy-start = (f32[1,128,1024]{2,1,0:T(8,128)S(1)}, f32[1,128,1024]{2,1,0:T(8,128)}, u32[]{:S(2)}) copy-start(f32[1,128,1024]{2,1,0:T(8,128)} %param.9) | copy-start | bytes 1572868
  7.2 68.7 %all-gather.3.cloned.1.call-start = ((), (), s32[]{:S(2)}) async-start(), calls=%async_computation.6 | async-start | bytes 4325376 | tf_op jit(solution)/shard_map/all_gather | solution.py:33
  7.9 131.7 %all-gather.5.cloned.1.call-start = ((), (), s32[]{:S(2)}) async-start(), calls=%async_computation.7 | async-start | bytes 4325376 | tf_op jit(solution)/shard_map/all_gather | solution.py:32
  84.5 10.0 %copy-start.2 = (s32[1024]{0:T(1024)S(1)}, s32[1024]{0:T(1024)}, u32[]{:S(2)}) copy-start(s32[1024]{0:T(1024)} %param.12) | copy-start | bytes 12292
  91.0 12.3 %all-to-all-start = ((f32[128,4,256]{0,2,1:T(8,128)}), f32[128,4,256]{0,2,1:T(8,128)S(1)}, u32[]{:S(2)}, u32[]{:S(2)}) async-start(f32[128,4,256]{0,2,1:T(8,128)} %bitcast.2), calls=%async_computation | async-start | bytes 1048576 | tf_op jit(solution)/shard_map/all_to_all | solution.py:57
  94.5 96.4 %reduce-scatter.5.cloned.1.call-start = ((), (), s32[]{:S(2)}) async-start(), calls=%async_computation.8 | async-start | bytes 5242880 | tf_op jit(solution)/shard_map/reduce_scatter | solution.py:64
  112.9 35.3 %copy-start.1 = (f32[1,128,1024]{2,1,0:T(8,128)S(1)}, f32[1,128,1024]{2,1,0:T(8,128)}, u32[]{:S(2)}) copy-start(f32[1,128,1024]{2,1,0:T(8,128)} %param.8) | copy-start | bytes 1572868
  148.2 14.0 %copy-start.3 = (s32[1024]{0:T(1024)S(1)}, s32[1024]{0:T(1024)}, u32[]{:S(2)}) copy-start(s32[1024]{0:T(1024)} %param.13) | copy-start | bytes 12292
  158.7 18.2 %all-to-all-start.1 = ((f32[128,4,256]{0,2,1:T(8,128)}), f32[128,4,256]{0,2,1:T(8,128)S(1)}, u32[]{:S(2)}, u32[]{:S(2)}) async-start(f32[128,4,256]{0,2,1:T(8,128)} %bitcast.8), calls=%async_computation.3 | async-start | bytes 1048576 | tf_op jit(solution)/shard_map/all_to_all | solution.py:45
  162.2 75.8 %reduce-scatter.9.cloned.1.call-start = ((), (), s32[]{:S(2)}) async-start(), calls=%async_computation.10 | async-start | bytes 5242880 | tf_op jit(solution)/shard_map/reduce_scatter | solution.py:53
  184.8 119.9 %reduce-scatter.7.cloned.1.call-start = ((), (), s32[]{:S(2)}) async-start(), calls=%async_computation.9 | async-start | bytes 1179648 | tf_op jit(solution)/shard_map/reduce_scatter | solution.py:67
  190.9 179.8 %reduce-scatter.11.cloned.1.call-start = ((), (), s32[]{:S(2)}) async-start(), calls=%async_computation.11 | async-start | bytes 1179648 | tf_op jit(solution)/shard_map/reduce_scatter | solution.py:56
Sparse Core Ops, SparseCore 0:
  11.1 64.7 all-gather.2
  79.0 60.6 all-gather.4
  142.2 48.6 reduce-scatter.4
  193.4 44.4 reduce-scatter.8
  241.2 63.4 reduce-scatter.6
  308.3 62.3 reduce-scatter.10
where the time goes:
time: 380 us; the launch traced here: 379 us
  waiting for transfers between devices  286 us (75%)
  matrix products  34.6 us (9%)
  local copies, waits for them, and re-layouts  32.8 us (9%)
  between operations  14.2 us (4%)
  starting transfers between devices  7.4 us (2%)
  other arithmetic  3.87 us (1%)
    reduce_scatter x1, waiting for transfers between devices, on_device(): lax.psum_scatter(outer_second, 'gy', scatter_dimension=0, tiled=True)  64.5 us
    all_gather x1, waiting for transfers between devices, on_device(): lax.all_gather(branch_second, ('gx', 'gy'), axis=0, tiled=True)  61 us
    reduce_scatter x1, waiting for transfers between devices, on_device(): lax.psum_scatter(outer_first, 'gy', scatter_dimension=0, tiled=True)  59.3 us
    reduce_scatter x1, waiting for transfers between devices, on_device(): lax.psum_scatter(gradient_rows(regrouped, bond_second, cotan_rows), 'gx',...  46.8 us
    all_gather x1, waiting for transfers between devices, on_device(): lax.all_gather(branch_first, ('gx', 'gy'), axis=0, tiled=True)  26.7 us
    dot_general x3, matrix products, product(): jnp.dot(left, right, precision=lax.Precision.HIGHEST, preferred_element_t...  24.4 us
    all_to_all x1, waiting for transfers between devices, on_device(): lax.all_to_all(stem_mid.reshape(height, groups, width // groups), 'gx', s...  14.7 us
    dot_general x2, matrix products, column_product(): lax.dot_general(picked, other, (((0,), (0,)), ((), ())), precision=lax.Pr...  10.2 us
  transfers between devices with their start and end apart: 8, of which 8 were waited for; matrix products, arithmetic and copies ran while one was open for 18% of the time, Pallas kernels for 0%

commit v1 on v0

v1 whole, which is shorter than its diff:
```python
import jax
import jax.numpy as jnp
from jax import lax
from jax.sharding import PartitionSpec as P


def product(left, right, contract):
    return lax.dot_general(
        left,
        right,
        (contract, ((), ())),
        precision=lax.Precision.HIGH,
        preferred_element_type=jnp.float32,
    )


def inverse(ordering):
    return jnp.zeros_like(ordering).at[ordering].set(jnp.arange(ordering.shape[0], dtype=jnp.int32))


def swap(block, mask):
    size = lax.axis_size("gx")
    return lax.ppermute(block, "gx", [(i, i ^ mask) for i in range(size)])


def masks(size):
    return [1 << bit for bit in range(size.bit_length() - 1)]


def gx_gather(block):
    held = {0: block}
    for mask in reversed(masks(lax.axis_size("gx"))):
        held.update({rel ^ mask: swap(held[rel], mask) for rel in list(held)})
    return [held[rel] for rel in range(len(held))]


def gx_reduce(blocks):
    held = dict(enumerate(blocks))
    for mask in masks(lax.axis_size("gx")):
        held = {rel: held[rel] + swap(held[rel ^ mask], mask) for rel in held if not rel & mask}
    return held[0]


def gx_exchange(blocks):
    return [block if rel == 0 else swap(block, rel) for rel, block in enumerate(blocks)]


def ring_order(size):
    return [i for i in range(size) if i % 2 == 0] + [i for i in reversed(range(size)) if i % 2]


def ring_step(block, step):
    order = ring_order(lax.axis_size("gy"))
    size = len(order)
    return lax.ppermute(block, "gy", [(order[k], order[(k + step) % size]) for k in range(size)])


def gy_gather(block):
    size = lax.axis_size("gy")
    half = block.shape[0] // 2
    pieces = [None] * size
    pieces[0] = block
    ahead = behind = block
    for step in range(1, size // 2):
        ahead, behind = ring_step(ahead, -1), ring_step(behind, 1)
        pieces[step], pieces[size - step] = ahead, behind
    pieces[size // 2] = jnp.concatenate([ring_step(ahead[:half], -1), ring_step(behind[half:], 1)], axis=0)
    return jnp.concatenate(pieces, axis=0)


def gy_reduce(blocks):
    size = lax.axis_size("gy")
    half = blocks[0].shape[0] // 2
    far = blocks[size // 2]
    ahead, behind = ring_step(far[:half], 1), ring_step(far[half:], -1)
    near, back = blocks[size // 2 - 1], blocks[size // 2 + 1]
    ahead = jnp.concatenate([near[:half] + ahead, near[half:]], axis=0)
    behind = jnp.concatenate([back[:half], back[half:] + behind], axis=0)
    for step in range(size // 2 - 2, 0, -1):
        ahead = blocks[step] + ring_step(ahead, 1)
        behind = blocks[size - step] + ring_step(behind, -1)
    return blocks[0] + ring_step(ahead, 1) + ring_step(behind, -1)


def on_device(stem_first, cotangent, branch_first, branch_second, bond_first, bond_second):
    groups, splits = lax.axis_size("gx"), lax.axis_size("gy")
    me_x, me_y = lax.axis_index("gx"), lax.axis_index("gy")
    height, width = stem_first.shape[1:]
    low = width // groups
    own = width // (groups * splits)
    factor = 1.0 / jnp.sqrt(jnp.float32(height * groups * splits))
    stem_rows = stem_first.reshape(height, width)
    cotan_rows = cotangent.reshape(height, width)

    partner = me_x ^ jnp.arange(groups, dtype=jnp.int32)
    order = jnp.array(ring_order(splits), jnp.int32)
    place = jnp.zeros_like(order).at[order].set(jnp.arange(splits, dtype=jnp.int32))
    ahead = order[(place[me_y] + jnp.arange(splits, dtype=jnp.int32)) % splits]
    rows = (
        partner[:, None, None] * low + ahead[None, :, None] * own + jnp.arange(own, dtype=jnp.int32)[None, None, :]
    ).reshape(width)
    bond_first, bond_second = bond_first[rows], bond_second[rows]
    bond_second = ((bond_second // low) ^ me_x) * low + bond_second % low
    back_first, back_second = inverse(bond_first), inverse(bond_second)

    block_first, block_second = gy_gather(branch_first), gy_gather(branch_second)
    cotan_all = jnp.concatenate(gx_gather(cotan_rows), axis=0)
    picked = jnp.take(stem_rows, bond_first, axis=1)
    picked = gx_exchange([picked[:, rel * low : (rel + 1) * low] for rel in range(groups)])
    picked = jnp.concatenate(picked, axis=0)

    mid = product(picked, block_first, ((1,), (0,)))
    mid = mid.reshape(groups, height, groups, low).transpose(2, 1, 0, 3).reshape(groups * height, width)
    mid = jnp.take(mid, bond_second, axis=1)
    regrouped = gx_reduce([mid[:, rel * low : (rel + 1) * low] for rel in range(groups)])
    regrouped = regrouped.reshape(groups, height, low)[partner].reshape(groups * height, low)
    outer_second = product(regrouped, cotan_all, ((0,), (0,)))
    grad_second = gy_reduce([outer_second[k * own : (k + 1) * own] for k in range(splits)])

    back = product(cotan_all, block_second, ((1,), (1,)))
    pieces = gx_gather(back)
    pieces = [
        jnp.concatenate([piece.reshape(groups, height, low)[h ^ rel] for h in range(groups)], axis=0)
        for rel, piece in enumerate(pieces)
    ]
    back_mid = jnp.take(jnp.concatenate(pieces, axis=1), back_second, axis=1)
    back_mid = back_mid.reshape(groups, height, groups, low).transpose(2, 1, 0, 3).reshape(groups * height, width)

    outer_first = product(picked, back_mid, ((0,), (0,)))
    grad_first = gy_reduce([outer_first[k * own : (k + 1) * own] for k in range(splits)])
    grad_first = grad_first.reshape(own, groups, low)[:, partner].reshape(own, width)

    turned = block_first.reshape(low, groups, low)[:, partner].reshape(low, width)
    grad = product(back_mid, turned, ((1,), (1,)))
    grad = gx_exchange([grad[rel * height : (rel + 1) * height] for rel in range(groups)])
    grad_stem = jnp.take(jnp.concatenate(grad, axis=1), back_first, axis=1).reshape(1, height, width)
    return (grad_stem, grad_first * factor, grad_second * factor)


def solution(mesh):
    return jax.shard_map(
        on_device,
        mesh=mesh,
        in_specs=(
            P("gx", "gy", None),
            P("gx", "gy", None),
            P(("gx", "gy"), None),
            P(("gx", "gy"), None),
            P(),
            P(),
        ),
        out_specs=(P("gx", "gy", None), P(("gx", "gy"), None), P(("gx", "gy"), None)),
        check_vma=False,
    )
```

time: 380 us -> 206 us (0.54)
  waiting for transfers between devices: 286 us -> 67.3 us
  local copies, waits for them, and re-layouts: 32.8 us -> 71.5 us
  starting transfers between devices: 7.4 us -> 41.3 us
  matrix products: 34.6 us -> 10.9 us
  between operations: 14.2 us -> 1.34 us
  other arithmetic: 3.87 us -> 13 us
    reduce_scatter x4 -> x0, waiting for transfers between devices: 176 us -> none  [the longest x1 64.5 us: on_device(): lax.psum_scatter(outer_second, 'gy', scatter_dimension=0, tiled=True)]
    all_gather x2 -> x0, waiting for transfers between devices: 87.7 us -> none  [the longest x1 61 us: on_device(): lax.all_gather(branch_second, ('gx', 'gy'), axis=0, tiled=True)]
    ppermute x0 -> x47, waiting for transfers between devices: none -> 67.3 us  [the longest x32 57.8 us: ring_step(): lax.ppermute(block, 'gy', [(order[k], order[(k + step) % size]) for k in...]
    ppermute x0 -> x47, starting transfers between devices: none -> 41.3 us  [the longest x32 35.3 us: ring_step(): lax.ppermute(block, 'gy', [(order[k], order[(k + step) % size]) for k in...]
    dot_general x5, matrix products: 34.6 us -> 10.9 us  [product(): lax.dot_general(left, right, (contract, ((), ())), precision=lax.Precisio...]
    all_to_all x2 -> x0, waiting for transfers between devices: 20.6 us -> none  [the longest x1 14.7 us: on_device(): lax.all_to_all(stem_mid.reshape(height, groups, width // groups), 'gx', s...]
    unnamed x9 -> x57, local copies, waits for them, and re-layouts: 1.26 us -> 11.9 us
    reshape x0 -> x6, local copies, waits for them, and re-layouts: none -> 7.11 us  [the longest x2 4.58 us: on_device(): back_mid.reshape(groups, height, groups, low).transpose(2, 1, 0, 3)]
  transfers between devices with their start and end apart: 8 -> 47, of which waited for: 8 -> 22; matrix products, arithmetic and copies ran while one was open for 18% -> 44% of each run, Pallas kernels for 0% -> 0%
where the time goes in v1:
time: 206 us; the launch traced here: 205 us
  local copies, waits for them, and re-layouts  71.5 us (35%)
  waiting for transfers between devices  67.3 us (33%)
  starting transfers between devices  41.3 us (20%)
  other arithmetic  13 us (6%)
  matrix products  10.9 us (5%)
    ppermute x32, waiting for transfers between devices, ring_step(): lax.ppermute(block, 'gy', [(order[k], order[(k + step) % size]) for k in...  57.8 us
    ppermute x32, starting transfers between devices, ring_step(): lax.ppermute(block, 'gy', [(order[k], order[(k + step) % size]) for k in...  35.3 us
    unnamed x57, local copies, waits for them, and re-layouts  11.9 us
    dot_general x5, matrix products, product(): lax.dot_general(left, right, (contract, ((), ())), precision=lax.Precisio...  10.9 us
    ppermute x15, waiting for transfers between devices, swap(): return lax.ppermute(block, 'gx', [(i, i ^ mask) for i in range(size)])  9.49 us
    gather x2, local copies, waits for them, and re-layouts, on_device(): bond_first, bond_second = (bond_first[rows], bond_second[rows])  9.06 us
    scatter x2, local copies, waits for them, and re-layouts, inverse(): jnp.zeros_like(ordering).at[ordering]  8.62 us
    ppermute x15, starting transfers between devices, swap(): return lax.ppermute(block, 'gx', [(i, i ^ mask) for i in range(size)])  6.08 us
  transfers between devices with their start and end apart: 47, of which 22 were waited for; matrix products, arithmetic and copies ran while one was open for 44% of the time, Pallas kernels for 0%

profile of v1, /device:TPU:0, one launch (start us, length us, event | category | flops | bytes accessed | tf_op | source)
XLA Modules:
  0.0 205.3 jit_solution(7550176743297953000)
XLA Ops:
  1.8 3.1 %collective-permute-start.18 = (f32[32,1024]{0,1:T(8,128)S(1)}, f32[32,1024]{0,1:T(8,128)S(1)}, u32[]{:S(2)}, u32[]{:S(2)}) collective-permute-start(f32[32,1024]{0,1:T(8,128)S(1)} %copy.22), channel_id=1, source_target_pairs={{0,2},{2,4},{4,6},{6,7},{7,5},{5,3},{3,1},{1,0},{8,10},{10,12},{12... | collective-permute-start | bytes 393224 | tf_op jit(solution)/shard_map/ppermute | solution.py:55
  4.8 2.0 collective-permute-start.3
  11.0 4.5 %gather_fusion.3 = s32[1024]{0:T(1024)S(1)} fusion(s32[1024]{0:T(1024)S(1)} %copy-done, s32[1024]{0:T(1024)S(1)} %broadcast_clamp_fusion.1), kind=kCustom, calls=%fused_computation.7 | custom fusion | bytes 12288 | tf_op jit(solution)/shard_map/gather | solution.py:102
  15.8 2.8 %gather_fusion.8 = f32[1024,128]{1,0:T(8,128)S(1)} fusion(f32[128,1024]{0,1:T(8,128)S(1)} %bitcast.57, s32[1024]{0:T(1024)S(1)} %fusion.18), kind=kCustom, calls=%fused_computation.3.clone | custom fusion | bytes 1052672 | tf_op jit(solution)/shard_map/jit(_take)/gather | solution.py:108
  19.6 4.5 %gather_fusion.1 = s32[1024]{0:T(1024)S(1)} fusion(s32[1024]{0:T(1024)S(1)} %copy-done.1, s32[1024]{0:T(1024)S(1)} %broadcast_clamp_fusion.1), kind=kCustom, calls=%fused_computation.5 | custom fusion | bytes 12288 | tf_op jit(solution)/shard_map/gather | solution.py:102
  24.2 4.3 %scatter_custom_fusion = s32[1024]{0:T(1024)S(1)} fusion(s32[1024]{0:T(1024)S(1)} %bitcast.76, s32[1024]{0:T(1024)S(1)} %iota.28, s32[]{:T(128)} %constant.75.clone.1), kind=kCustom, calls=%fused_computation.104 | custom fusion | bytes 4100 | tf_op jit(solution)/shard_map/scatter | solution.py:18
  28.5 4.3 %scatter_custom_fusion.1 = s32[1024]{0:T(1024)S(1)} fusion(s32[1024]{0:T(1024)S(1)} %bitcast.75, s32[1024]{0:T(1024)S(1)} %iota.30, s32[]{:T(128)} %constant.75.clone.1), kind=kCustom, calls=%fused_computation.102 | custom fusion | bytes 4100 | tf_op jit(solution)/shard_map/scatter | solution.py:18
  33.4 2.0 collective-permute-start.19
  35.5 12.5 %collective-permute-done.19 = f32[32,1024]{0,1:T(8,128)S(1)} collective-permute-done((f32[32,1024]{0,1:T(8,128)S(1)}, f32[32,1024]{0,1:T(8,128)S(1)}, u32[]{:S(2)}, u32[]{:S(2)}) %collective-permute-start.19) | collective-permute-done | bytes 131104 | tf_op jit(solution)/shard_map/ppermute | solution.py:55
  48.0 1.8 collective-permute-start.20
  50.0 11.6 %collective-permute-done.20 = f32[32,1024]{0,1:T(8,128)S(1)} collective-permute-done((f32[32,1024]{0,1:T(8,128)S(1)}, f32[32,1024]{0,1:T(8,128)S(1)}, u32[]{:S(2)}, u32[]{:S(2)}) %collective-permute-start.20) | collective-permute-done | bytes 131104 | tf_op jit(solution)/shard_map/ppermute | solution.py:55
  61.8 1.7 collective-permute-start.21
  65.2 1.6 collective-permute-start.26
  66.8 7.9 %collective-permute-done.21 = f32[16,1024]{0,1:T(8,128)S(1)} collective-permute-done((f32[16,1024]{0,1:T(8,128)S(1)}, f32[16,1024]{0,1:T(8,128)S(1)}, u32[]{:S(2)}, u32[]{:S(2)}) %collective-permute-start.21) | collective-permute-done | bytes 65568 | tf_op jit(solution)/shard_map/ppermute | solution.py:55
  76.3 1.7 collective-permute-start.8
  79.3 4.0 %concatenate.48 = f32[256,1024]{0,1:T(8,128)S(1)} concatenate(f32[32,1024]{0,1:T(8,128)S(1)} %copy.22, f32[32,1024]{0,1:T(8,128)} %copy-done.8, f32[32,1024]{0,1:T(8,128)} %copy-done.10, f32[32,1024]{0,1:T(8,128)} %copy-done.11, f32[16,1024]{0,1:T(8,128)} %copy-done.13, f32[16,1024]{0,1:T(8,128)} %copy-done.12, f32[32,1024]{0,1:T(8,128)S(1)} %collective-permute-done.20, ...), dimensions={0} | concatenate | bytes 2097152 | tf_op jit(solution)/shard_map/concatenate | solution.py:68
  83.3 1.6 collective-permute-start.1
  85.4 1.6 collective-permute-start.9
  87.6 2.8 %fusion.3 = f32[512,1024]{1,0:T(8,128)S(1)} fusion(f32[256,1024]{0,1:T(8,128)S(1)} %concatenate.48, f32[128,256]{0,1:T(8,128)} %copy-done.4, f32[128,256]{0,1:T(8,128)S(1)} %collective-permute-done.26, f32[128,256]{0,1:T(8,128)S(1)} %collective-permute-done.25, f32[128,256]{0,1:T(8,128)S(1)} %get-tuple-element.30), kind=kOutput, calls=%fused_computation.26 | convolution fusion | flops 805699584 | bytes 3670016 | tf_op jit(solution)/shard_map/dot_general | solution.py:8
  90.5 2.0 reshape.347
  92.4 4.1 %copy.28 = f32[4,128,4,256]{1,0,3,2:T(4,128)} copy(f32[4,128,4,256]{3,0,1,2:T(4,128)} %bitcast.61) | data formatting | bytes 4194304 | tf_op jit(solution)/shard_map/transpose | solution.py:113
  96.6 1.8 copy.38
  98.3 4.9 %gather_fusion.9 = f32[1024,512]{1,0:T(8,128)} fusion(f32[512,1024]{0,1:T(8,128)S(1)} %bitcast.56, s32[1024]{0:T(1024)S(1)} %broadcast_clamp_fusion), kind=kCustom, calls=%fused_computation.2.clone | custom fusion | bytes 4198400 | tf_op jit(solution)/shard_map/jit(_take)/gather | solution.py:114
  103.3 1.8 select_bitcast_fusion
  109.5 1.6 collective-permute-start.10
  117.1 3.4 %fusion.1 = f32[512,256]{0,1:T(8,128)} fusion(f32[256,1024]{1,0:T(8,128)S(1)} %constant_dynamic-update-slice_fusion, f32[128,1024]{1,0:T(8,128)S(1)} %collective-permute-done.2, f32[128,1024]{1,0:T(8,128)} %collective-permute-done.1, f32[128,1024]{1,0:T(8,128)} %collective-permute-done, f32[128,1024]{1,0:T(8,128)} %bitcast.7), kind=kOutput, calls=%fused_computation.18 | convolution fusion | flops 806879232 | bytes 3670016 | tf_op jit(solution)/shard_map/dot_general | solution.py:8
  120.5 1.7 collective-permute-start.12
  122.2 6.5 %collective-permute-done.38 = f32[512,256]{0,1:T(8,128)S(1)} collective-permute-done((f32[512,256]{0,1:T(8,128)S(1)}, f32[512,256]{0,1:T(8,128)S(1)}, u32[]{:S(2)}, u32[]{:S(2)}) %collective-permute-start.38) | collective-permute-done | bytes 524320 | tf_op jit(solution)/shard_map/ppermute | solution.py:23
  129.9 2.5 %fusion = f32[256,1024]{1,0:T(8,128)S(1)} fusion(f32[512,256]{1,0:T(8,128)S(1)} %bitcast.68, f32[128,1024]{1,0:T(8,128)S(1)} %copy-done.21, f32[128,1024]{1,0:T(8,128)} %collective-permute-done.1, f32[128,1024]{1,0:T(8,128)} %collective-permute-done, f32[128,1024]{1,0:T(8,128)} %bitcast.7), kind=kOutput, calls=%fused_computation.17 | convolution fusion | flops 806879232 | bytes 3670016 | tf_op jit(solution)/shard_map/dot_general | solution.py:8
  133.1 1.6 collective-permute-start.39
  140.7 2.2 %collective-permute-done.43 = f32[16,1024]{1,0:T(8,128)S(1)} collective-permute-done((f32[16,1024]{1,0:T(8,128)S(1)}, f32[16,1024]{1,0:T(8,128)S(1)}, u32[]{:S(2)}, u32[]{:S(2)}) %collective-permute-start.43) | collective-permute-done | bytes 65568 | tf_op jit(solution)/shard_map/ppermute | solution.py:55
  147.9 2.0 collective-permute-done.41
  150.6 1.6 collective-permute-start.45
  152.8 4.2 %collective-permute-done.45 = f32[32,1024]{1,0:T(8,128)S(1)} collective-permute-done((f32[32,1024]{1,0:T(8,128)S(1)}, f32[32,1024]{1,0:T(8,128)S(1)}, u32[]{:S(2)}, u32[]{:S(2)}) %collective-permute-start.45) | collective-permute-done | bytes 131104 | tf_op jit(solution)/shard_map/ppermute | solution.py:55
  160.3 4.9 %gather_fusion.6 = f32[1024,512]{1,0:T(8,128)} fusion(f32[512,1024]{0,1:T(8,128)S(1)} %maximum_maximum_fusion, s32[1024]{0:T(1024)S(1)} %fusion.16), kind=kCustom, calls=%fused_computation.clone | custom fusion | bytes 4198400 | tf_op jit(solution)/shard_map/jit(_take)/gather | solution.py:126
  165.2 1.8 select_bitcast_fusion.1
  167.1 1.7 reshape.340
  168.8 2.9 %copy.19 = f32[4,128,4,256]{3,0,1,2:T(4,128)S(1)} copy(f32[4,128,4,256]{1,0,3,2:T(4,128)} %reshape.340) | data formatting | bytes 4194304 | tf_op jit(solution)/shard_map/reshape | solution.py:127
  175.5 2.5 %collective-permute-done.28 = f32[16,1024]{1,0:T(8,128)S(1)} collective-permute-done((f32[16,1024]{1,0:T(8,128)S(1)}, f32[16,1024]{1,0:T(8,128)S(1)}, u32[]{:S(2)}, u32[]{:S(2)}) %collective-permute-start.28) | collective-permute-done | bytes 65568 | tf_op jit(solution)/shard_map/ppermute | solution.py:55
  178.0 2.1 %collective-permute-start.32 = (f32[16,1024]{1,0:T(8,128)S(1)}, f32[16,1024]{1,0:T(8,128)S(1)}, u32[]{:S(2)}, u32[]{:S(2)}) collective-permute-start(f32[16,1024]{1,0:T(8,128)S(1)} %get-tuple-element.27), channel_id=1, source_target_pairs={{0,1},{2,0},{4,2},{6,4},{7,6},{5,7},{3,5},{1,3},{8,9},{10,8},{12,1... | collective-permute-start | bytes 196616 | tf_op jit(solution)/shard_map/ppermute | solution.py:55
  180.2 2.2 %collective-permute-done.32 = f32[16,1024]{1,0:T(8,128)S(1)} collective-permute-done((f32[16,1024]{1,0:T(8,128)S(1)}, f32[16,1024]{1,0:T(8,128)S(1)}, u32[]{:S(2)}, u32[]{:S(2)}) %collective-permute-start.32) | collective-permute-done | bytes 65568 | tf_op jit(solution)/shard_map/ppermute | solution.py:55
  182.4 2.1 %collective-permute-start.33 = (f32[32,1024]{1,0:T(8,128)S(1)}, f32[32,1024]{1,0:T(8,128)S(1)}, u32[]{:S(2)}, u32[]{:S(2)}) collective-permute-start(f32[32,1024]{1,0:T(8,128)S(1)} %pad_maximum_fusion.8), channel_id=1, source_target_pairs={{0,1},{2,0},{4,2},{6,4},{7,6},{5,7},{3,5},{1,3},{8,9},{10,8},{12,1... | collective-permute-start | bytes 393224 | tf_op jit(solution)/shard_map/ppermute | solution.py:55
  185.4 2.0 collective-permute-done.33
  187.9 2.3 %collective-permute-done.30 = f32[32,1024]{1,0:T(8,128)S(1)} collective-permute-done((f32[32,1024]{1,0:T(8,128)S(1)}, f32[32,1024]{1,0:T(8,128)S(1)}, u32[]{:S(2)}, u32[]{:S(2)}) %collective-permute-start.30) | collective-permute-done | bytes 131104 | tf_op jit(solution)/shard_map/ppermute | solution.py:55
  190.5 1.7 fusion.6
  192.4 2.8 %collective-permute-done.24 = f32[128,256]{0,1:T(8,128)S(1)} collective-permute-done((f32[128,256]{0,1:T(8,128)S(1)}, f32[128,256]{0,1:T(8,128)S(1)}, u32[]{:S(2)}, u32[]{:S(2)}) %collective-permute-start.24) | collective-permute-done | bytes 131104 | tf_op jit(solution)/shard_map/ppermute | solution.py:23
  195.2 2.8 %gather_fusion.7 = f32[1024,128]{1,0:T(8,128)S(1)} fusion(f32[128,1024]{0,1:T(8,128)S(1)} %pad_maximum_fusion.3, s32[1024]{0:T(1024)S(1)} %copy-done.18), kind=kCustom, calls=%fused_computation.1.clone | custom fusion | bytes 1052672 | tf_op jit(solution)/shard_map/jit(_take)/gather | solution.py:136
  201.4 2.2 %collective-permute-done.31 = f32[32,1024]{1,0:T(8,128)S(1)} collective-permute-done((f32[32,1024]{1,0:T(8,128)S(1)}, f32[32,1024]{1,0:T(8,128)S(1)}, u32[]{:S(2)}, u32[]{:S(2)}) %collective-permute-start.31) | collective-permute-done | bytes 131104 | tf_op jit(solution)/shard_map/ppermute | solution.py:55
  (190 shorter events, 51.9 us)
Async XLA Ops:
  1.8 31.7 %collective-permute-start.18 = (f32[32,1024]{0,1:T(8,128)S(1)}, f32[32,1024]{0,1:T(8,128)S(1)}, u32[]{:S(2)}, u32[]{:S(2)}) collective-permute-start(f32[32,1024]{0,1:T(8,128)S(1)} %copy.22), channel_id=1, source_target_pairs={{0,2},{2,4},{4,6},{6,7},{7,5},{5,3},{3,1},{1,0},{8,10},{10,12},{12... | collective-permute-start | bytes 393224 | tf_op jit(solution)/shard_map/ppermute | solution.py:55
  4.8 30.6 %collective-permute-start.14 = (f32[32,1024]{0,1:T(8,128)S(1)}, f32[32,1024]{0,1:T(8,128)S(1)}, u32[]{:S(2)}, u32[]{:S(2)}) collective-permute-start(f32[32,1024]{0,1:T(8,128)S(1)} %copy.22), channel_id=1, source_target_pairs={{0,1},{2,0},{4,2},{6,4},{7,6},{5,7},{3,5},{1,3},{8,9},{10,8},{12,1... | collective-permute-start | bytes 393224 | tf_op jit(solution)/shard_map/ppermute | solution.py:55
  4.8 59.7 %collective-permute-start.3 = (f32[32,1024]{1,0:T(8,128)}, f32[32,1024]{1,0:T(8,128)S(1)}, u32[]{:S(2)}, u32[]{:S(2)}) collective-permute-start(f32[32,1024]{1,0:T(8,128)} %param.14), channel_id=1, source_target_pairs={{0,1},{2,0},{4,2},{6,4},{7,6},{5,7},{3,5},{1,3},{8,9},{10,8},{12,1... | collective-permute-start | bytes 393224 | tf_op jit(solution)/shard_map/ppermute | solution.py:55
  6.8 60.0 %collective-permute-start.7 = (f32[32,1024]{1,0:T(8,128)}, f32[32,1024]{1,0:T(8,128)}, u32[]{:S(2)}, u32[]{:S(2)}) collective-permute-start(f32[32,1024]{1,0:T(8,128)} %param.14), channel_id=1, source_target_pairs={{0,2},{2,4},{4,6},{6,7},{7,5},{5,3},{3,1},{1,0},{8,10},{10,12},{12... | collective-permute-start | bytes 393224 | tf_op jit(solution)/shard_map/ppermute | solution.py:55
  19.6 59.1 %copy-start.14 = (f32[32,1024]{1,0:T(8,128)S(1)}, f32[32,1024]{1,0:T(8,128)}, u32[]{:S(2)}) copy-start(f32[32,1024]{1,0:T(8,128)} %param.14) | copy-start | bytes 393220
  19.6 63.7 %collective-permute-start.25 = (f32[128,256]{0,1:T(8,128)}, f32[128,256]{0,1:T(8,128)S(1)}, u32[]{:S(2)}, u32[]{:S(2)}) collective-permute-start(f32[128,256]{0,1:T(8,128)} %get-tuple-element.33), channel_id=1, source_target_pairs={{0,8},{8,0},{16,24},{24,16},{1,9},{9,1},{17,25},{25,17},{2,10},{10... | collective-permute-start | bytes 393224 | tf_op jit(solution)/shard_map/ppermute | solution.py:23
  33.4 14.5 %collective-permute-start.19 = (f32[32,1024]{0,1:T(8,128)S(1)}, f32[32,1024]{0,1:T(8,128)S(1)}, u32[]{:S(2)}, u32[]{:S(2)}) collective-permute-start(f32[32,1024]{0,1:T(8,128)S(1)} %collective-permute-done.18), channel_id=1, source_target_pairs={{0,2},{2,4},{4,6},{6,7},{7,5},{5,3},{3,1},{1,0},{8,10},{10,12},{12... | collective-permute-start | bytes 393224 | tf_op jit(solution)/shard_map/ppermute | solution.py:55
  35.4 14.3 %collective-permute-start.15 = (f32[32,1024]{0,1:T(8,128)S(1)}, f32[32,1024]{0,1:T(8,128)S(1)}, u32[]{:S(2)}, u32[]{:S(2)}) collective-permute-start(f32[32,1024]{0,1:T(8,128)S(1)} %collective-permute-done.14), channel_id=1, source_target_pairs={{0,1},{2,0},{4,2},{6,4},{7,6},{5,7},{3,5},{1,3},{8,9},{10,8},{12,1... | collective-permute-start | bytes 393224 | tf_op jit(solution)/shard_map/ppermute | solution.py:55
  48.0 13.7 %collective-permute-start.20 = (f32[32,1024]{0,1:T(8,128)S(1)}, f32[32,1024]{0,1:T(8,128)S(1)}, u32[]{:S(2)}, u32[]{:S(2)}) collective-permute-start(f32[32,1024]{0,1:T(8,128)S(1)} %collective-permute-done.19), channel_id=1, source_target_pairs={{0,2},{2,4},{4,6},{6,7},{7,5},{5,3},{3,1},{1,0},{8,10},{10,12},{12... | collective-permute-start | bytes 393224 | tf_op jit(solution)/shard_map/ppermute | solution.py:55
  49.8 13.8 %collective-permute-start.16 = (f32[32,1024]{0,1:T(8,128)S(1)}, f32[32,1024]{0,1:T(8,128)S(1)}, u32[]{:S(2)}, u32[]{:S(2)}) collective-permute-start(f32[32,1024]{0,1:T(8,128)S(1)} %collective-permute-done.15), channel_id=1, source_target_pairs={{0,1},{2,0},{4,2},{6,4},{7,6},{5,7},{3,5},{1,3},{8,9},{10,8},{12,1... | collective-permute-start | bytes 393224 | tf_op jit(solution)/shard_map/ppermute | solution.py:55
  61.8 12.8 %collective-permute-start.21 = (f32[16,1024]{0,1:T(8,128)S(1)}, f32[16,1024]{0,1:T(8,128)S(1)}, u32[]{:S(2)}, u32[]{:S(2)}) collective-permute-start(f32[16,1024]{0,1:T(8,128)S(1)} %slice.268), channel_id=1, source_target_pairs={{0,2},{2,4},{4,6},{6,7},{7,5},{5,3},{3,1},{1,0},{8,10},{10,12},{12... | collective-permute-start | bytes 196616 | tf_op jit(solution)/shard_map/ppermute | solution.py:55
  63.6 12.7 %collective-permute-start.17 = (f32[16,1024]{0,1:T(8,128)S(1)}, f32[16,1024]{0,1:T(8,128)S(1)}, u32[]{:S(2)}, u32[]{:S(2)}) collective-permute-start(f32[16,1024]{0,1:T(8,128)S(1)} %bitcast.70), channel_id=1, source_target_pairs={{0,1},{2,0},{4,2},{6,4},{7,6},{5,7},{3,5},{1,3},{8,9},{10,8},{12,1... | collective-permute-start | bytes 196616 | tf_op jit(solution)/shard_map/ppermute | solution.py:55
  65.2 19.7 %collective-permute-start.26 = (f32[128,256]{0,1:T(8,128)}, f32[128,256]{0,1:T(8,128)S(1)}, u32[]{:S(2)}, u32[]{:S(2)}) collective-permute-start(f32[128,256]{0,1:T(8,128)} %get-tuple-element.32), channel_id=1, source_target_pairs={{0,16},{8,24},{16,0},{24,8},{1,17},{9,25},{17,1},{25,9},{2,18},{10... | collective-permute-start | bytes 393224 | tf_op jit(solution)/shard_map/ppermute | solution.py:23
  66.8 20.2 %collective-permute-start.27 = (f32[128,256]{0,1:T(8,128)}, f32[128,256]{0,1:T(8,128)S(1)}, u32[]{:S(2)}, u32[]{:S(2)}) collective-permute-start(f32[128,256]{0,1:T(8,128)} %get-tuple-element.31), channel_id=1, source_target_pairs={{0,24},{8,16},{16,8},{24,0},{1,25},{9,17},{17,9},{25,1},{2,26},{10... | collective-permute-start | bytes 393224 | tf_op jit(solution)/shard_map/ppermute | solution.py:23
  74.7 10.2 %collective-permute-start.4 = (f32[32,1024]{1,0:T(8,128)}, f32[32,1024]{1,0:T(8,128)}, u32[]{:S(2)}, u32[]{:S(2)}) collective-permute-start(f32[32,1024]{1,0:T(8,128)} %copy-done.15), channel_id=1, source_target_pairs={{0,1},{2,0},{4,2},{6,4},{7,6},{5,7},{3,5},{1,3},{8,9},{10,8},{12,1... | collective-permute-start | bytes 393224 | tf_op jit(solution)/shard_map/ppermute | solution.py:55
  76.3 9.1 %collective-permute-start.8 = (f32[32,1024]{1,0:T(8,128)}, f32[32,1024]{1,0:T(8,128)}, u32[]{:S(2)}, u32[]{:S(2)}) collective-permute-start(f32[32,1024]{1,0:T(8,128)} %collective-permute-done.7), channel_id=1, source_target_pairs={{0,2},{2,4},{4,6},{6,7},{7,5},{5,3},{3,1},{1,0},{8,10},{10,12},{12... | collective-permute-start | bytes 393224 | tf_op jit(solution)/shard_map/ppermute | solution.py:55
  83.3 30.4 %collective-permute-start.1 = (f32[128,1024]{1,0:T(8,128)}, f32[128,1024]{1,0:T(8,128)}, u32[]{:S(2)}, u32[]{:S(2)}) collective-permute-start(f32[128,1024]{1,0:T(8,128)} %bitcast.7), channel_id=1, source_target_pairs={{0,16},{8,24},{16,0},{24,8},{1,17},{9,25},{17,1},{25,9},{2,18},{10... | collective-permute-start | bytes 1572872 | tf_op jit(solution)/shard_map/ppermute | solution.py:23
  84.9 32.2 %collective-permute-start = (f32[128,1024]{1,0:T(8,128)}, f32[128,1024]{1,0:T(8,128)}, u32[]{:S(2)}, u32[]{:S(2)}) collective-permute-start(f32[128,1024]{1,0:T(8,128)} %bitcast.7), channel_id=1, source_target_pairs={{0,8},{8,0},{16,24},{24,16},{1,9},{9,1},{17,25},{25,17},{2,10},{10... | collective-permute-start | bytes 1572872 | tf_op jit(solution)/shard_map/ppermute | solution.py:23
  84.9 22.4 %collective-permute-start.5 = (f32[32,1024]{1,0:T(8,128)}, f32[32,1024]{1,0:T(8,128)}, u32[]{:S(2)}, u32[]{:S(2)}) collective-permute-start(f32[32,1024]{1,0:T(8,128)} %collective-permute-done.4), channel_id=1, source_target_pairs={{0,1},{2,0},{4,2},{6,4},{7,6},{5,7},{3,5},{1,3},{8,9},{10,8},{12,1... | collective-permute-start | bytes 393224 | tf_op jit(solution)/shard_map/ppermute | solution.py:55
  85.4 23.2 %collective-permute-start.9 = (f32[32,1024]{1,0:T(8,128)}, f32[32,1024]{1,0:T(8,128)}, u32[]{:S(2)}, u32[]{:S(2)}) collective-permute-start(f32[32,1024]{1,0:T(8,128)} %collective-permute-done.8), channel_id=1, source_target_pairs={{0,2},{2,4},{4,6},{6,7},{7,5},{5,3},{3,1},{1,0},{8,10},{10,12},{12... | collective-permute-start | bytes 393224 | tf_op jit(solution)/shard_map/ppermute | solution.py:55
  105.2 8.6 %collective-permute-start.37 = (f32[512,256]{0,1:T(8,128)S(1)}, f32[512,256]{0,1:T(8,128)S(1)}, u32[]{:S(2)}, u32[]{:S(2)}) collective-permute-start(f32[512,256]{0,1:T(8,128)S(1)} %get-tuple-element.17), channel_id=1, source_target_pairs={{0,8},{8,0},{16,24},{24,16},{1,9},{9,1},{17,25},{25,17},{2,10},{10... | collective-permute-start | bytes 1572872 | tf_op jit(solution)/shard_map/ppermute | solution.py:23
  108.2 4.3 %collective-permute-start.6 = (f32[16,1024]{1,0:T(8,128)S(1)}, f32[16,1024]{1,0:T(8,128)S(1)}, u32[]{:S(2)}, u32[]{:S(2)}) collective-permute-start(f32[16,1024]{1,0:T(8,128)S(1)} %slice.255), channel_id=1, source_target_pairs={{0,1},{2,0},{4,2},{6,4},{7,6},{5,7},{3,5},{1,3},{8,9},{10,8},{12,1... | collective-permute-start | bytes 196616 | tf_op jit(solution)/shard_map/ppermute | solution.py:55
  109.5 4.3 %collective-permute-start.10 = (f32[16,1024]{1,0:T(8,128)S(1)}, f32[16,1024]{1,0:T(8,128)S(1)}, u32[]{:S(2)}, u32[]{:S(2)}) collective-permute-start(f32[16,1024]{1,0:T(8,128)S(1)} %slice.256), channel_id=1, source_target_pairs={{0,2},{2,4},{4,6},{6,7},{7,5},{5,3},{3,1},{1,0},{8,10},{10,12},{12... | collective-permute-start | bytes 196616 | tf_op jit(solution)/shard_map/ppermute | solution.py:55
  112.4 9.8 %collective-permute-start.36 = (f32[512,256]{0,1:T(8,128)S(1)}, f32[512,256]{0,1:T(8,128)S(1)}, u32[]{:S(2)}, u32[]{:S(2)}) collective-permute-start(f32[512,256]{0,1:T(8,128)S(1)} %get-tuple-element.16), channel_id=1, source_target_pairs={{0,8},{8,0},{16,24},{24,16},{1,9},{9,1},{17,25},{25,17},{2,10},{10... | collective-permute-start | bytes 1572872 | tf_op jit(solution)/shard_map/ppermute | solution.py:23
  113.7 3.4 %collective-permute-start.2 = (f32[128,1024]{1,0:T(8,128)}, f32[128,1024]{1,0:T(8,128)S(1)}, u32[]{:S(2)}, u32[]{:S(2)}) collective-permute-start(f32[128,1024]{1,0:T(8,128)} %collective-permute-done.1), channel_id=1, source_target_pairs={{0,8},{8,0},{16,24},{24,16},{1,9},{9,1},{17,25},{25,17},{2,10},{10... | collective-permute-start | bytes 1572872 | tf_op jit(solution)/shard_map/ppermute | solution.py:23
  113.9 14.8 %collective-permute-start.38 = (f32[512,256]{0,1:T(8,128)S(1)}, f32[512,256]{0,1:T(8,128)S(1)}, u32[]{:S(2)}, u32[]{:S(2)}) collective-permute-start(f32[512,256]{0,1:T(8,128)S(1)} %slice_add_fusion), channel_id=1, source_target_pairs={{0,16},{8,24},{16,0},{24,8},{1,17},{9,25},{17,1},{25,9},{2,18},{10... | collective-permute-start | bytes 1572872 | tf_op jit(solution)/shard_map/ppermute | solution.py:23
  120.5 20.1 %collective-permute-start.12 = (f32[512,256]{0,1:T(8,128)}, f32[512,256]{0,1:T(8,128)}, u32[]{:S(2)}, u32[]{:S(2)}) collective-permute-start(f32[512,256]{0,1:T(8,128)} %fusion.1), channel_id=1, source_target_pairs={{0,16},{8,24},{16,0},{24,8},{1,17},{9,25},{17,1},{25,9},{2,18},{10... | collective-permute-start | bytes 1572872 | tf_op jit(solution)/shard_map/ppermute | solution.py:23
  133.1 4.6 %collective-permute-start.39 = (f32[16,1024]{1,0:T(8,128)}, f32[16,1024]{1,0:T(8,128)}, u32[]{:S(2)}, u32[]{:S(2)}) collective-permute-start(f32[16,1024]{1,0:T(8,128)} %slice.296), channel_id=1, source_target_pairs={{0,2},{2,4},{4,6},{6,7},{7,5},{5,3},{3,1},{1,0},{8,10},{10,12},{12... | collective-permute-start | bytes 196616 | tf_op jit(solution)/shard_map/ppermute | solution.py:55
  136.1 16.1 %collective-permute-start.11 = (f32[512,256]{0,1:T(8,128)}, f32[512,256]{0,1:T(8,128)S(1)}, u32[]{:S(2)}, u32[]{:S(2)}) collective-permute-start(f32[512,256]{0,1:T(8,128)} %fusion.1), channel_id=1, source_target_pairs={{0,8},{8,0},{16,24},{24,16},{1,9},{9,1},{17,25},{25,17},{2,10},{10... | collective-permute-start | bytes 1572872 | tf_op jit(solution)/shard_map/ppermute | solution.py:23
  138.5 4.3 %collective-permute-start.43 = (f32[16,1024]{1,0:T(8,128)S(1)}, f32[16,1024]{1,0:T(8,128)S(1)}, u32[]{:S(2)}, u32[]{:S(2)}) collective-permute-start(f32[16,1024]{1,0:T(8,128)S(1)} %get-tuple-element.21), channel_id=1, source_target_pairs={{0,1},{2,0},{4,2},{6,4},{7,6},{5,7},{3,5},{1,3},{8,9},{10,8},{12,1... | collective-permute-start | bytes 196616 | tf_op jit(solution)/shard_map/ppermute | solution.py:55
  139.9 5.0 %collective-permute-start.40 = (f32[32,1024]{1,0:T(8,128)S(1)}, f32[32,1024]{1,0:T(8,128)S(1)}, u32[]{:S(2)}, u32[]{:S(2)}) collective-permute-start(f32[32,1024]{1,0:T(8,128)S(1)} %pad_maximum_fusion.9), channel_id=1, source_target_pairs={{0,2},{2,4},{4,6},{6,7},{7,5},{5,3},{3,1},{1,0},{8,10},{10,12},{12... | collective-permute-start | bytes 393224 | tf_op jit(solution)/shard_map/ppermute | solution.py:55
  140.7 18.3 %collective-permute-start.13 = (f32[512,256]{0,1:T(8,128)}, f32[512,256]{0,1:T(8,128)S(1)}, u32[]{:S(2)}, u32[]{:S(2)}) collective-permute-start(f32[512,256]{0,1:T(8,128)} %collective-permute-done.12), channel_id=1, source_target_pairs={{0,8},{8,0},{16,24},{24,16},{1,9},{9,1},{17,25},{25,17},{2,10},{10... | collective-permute-start | bytes 1572872 | tf_op jit(solution)/shard_map/ppermute | solution.py:23
  142.9 5.0 %collective-permute-start.44 = (f32[32,1024]{1,0:T(8,128)S(1)}, f32[32,1024]{1,0:T(8,128)S(1)}, u32[]{:S(2)}, u32[]{:S(2)}) collective-permute-start(f32[32,1024]{1,0:T(8,128)S(1)} %pad_maximum_fusion.10), channel_id=1, source_target_pairs={{0,1},{2,0},{4,2},{6,4},{7,6},{5,7},{3,5},{1,3},{8,9},{10,8},{12,1... | collective-permute-start | bytes 393224 | tf_op jit(solution)/shard_map/ppermute | solution.py:55
  144.9 5.0 %collective-permute-start.41 = (f32[32,1024]{1,0:T(8,128)S(1)}, f32[32,1024]{1,0:T(8,128)S(1)}, u32[]{:S(2)}, u32[]{:S(2)}) collective-permute-start(f32[32,1024]{1,0:T(8,128)S(1)} %slice_add_fusion.4), channel_id=1, source_target_pairs={{0,2},{2,4},{4,6},{6,7},{7,5},{5,3},{3,1},{1,0},{8,10},{10,12},{12... | collective-permute-start | bytes 393224 | tf_op jit(solution)/shard_map/ppermute | solution.py:55
  150.6 6.3 %collective-permute-start.45 = (f32[32,1024]{1,0:T(8,128)S(1)}, f32[32,1024]{1,0:T(8,128)S(1)}, u32[]{:S(2)}, u32[]{:S(2)}) collective-permute-start(f32[32,1024]{1,0:T(8,128)S(1)} %get-tuple-element.19), channel_id=1, source_target_pairs={{0,1},{2,0},{4,2},{6,4},{7,6},{5,7},{3,5},{1,3},{8,9},{10,8},{12,1... | collective-permute-start | bytes 393224 | tf_op jit(solution)/shard_map/ppermute | solution.py:55
  152.3 38.0 %collective-permute-start.42 = (f32[32,1024]{1,0:T(8,128)}, f32[32,1024]{1,0:T(8,128)}, u32[]{:S(2)}, u32[]{:S(2)}) collective-permute-start(f32[32,1024]{1,0:T(8,128)} %get-tuple-element.18), channel_id=1, source_target_pairs={{0,2},{2,4},{4,6},{6,7},{7,5},{5,3},{3,1},{1,0},{8,10},{10,12},{12... | collective-permute-start | bytes 393224 | tf_op jit(solution)/shard_map/ppermute | solution.py:55
  157.7 32.8 %collective-permute-start.46 = (f32[32,1024]{1,0:T(8,128)}, f32[32,1024]{1,0:T(8,128)}, u32[]{:S(2)}, u32[]{:S(2)}) collective-permute-start(f32[32,1024]{1,0:T(8,128)} %slice_add_fusion.3), channel_id=1, source_target_pairs={{0,1},{2,0},{4,2},{6,4},{7,6},{5,7},{3,5},{1,3},{8,9},{10,8},{12,1... | collective-permute-start | bytes 393224 | tf_op jit(solution)/shard_map/ppermute | solution.py:55
  173.7 4.3 %collective-permute-start.28 = (f32[16,1024]{1,0:T(8,128)S(1)}, f32[16,1024]{1,0:T(8,128)S(1)}, u32[]{:S(2)}, u32[]{:S(2)}) collective-permute-start(f32[16,1024]{1,0:T(8,128)S(1)} %slice.281), channel_id=1, source_target_pairs={{0,2},{2,4},{4,6},{6,7},{7,5},{5,3},{3,1},{1,0},{8,10},{10,12},{12... | collective-permute-start | bytes 196616 | tf_op jit(solution)/shard_map/ppermute | solution.py:55
  178.0 4.3 %collective-permute-start.32 = (f32[16,1024]{1,0:T(8,128)S(1)}, f32[16,1024]{1,0:T(8,128)S(1)}, u32[]{:S(2)}, u32[]{:S(2)}) collective-permute-start(f32[16,1024]{1,0:T(8,128)S(1)} %get-tuple-element.27), channel_id=1, source_target_pairs={{0,1},{2,0},{4,2},{6,4},{7,6},{5,7},{3,5},{1,3},{8,9},{10,8},{12,1... | collective-permute-start | bytes 196616 | tf_op jit(solution)/shard_map/ppermute | solution.py:55
  180.1 5.0 %collective-permute-start.29 = (f32[32,1024]{1,0:T(8,128)S(1)}, f32[32,1024]{1,0:T(8,128)S(1)}, u32[]{:S(2)}, u32[]{:S(2)}) collective-permute-start(f32[32,1024]{1,0:T(8,128)S(1)} %pad_maximum_fusion.7), channel_id=1, source_target_pairs={{0,2},{2,4},{4,6},{6,7},{7,5},{5,3},{3,1},{1,0},{8,10},{10,12},{12... | collective-permute-start | bytes 393224 | tf_op jit(solution)/shard_map/ppermute | solution.py:55
  182.4 5.0 %collective-permute-start.33 = (f32[32,1024]{1,0:T(8,128)S(1)}, f32[32,1024]{1,0:T(8,128)S(1)}, u32[]{:S(2)}, u32[]{:S(2)}) collective-permute-start(f32[32,1024]{1,0:T(8,128)S(1)} %pad_maximum_fusion.8), channel_id=1, source_target_pairs={{0,1},{2,0},{4,2},{6,4},{7,6},{5,7},{3,5},{1,3},{8,9},{10,8},{12,1... | collective-permute-start | bytes 393224 | tf_op jit(solution)/shard_map/ppermute | solution.py:55
  185.2 5.0 %collective-permute-start.30 = (f32[32,1024]{1,0:T(8,128)S(1)}, f32[32,1024]{1,0:T(8,128)S(1)}, u32[]{:S(2)}, u32[]{:S(2)}) collective-permute-start(f32[32,1024]{1,0:T(8,128)S(1)} %slice_add_fusion.9), channel_id=1, source_target_pairs={{0,2},{2,4},{4,6},{6,7},{7,5},{5,3},{3,1},{1,0},{8,10},{10,12},{12... | collective-permute-start | bytes 393224 | tf_op jit(solution)/shard_map/ppermute | solution.py:55
  185.3 6.9 %collective-permute-start.22 = (f32[128,256]{0,1:T(8,128)S(1)}, f32[128,256]{0,1:T(8,128)S(1)}, u32[]{:S(2)}, u32[]{:S(2)}) collective-permute-start(f32[128,256]{0,1:T(8,128)S(1)} %get-tuple-element.37), channel_id=1, source_target_pairs={{0,8},{8,0},{16,24},{24,16},{1,9},{9,1},{17,25},{25,17},{2,10},{10... | collective-permute-start | bytes 393224 | tf_op jit(solution)/shard_map/ppermute | solution.py:23
  187.4 5.0 %collective-permute-start.23 = (f32[128,256]{0,1:T(8,128)S(1)}, f32[128,256]{0,1:T(8,128)S(1)}, u32[]{:S(2)}, u32[]{:S(2)}) collective-permute-start(f32[128,256]{0,1:T(8,128)S(1)} %get-tuple-element.36), channel_id=1, source_target_pairs={{0,16},{8,24},{16,0},{24,8},{1,17},{9,25},{17,1},{25,9},{2,18},{10... | collective-permute-start | bytes 393224 | tf_op jit(solution)/shard_map/ppermute | solution.py:23
  190.2 5.0 %collective-permute-start.24 = (f32[128,256]{0,1:T(8,128)S(1)}, f32[128,256]{0,1:T(8,128)S(1)}, u32[]{:S(2)}, u32[]{:S(2)}) collective-permute-start(f32[128,256]{0,1:T(8,128)S(1)} %get-tuple-element.35), channel_id=1, source_target_pairs={{0,24},{8,16},{16,8},{24,0},{1,25},{9,17},{17,9},{25,1},{2,26},{10... | collective-permute-start | bytes 393224 | tf_op jit(solution)/shard_map/ppermute | solution.py:23
  190.2 8.5 %collective-permute-start.34 = (f32[32,1024]{1,0:T(8,128)S(1)}, f32[32,1024]{1,0:T(8,128)S(1)}, u32[]{:S(2)}, u32[]{:S(2)}) collective-permute-start(f32[32,1024]{1,0:T(8,128)S(1)} %get-tuple-element.25), channel_id=1, source_target_pairs={{0,1},{2,0},{4,2},{6,4},{7,6},{5,7},{3,5},{1,3},{8,9},{10,8},{12,1... | collective-permute-start | bytes 393224 | tf_op jit(solution)/shard_map/ppermute | solution.py:55
  198.0 5.6 %collective-permute-start.31 = (f32[32,1024]{1,0:T(8,128)S(1)}, f32[32,1024]{1,0:T(8,128)S(1)}, u32[]{:S(2)}, u32[]{:S(2)}) collective-permute-start(f32[32,1024]{1,0:T(8,128)S(1)} %get-tuple-element.24), channel_id=1, source_target_pairs={{0,2},{2,4},{4,6},{6,7},{7,5},{5,3},{3,1},{1,0},{8,10},{10,12},{12... | collective-permute-start | bytes 393224 | tf_op jit(solution)/shard_map/ppermute | solution.py:55
  198.8 5.1 %collective-permute-start.35 = (f32[32,1024]{1,0:T(8,128)S(1)}, f32[32,1024]{1,0:T(8,128)S(1)}, u32[]{:S(2)}, u32[]{:S(2)}) collective-permute-start(f32[32,1024]{1,0:T(8,128)S(1)} %slice_add_fusion.8), channel_id=1, source_target_pairs={{0,1},{2,0},{4,2},{6,4},{7,6},{5,7},{3,5},{1,3},{8,9},{10,8},{12,1... | collective-permute-start | bytes 393224 | tf_op jit(solution)/shard_map/ppermute | solution.py:55
  (21 other events, 117.9 us)

commit v2 on v1

--- a/solution.py
+++ b/solution.py
@@ -1,6 +1,10 @@
+import functools
+
 import jax
 import jax.numpy as jnp
 from jax import lax
+from jax.experimental import pallas as pl
+from jax.experimental.pallas import tpu as pltpu
 from jax.sharding import PartitionSpec as P
 
 
@@ -55,7 +59,7 @@
     return lax.ppermute(block, "gy", [(order[k], order[(k + step) % size]) for k in range(size)])
 
 
-def gy_gather(block):
+def gy_pieces(block):
     size = lax.axis_size("gy")
     half = block.shape[0] // 2
     pieces = [None] * size
@@ -64,8 +68,12 @@
     for step in range(1, size // 2):
         ahead, behind = ring_step(ahead, -1), ring_step(behind, 1)
         pieces[step], pieces[size - step] = ahead, behind
-    pieces[size // 2] = jnp.concatenate([ring_step(ahead[:half], -1), ring_step(behind[half:], 1)], axis=0)
-    return jnp.concatenate(pieces, axis=0)
+    pieces[size // 2 : size // 2 + 1] = [ring_step(ahead[:half], -1), ring_step(behind[half:], 1)]
+    return pieces
+
+
+def gy_gather(block):
+    return jnp.concatenate(gy_pieces(block), axis=0)
 
 
 def gy_reduce(blocks):
@@ -82,7 +90,7 @@
     return blocks[0] + ring_step(ahead, 1) + ring_step(behind, -1)
 
 
-def on_device(stem_first, cotangent, branch_first, branch_second, bond_first, bond_second):
+def plain(stem_first, cotangent, branch_first, branch_second, bond_first, bond_second):
     groups, splits = lax.axis_size("gx"), lax.axis_size("gy")
     me_x, me_y = lax.axis_index("gx"), lax.axis_index("gy")
     height, width = stem_first.shape[1:]
@@ -135,6 +143,256 @@
     grad = gx_exchange([grad[rel * height : (rel + 1) * height] for rel in range(groups)])
     grad_stem = jnp.take(jnp.concatenate(grad, axis=1), back_first, axis=1).reshape(1, height, width)
     return (grad_stem, grad_first * factor, grad_second * factor)
+
+
+def split(value):
+    high = value.astype(jnp.bfloat16)
+    return high, (value - high.astype(jnp.float32)).astype(jnp.bfloat16)
+
+
+def dot(left, right, contract):
+    return lax.dot_general(left, right, (contract, ((), ())), preferred_element_type=jnp.float32)
+
+
+def dot_parts(left, right, contract):
+    return dot(left[0], right[0], contract) + dot(left[0], right[1], contract) + dot(left[1], right[0], contract)
+
+
+def ring_owner(offset):
+    size = lax.axis_size("gy")
+    me = lax.axis_index("gy")
+    place = jnp.where(me % 2 == 0, me // 2, size - 1 - me // 2)
+    place = (place + offset) % size
+    return jnp.where(place < size // 2, 2 * place, 2 * (size - 1 - place) + 1)
+
+
+def group(rel):
+    return lax.axis_index("gx") ^ rel
+
+
+def piece_rows(own, size):
+    found = []
+    for k in range(size):
+        found += [(k, 0, own)] if k != size // 2 else [(k, 0, own // 2), (k, own // 2, own // 2)]
+    return found
+
+
+def aligned(index, size):
+    return pl.ds(pl.multiple_of(index * size, size), size)
+
+
+def store_split(high_ref, low_ref, where, value):
+    high_ref[where], low_ref[where] = split(value)
+
+
+def load_branch(pieces, high_ref, low_ref, own):
+    size = lax.axis_size("gy")
+    for ref, (k, first, count) in zip(pieces, piece_rows(own, size), strict=True):
+        start = pl.multiple_of(ring_owner(k) * own + first, count)
+        store_split(high_ref, low_ref, pl.ds(start, count), ref[...])
+
+
+def chosen(bond_ref, rel, low, width):
+    columns = bond_ref[:, aligned(group(rel), low)]
+    position = lax.broadcasted_iota(jnp.int32, (width, low), 0)
+    return (position == columns).astype(jnp.bfloat16)
+
+
+def pick_kernel(stem_ref, bond_ref, *out_refs):
+    high, low_part = split(stem_ref[...])
+    width = stem_ref.shape[1]
+    for rel, out_ref in enumerate(out_refs):
+        select = chosen(bond_ref, rel, out_ref.shape[1], width)
+        out_ref[...] = dot(high, select, ((1,), (0,))) + dot(low_part, select, ((1,), (0,)))
+
+
+def mid_kernel(groups, own, bond_ref, *refs):
+    picked, refs = refs[:groups], refs[groups:]
+    out_refs, (branch_high, branch_low), (mid_high, mid_low) = refs[-groups - 4 : -4], refs[-4:-2], refs[-2:]
+    pieces = refs[: -groups - 4]
+    height, low = picked[0].shape
+    width = groups * low
+    load_branch(pieces, branch_high, branch_low, own)
+    branch = branch_high[...], branch_low[...]
+    for rel, ref in enumerate(picked):
+        high, low_part = split(dot_parts(split(ref[...]), branch, ((1,), (0,))))
+        columns = aligned(group(rel), low)
+        for h in range(groups):
+            mid_high[h * height : (h + 1) * height, columns] = high[:, h * low : (h + 1) * low]
+            mid_low[h * height : (h + 1) * height, columns] = low_part[:, h * low : (h + 1) * low]
+    for rel, out_ref in enumerate(out_refs):
+        select = chosen(bond_ref, rel, low, width)
+        out_ref[...] = dot(mid_high[...], select, ((1,), (0,))) + dot(mid_low[...], select, ((1,), (0,)))
+
+
+def back_kernel(groups, own, *refs):
+    cotan, refs = refs[:groups], refs[groups:]
+    pieces, (out_ref, cotan_high, cotan_low, branch_high, branch_low) = refs[:-5], refs[-5:]
+    height = cotan[0].shape[0]
+    load_branch(pieces, branch_high, branch_low, own)
+    branch = branch_high[...], branch_low[...]
+    for rel, ref in enumerate(cotan):
+        parts = split(ref[...])
+        rows = aligned(group(rel), height)
+        cotan_high[rows], cotan_low[rows] = parts
+        out_ref[rows] = dot_parts(parts, branch, ((1,), (1,)))
+
+
+def put_blocks(total, out_refs, total_ref):
+    own = out_refs[0].shape[0]
+    total_ref[...] = total
+    for k, out_ref in enumerate(out_refs):
+        out_ref[...] = total_ref[aligned(ring_owner(k), own)]
+
+
+def second_kernel(factor, near_ref, far_ref, cotan_high, cotan_low, *refs):
+    out_refs, total_ref = refs[:-1], refs[-1]
+    regrouped = (near_ref[...] + far_ref[...]) * factor
+    parts = split(regrouped.T)
+    put_blocks(dot_parts(parts, (cotan_high[...], cotan_low[...]), ((1,), (0,))), out_refs, total_ref)
+
+
+def first_kernel(groups, factor, bond_ref, *refs):
+    back, picked, refs = refs[:groups], refs[groups : 2 * groups], refs[2 * groups :]
+    out_refs, (back_high, back_low, picked_high, picked_low, total_ref) = refs[:-5], refs[-5:]
+    height, low = picked[0].shape
+    width = groups * low
+    total = None
+    for rel, ref in enumerate(back):
+        select = chosen(bond_ref, rel, low, width)
+        high, low_part = split(ref[...])
+        term = dot(high, select, ((1,), (1,))) + dot(low_part, select, ((1,), (1,)))
+        total = term if total is None else total + term
+    for h in range(groups):
+        for a in range(groups):
+            value = total[h * height : (h + 1) * height, a * low : (a + 1) * low]
+            where = (slice(a * height, (a + 1) * height), slice(h * low, (h + 1) * low))
+            store_split(back_high, back_low, where, value)
+    for rel, ref in enumerate(picked):
+        store_split(picked_high, picked_low, (slice(None), aligned(group(rel), height)), (ref[...] * factor).T)
+    parts = (picked_high[...], picked_low[...])
+    put_blocks(dot_parts(parts, (back_high[...], back_low[...]), ((1,), (0,))), out_refs, total_ref)
+
+
+def stem_kernel(groups, back_high, back_low, branch_high, branch_low, *out_refs):
+    height = out_refs[0].shape[0]
+    branch = branch_high[...], branch_low[...]
+    for rel, out_ref in enumerate(out_refs):
+        rows = aligned(group(rel), height)
+        out_ref[...] = dot_parts((back_high[rows], back_low[rows]), branch, ((1,), (1,)))
+
+
+def place_kernel(bond_ref, *refs):
+    blocks, out_ref = refs[:-1], refs[-1]
+    total = None
+    for rel, ref in enumerate(blocks):
+        select = chosen(bond_ref, rel, ref.shape[1], out_ref.shape[1])
+        high, low_part = split(ref[...])
+        term = dot(high, select, ((1,), (1,))) + dot(low_part, select, ((1,), (1,)))
+        total = term if total is None else total + term
+    out_ref[...] = total
+
+
+def call(kernel, name, outs, flops, scratch, *operands):
+    moved = sum(x.size * x.dtype.itemsize for x in (*operands, *outs))
+    whole = pl.BlockSpec(memory_space=pltpu.VMEM)
+    return pl.pallas_call(
+        kernel,
+        name=name,
+        out_shape=outs,
+        in_specs=[whole] * len(operands),
+        out_specs=[whole] * len(outs),
+        scratch_shapes=scratch,
+        compiler_params=pltpu.CompilerParams(vmem_limit_bytes=32 * 1024 * 1024),
+        cost_estimate=pl.CostEstimate(flops=flops, bytes_accessed=moved, transcendentals=0),
+    )(*operands)
+
+
+def f32(*shape):
+    return jax.ShapeDtypeStruct(shape, jnp.float32)
+
+
+def b16(*shape):
+    return jax.ShapeDtypeStruct(shape, jnp.bfloat16)
+
+
+def on_device(stem_first, cotangent, branch_first, branch_second, bond_first, bond_second):
+    groups, splits = lax.axis_size("gx"), lax.axis_size("gy")
+    height, width = stem_first.shape[1:]
+    low = width // groups
+    own = width // (groups * splits)
+    if groups != 4 or low % 128 or own % 32 or height % 128:
+        return plain(stem_first, cotangent, branch_first, branch_second, bond_first, bond_second)
+    factor = (height * groups * splits) ** -0.5
+    tall = groups * height
+    unit = 2 * height * width * width
+    first_bond, second_bond = bond_first.reshape(1, width), bond_second.reshape(1, width)
+    stem_rows, cotan_rows = stem_first.reshape(height, width), cotangent.reshape(height, width)
+    blocks = [f32(own, width)] * splits
+
+    picked = call(pick_kernel, "pick", [f32(height, low)] * groups, 2 * unit, [], stem_rows, first_bond)
+    picked = gx_exchange(picked)
+    pieces_first = gy_pieces(branch_first)
+    cotan = gx_gather(cotan_rows)
+    pieces_second = gy_pieces(branch_second)
+
+    *partial, first_high, first_low = call(
+        functools.partial(mid_kernel, groups, own),
+        "mid",
+        [f32(tall, low)] * groups + [b16(low, width)] * 2,
+        3 * unit + 2 * groups * unit,
+        [pltpu.VMEM((tall, width), jnp.bfloat16)] * 2,
+        second_bond,
+        *picked,
+        *pieces_first,
+    )
+    back, cotan_high, cotan_low = call(
+        functools.partial(back_kernel, groups, own),
+        "back",
+        [f32(tall, low)] + [b16(tall, width)] * 2,
+        3 * unit,
+        [pltpu.VMEM((low, width), jnp.bfloat16)] * 2,
+        *cotan,
+        *pieces_second,
+    )
+    near, far = partial[0] + swap(partial[1], 1), partial[2] + swap(partial[3], 1)
+    outer_second = call(
+        functools.partial(second_kernel, factor),
+        "grad_second",
+        blocks,
+        3 * unit,
+        [pltpu.VMEM((low, width), jnp.float32)],
+        near,
+        swap(far, 2),
+        cotan_high,
+        cotan_low,
+    )
+    grad_second = gy_reduce(outer_second)
+
+    *outer_first, back_high, back_low = call(
+        functools.partial(first_kernel, groups, factor),
+        "grad_first",
+        blocks + [b16(tall, width)] * 2,
+        3 * unit + 2 * groups * unit,
+        [pltpu.VMEM((low, tall), jnp.bfloat16)] * 2 + [pltpu.VMEM((low, width), jnp.float32)],
+        second_bond,
+        *gx_gather(back),
+        *picked,
+    )
+    grad_first = gy_reduce(outer_first)
+    grad = call(
+        functools.partial(stem_kernel, groups),
+        "grad_stem",
+        [f32(height, low)] * groups,
+        3 * unit,
+        [],
+        back_high,
+        back_low,
+        first_high,
+        first_low,
+    )
+    grad = call(place_kernel, "place", [f32(height, width)], 2 * unit, [], first_bond, *gx_exchange(grad))[0]
+    return grad.reshape(1, height, width), grad_first, grad_second
 
 
 def solution(mesh):

time: 206 us -> 109 us (0.53)
  local copies, waits for them, and re-layouts: 71.5 us -> 1.79 us
  waiting for transfers between devices: 67.3 us -> 38.7 us
  Pallas kernels: 0 us -> 16.2 us
  other arithmetic: 13 us -> 1.74 us
  matrix products: 10.9 us -> 0 us
  starting transfers between devices: 41.3 us -> 49.2 us
    ppermute x32, waiting for transfers between devices: 57.8 us -> 27.5 us  [ring_step(): lax.ppermute(block, 'gy', [(order[k], order[(k + step) % size]) for k in...]
    gather x11 -> x0, local copies, waits for them, and re-layouts: 28.3 us -> none  [the longest x2 9.06 us: on_device(): bond_first, bond_second = (bond_first[rows], bond_second[rows])]
    pallas_call x0 -> x7, Pallas kernels: none -> 16.2 us  [call(): pl.pallas_call(kernel, name=name, out_shape=outs, in_specs=[whole] * len(...]
    dot_general x5 -> x0, matrix products: 10.9 us -> none  [product(): lax.dot_general(left, right, (contract, ((), ())), precision=lax.Precisio...]
    unnamed x57 -> x14, local copies, waits for them, and re-layouts: 11.9 us -> 1.75 us
    scatter x2 -> x0, local copies, waits for them, and re-layouts: 8.62 us -> none  [inverse(): jnp.zeros_like(ordering).at[ordering]]
    reshape x6 -> x0, local copies, waits for them, and re-layouts: 7.11 us -> none  [the longest x2 4.58 us: on_device(): back_mid.reshape(groups, height, groups, low).transpose(2, 1, 0, 3)]
    concatenate x2 -> x0, local copies, waits for them, and re-layouts: 4.9 us -> none  [gy_gather(): return jnp.concatenate(pieces, axis=0)]
  transfers between devices with their start and end apart: 47 -> 47, of which waited for: 22 -> 18; matrix products, arithmetic and copies ran while one was open for 44% -> 1% of each run, Pallas kernels for 0% -> 15%
where the time goes in v2:
time: 109 us
  starting transfers between devices  49.2 us (45%)
  waiting for transfers between devices  38.7 us (36%)
  Pallas kernels  16.2 us (15%)
  local copies, waits for them, and re-layouts  1.79 us (2%)
  other arithmetic  1.74 us (2%)
    ppermute x32, starting transfers between devices, ring_step(): lax.ppermute(block, 'gy', [(order[k], order[(k + step) % size]) for k in...  39.2 us
    ppermute x32, waiting for transfers between devices, ring_step(): lax.ppermute(block, 'gy', [(order[k], order[(k + step) % size]) for k in...  27.5 us
    pallas_call x7, Pallas kernels, call(): pl.pallas_call(kernel, name=name, out_shape=outs, in_specs=[whole] * len(...  16.2 us
    ppermute x15, waiting for transfers between devices, swap(): return lax.ppermute(block, 'gx', [(i, i ^ mask) for i in range(size)])  11.2 us
    ppermute x15, starting transfers between devices, swap(): return lax.ppermute(block, 'gx', [(i, i ^ mask) for i in range(size)])  10 us
  transfers between devices with their start and end apart: 47, of which 18 were waited for; matrix products, arithmetic and copies ran while one was open for 1% of the time, Pallas kernels for 15%

profile of v2, /device:TPU:0, one launch (start us, length us, event | category | flops | bytes accessed | tf_op | source)
XLA Modules:
  0.0 108.6 jit_solution(17931470680674154040)
XLA Ops:
  0.6 3.0 %collective-permute-start.17 = (f32[32,1024]{1,0:T(8,128)}, f32[32,1024]{1,0:T(8,128)S(1)}, u32[]{:S(2)}, u32[]{:S(2)}) collective-permute-start(f32[32,1024]{1,0:T(8,128)} %refs_4_.3), channel_id=1, source_target_pairs={{0,1},{2,0},{4,2},{6,4},{7,6},{5,7},{3,5},{1,3},{8,9},{10,8},{12,1... | collective-permute-start | bytes 393224 | tf_op jit(solution)/shard_map/ppermute | solution.py:59
  3.8 3.6 %collective-permute-done.17.refs_5_ = f32[32,1024]{1,0:T(8,128)S(1)} collective-permute-done((f32[32,1024]{1,0:T(8,128)}, f32[32,1024]{1,0:T(8,128)S(1)}, u32[]{:S(2)}, u32[]{:S(2)}) %collective-permute-start.17) | collective-permute-done | bytes 131104 | tf_op jit(solution)/shard_map/ppermute | solution.py:59
  7.4 1.7 %collective-permute-start.18 = (f32[32,1024]{1,0:T(8,128)S(1)}, f32[32,1024]{1,0:T(8,128)S(1)}, u32[]{:S(2)}, u32[]{:S(2)}) collective-permute-start(f32[32,1024]{1,0:T(8,128)S(1)} %collective-permute-done.17.refs_5_), channel_id=1, source_target_pairs={{0,1},{2,0},{4,2},{6,4},{7,6},{5,7},{3,5},{1,3},{8,9},{10,8},{12,1... | collective-permute-start | bytes 393224 | tf_op jit(solution)/shard_map/ppermute | solution.py:59
  9.4 2.9 %collective-permute-done.18.refs_6_ = f32[32,1024]{1,0:T(8,128)S(1)} collective-permute-done((f32[32,1024]{1,0:T(8,128)S(1)}, f32[32,1024]{1,0:T(8,128)S(1)}, u32[]{:S(2)}, u32[]{:S(2)}) %collective-permute-start.18) | collective-permute-done | bytes 131104 | tf_op jit(solution)/shard_map/ppermute | solution.py:59
  12.4 1.7 %collective-permute-start.19 = (f32[32,1024]{1,0:T(8,128)S(1)}, f32[32,1024]{1,0:T(8,128)S(1)}, u32[]{:S(2)}, u32[]{:S(2)}) collective-permute-start(f32[32,1024]{1,0:T(8,128)S(1)} %collective-permute-done.18.refs_6_), channel_id=1, source_target_pairs={{0,1},{2,0},{4,2},{6,4},{7,6},{5,7},{3,5},{1,3},{8,9},{10,8},{12,1... | collective-permute-start | bytes 393224 | tf_op jit(solution)/shard_map/ppermute | solution.py:59
  14.4 1.0 copy-done.2
  16.1 1.0 pick.1
  17.3 1.7 %collective-permute-start.15 = (f32[128,256]{1,0:T(8,128)S(1)}, f32[128,256]{1,0:T(8,128)S(1)}, u32[]{:S(2)}, u32[]{:S(2)}) collective-permute-start(f32[128,256]{1,0:T(8,128)S(1)} %get-tuple-element.41), channel_id=1, source_target_pairs={{0,16},{8,24},{16,0},{24,8},{1,17},{9,25},{17,1},{25,9},{2,18},{10... | collective-permute-start | bytes 393224 | tf_op jit(solution)/shard_map/ppermute | solution.py:27
  19.1 1.7 %collective-permute-start.20 = (f32[16,1024]{1,0:T(8,128)S(1)}, f32[16,1024]{1,0:T(8,128)S(1)}, u32[]{:S(2)}, u32[]{:S(2)}) collective-permute-start(f32[16,1024]{1,0:T(8,128)S(1)} %slice.66), channel_id=1, source_target_pairs={{0,1},{2,0},{4,2},{6,4},{7,6},{5,7},{3,5},{1,3},{8,9},{10,8},{12,1... | collective-permute-start | bytes 196616 | tf_op jit(solution)/shard_map/ppermute | solution.py:59
  21.3 1.7 %collective-permute-start.1 = (f32[128,1024]{1,0:T(8,128)S(1)}, f32[128,1024]{1,0:T(8,128)S(1)}, u32[]{:S(2)}, u32[]{:S(2)}) collective-permute-start(f32[128,1024]{1,0:T(8,128)S(1)} %bitcast.5), channel_id=1, source_target_pairs={{0,16},{8,24},{16,0},{24,8},{1,17},{9,25},{17,1},{25,9},{2,18},{10... | collective-permute-start | bytes 1572872 | tf_op jit(solution)/shard_map/ppermute | solution.py:27
  23.6 2.0 %collective-permute-done.16.refs_7_.refs_3_ = f32[128,256]{1,0:T(8,128)S(1)} collective-permute-done((f32[128,256]{1,0:T(8,128)S(1)}, f32[128,256]{1,0:T(8,128)S(1)}, u32[]{:S(2)}, u32[]{:S(2)}) %collective-permute-start.16) | collective-permute-done | bytes 131104 | tf_op jit(solution)/shard_map/ppermute | solution.py:27
  25.6 3.7 %mid.1 = (f32[512,256]{1,0:T(8,128)S(1)}, f32[512,256]{1,0:T(8,128)S(1)}, f32[512,256]{1,0:T(8,128)S(1)}, f32[512,256]{1,0:T(8,128)S(1)}, bf16[256,1024]{1,0:T(8,128)(2,1)S(1)}, /*index=5*/bf16[256,1024]{1,0:T(8,128)(2,1)S(1)}) custom-call(s32[1,1024]{1,0:T(1,128)S(1)} %bitcast.9, f32[128,256]{1,0:T(8,128)S(1)} %get-tuple-element.39.refs_4_.refs_0_, ...), custom_call_target="tpu_custom_call" | custom-call | flops 2952790016 | bytes 4722688 | tf_op jit(solution)/shard_map/mid/pallas_call | solution.py:299
  30.1 1.7 %collective-permute-start.7 = (f32[32,1024]{1,0:T(8,128)S(1)}, f32[32,1024]{1,0:T(8,128)S(1)}, u32[]{:S(2)}, u32[]{:S(2)}) collective-permute-start(f32[32,1024]{1,0:T(8,128)S(1)} %copy-done.1), channel_id=1, source_target_pairs={{0,2},{2,4},{4,6},{6,7},{7,5},{5,3},{3,1},{1,0},{8,10},{10,12},{12... | collective-permute-start | bytes 393224 | tf_op jit(solution)/shard_map/ppermute | solution.py:59
  32.1 3.4 %collective-permute-done.7.refs_12_ = f32[32,1024]{1,0:T(8,128)S(1)} collective-permute-done((f32[32,1024]{1,0:T(8,128)S(1)}, f32[32,1024]{1,0:T(8,128)S(1)}, u32[]{:S(2)}, u32[]{:S(2)}) %collective-permute-start.7) | collective-permute-done | bytes 131104 | tf_op jit(solution)/shard_map/ppermute | solution.py:59
  35.6 1.7 %collective-permute-start.8 = (f32[32,1024]{1,0:T(8,128)S(1)}, f32[32,1024]{1,0:T(8,128)S(1)}, u32[]{:S(2)}, u32[]{:S(2)}) collective-permute-start(f32[32,1024]{1,0:T(8,128)S(1)} %collective-permute-done.7.refs_12_), channel_id=1, source_target_pairs={{0,2},{2,4},{4,6},{6,7},{7,5},{5,3},{3,1},{1,0},{8,10},{10,12},{12... | collective-permute-start | bytes 393224 | tf_op jit(solution)/shard_map/ppermute | solution.py:59
  37.8 1.1 collective-permute-start.4
  38.9 1.6 %collective-permute-done.8.refs_11_ = f32[32,1024]{1,0:T(8,128)S(1)} collective-permute-done((f32[32,1024]{1,0:T(8,128)S(1)}, f32[32,1024]{1,0:T(8,128)S(1)}, u32[]{:S(2)}, u32[]{:S(2)}) %collective-permute-start.8) | collective-permute-done | bytes 131104 | tf_op jit(solution)/shard_map/ppermute | solution.py:59
  40.5 1.7 %collective-permute-start.9 = (f32[32,1024]{1,0:T(8,128)S(1)}, f32[32,1024]{1,0:T(8,128)S(1)}, u32[]{:S(2)}, u32[]{:S(2)}) collective-permute-start(f32[32,1024]{1,0:T(8,128)S(1)} %collective-permute-done.8.refs_11_), channel_id=1, source_target_pairs={{0,2},{2,4},{4,6},{6,7},{7,5},{5,3},{3,1},{1,0},{8,10},{10,12},{12... | collective-permute-start | bytes 393224 | tf_op jit(solution)/shard_map/ppermute | solution.py:59
  42.4 0.9 collective-permute-done.4.refs_6_
  43.3 1.5 %collective-permute-start.38 = (f32[512,256]{1,0:T(8,128)S(1)}, f32[512,256]{1,0:T(8,128)S(1)}, u32[]{:S(2)}, u32[]{:S(2)}) collective-permute-start(f32[512,256]{1,0:T(8,128)S(1)} %add.63), channel_id=1, source_target_pairs={{0,16},{8,24},{16,0},{24,8},{1,17},{9,25},{17,1},{25,9},{2,18},{10... | collective-permute-start | bytes 1572872 | tf_op jit(solution)/shard_map/ppermute | solution.py:27
  45.5 1.7 %collective-permute-start.5 = (f32[32,1024]{1,0:T(8,128)S(1)}, f32[32,1024]{1,0:T(8,128)S(1)}, u32[]{:S(2)}, u32[]{:S(2)}) collective-permute-start(f32[32,1024]{1,0:T(8,128)S(1)} %collective-permute-done.4.refs_6_), channel_id=1, source_target_pairs={{0,1},{2,0},{4,2},{6,4},{7,6},{5,7},{3,5},{1,3},{8,9},{10,8},{12,1... | collective-permute-start | bytes 393224 | tf_op jit(solution)/shard_map/ppermute | solution.py:59
  47.2 3.3 %collective-permute-done.5.refs_7_ = f32[32,1024]{1,0:T(8,128)S(1)} collective-permute-done((f32[32,1024]{1,0:T(8,128)S(1)}, f32[32,1024]{1,0:T(8,128)S(1)}, u32[]{:S(2)}, u32[]{:S(2)}) %collective-permute-start.5) | collective-permute-done | bytes 131104 | tf_op jit(solution)/shard_map/ppermute | solution.py:59
  50.5 1.7 %collective-permute-start.10 = (f32[16,1024]{1,0:T(8,128)S(1)}, f32[16,1024]{1,0:T(8,128)S(1)}, u32[]{:S(2)}, u32[]{:S(2)}) collective-permute-start(f32[16,1024]{1,0:T(8,128)S(1)} %slice.65), channel_id=1, source_target_pairs={{0,2},{2,4},{4,6},{6,7},{7,5},{5,3},{3,1},{1,0},{8,10},{10,12},{12... | collective-permute-start | bytes 196616 | tf_op jit(solution)/shard_map/ppermute | solution.py:59
  52.2 2.5 %collective-permute-done.10.refs_9_ = f32[16,1024]{1,0:T(8,128)S(1)} collective-permute-done((f32[16,1024]{1,0:T(8,128)S(1)}, f32[16,1024]{1,0:T(8,128)S(1)}, u32[]{:S(2)}, u32[]{:S(2)}) %collective-permute-start.10) | collective-permute-done | bytes 65568 | tf_op jit(solution)/shard_map/ppermute | solution.py:59
  54.8 1.7 %collective-permute-start.6 = (f32[16,1024]{1,0:T(8,128)S(1)}, f32[16,1024]{1,0:T(8,128)S(1)}, u32[]{:S(2)}, u32[]{:S(2)}) collective-permute-start(f32[16,1024]{1,0:T(8,128)S(1)} %slice.64), channel_id=1, source_target_pairs={{0,1},{2,0},{4,2},{6,4},{7,6},{5,7},{3,5},{1,3},{8,9},{10,8},{12,1... | collective-permute-start | bytes 196616 | tf_op jit(solution)/shard_map/ppermute | solution.py:59
  56.4 2.6 %collective-permute-done.6.refs_8_ = f32[16,1024]{1,0:T(8,128)S(1)} collective-permute-done((f32[16,1024]{1,0:T(8,128)S(1)}, f32[16,1024]{1,0:T(8,128)S(1)}, u32[]{:S(2)}, u32[]{:S(2)}) %collective-permute-start.6) | collective-permute-done | bytes 65568 | tf_op jit(solution)/shard_map/ppermute | solution.py:59
  59.0 2.4 %back.1 = (f32[512,256]{1,0:T(8,128)S(1)}, bf16[512,1024]{1,0:T(8,128)(2,1)S(1)}, bf16[512,1024]{1,0:T(8,128)(2,1)S(1)}) custom-call(f32[128,1024]{1,0:T(8,128)S(1)} %bitcast.7, f32[128,1024]{1,0:T(8,128)S(1)} %collective-permute-done.refs_1_, f32[128,1024]{1,0:T(8,128)S(1)} %collective-permute-done.1.refs_2_, ...), custom_call_target="tpu_custom_call" | custom-call | flops 805306368 | bytes 5767168 | tf_op jit(solution)/shard_map/back/pallas_call | solution.py:299
  61.4 1.7 %collective-permute-start.12 = (f32[512,256]{1,0:T(8,128)S(1)}, f32[512,256]{1,0:T(8,128)S(1)}, u32[]{:S(2)}, u32[]{:S(2)}) collective-permute-start(f32[512,256]{1,0:T(8,128)S(1)} %get-tuple-element.38.refs_0_), channel_id=1, source_target_pairs={{0,16},{8,24},{16,0},{24,8},{1,17},{9,25},{17,1},{25,9},{2,18},{10... | collective-permute-start | bytes 1572872 | tf_op jit(solution)/shard_map/ppermute | solution.py:27
  63.2 1.1 %grad_second.1 = (f32[32,1024]{1,0:T(8,128)S(1)}, f32[32,1024]{1,0:T(8,128)S(1)}, f32[32,1024]{1,0:T(8,128)S(1)}, f32[32,1024]{1,0:T(8,128)S(1)}, f32[32,1024]{1...) custom-call(f32[512,256]{1,0:T(8,128)S(1)} %add.62.near_ref, ...), custom_call_target="tpu_custom_call" | custom-call | flops 805306368 | bytes 4194304 | tf_op jit(solution)/shard_map/grad_second/pallas_call | solution.py:299
  64.4 1.6 %collective-permute-start.39 = (f32[16,1024]{1,0:T(8,128)S(1)}, f32[16,1024]{1,0:T(8,128)S(1)}, u32[]{:S(2)}, u32[]{:S(2)}) collective-permute-start(f32[16,1024]{1,0:T(8,128)S(1)} %get-tuple-element.75), channel_id=1, source_target_pairs={{0,2},{2,4},{4,6},{6,7},{7,5},{5,3},{3,1},{1,0},{8,10},{10,12},{12... | collective-permute-start | bytes 196616 | tf_op jit(solution)/shard_map/ppermute | solution.py:59
  66.4 5.0 %collective-permute-done.12.refs_2_ = f32[512,256]{1,0:T(8,128)S(1)} collective-permute-done((f32[512,256]{1,0:T(8,128)S(1)}, f32[512,256]{1,0:T(8,128)S(1)}, u32[]{:S(2)}, u32[]{:S(2)}) %collective-permute-start.12) | collective-permute-done | bytes 524320 | tf_op jit(solution)/shard_map/ppermute | solution.py:27
  71.5 1.8 %collective-permute-start.40 = (f32[32,1024]{1,0:T(8,128)S(1)}, f32[32,1024]{1,0:T(8,128)S(1)}, u32[]{:S(2)}, u32[]{:S(2)}) collective-permute-start(f32[32,1024]{1,0:T(8,128)S(1)} %pad_maximum_fusion.2), channel_id=1, source_target_pairs={{0,2},{2,4},{4,6},{6,7},{7,5},{5,3},{3,1},{1,0},{8,10},{10,12},{12... | collective-permute-start | bytes 393224 | tf_op jit(solution)/shard_map/ppermute | solution.py:59
  73.3 3.5 %grad_first.1 = (f32[32,1024]{1,0:T(8,128)S(1)}, f32[32,1024]{1,0:T(8,128)S(1)}, f32[32,1024]{1,0:T(8,128)S(1)}, f32[32,1024]{1,0:T(8,128)S(1)}, f32[32,1024]{1,...) custom-call(s32[1,1024]{1,0:T(1,128)S(1)} %bitcast.10, ...), custom_call_target="tpu_custom_call" | custom-call | flops 2952790016 | bytes 5771264 | tf_op jit(solution)/shard_map/grad_first/pallas_call | solution.py:299
  76.8 1.6 %collective-permute-start.28 = (f32[16,1024]{1,0:T(8,128)S(1)}, f32[16,1024]{1,0:T(8,128)S(1)}, u32[]{:S(2)}, u32[]{:S(2)}) collective-permute-start(f32[16,1024]{1,0:T(8,128)S(1)} %get-tuple-element.81), channel_id=1, source_target_pairs={{0,2},{2,4},{4,6},{6,7},{7,5},{5,3},{3,1},{1,0},{8,10},{10,12},{12... | collective-permute-start | bytes 196616 | tf_op jit(solution)/shard_map/ppermute | solution.py:59
  79.0 1.6 %collective-permute-start.32 = (f32[16,1024]{1,0:T(8,128)S(1)}, f32[16,1024]{1,0:T(8,128)S(1)}, u32[]{:S(2)}, u32[]{:S(2)}) collective-permute-start(f32[16,1024]{1,0:T(8,128)S(1)} %get-tuple-element.82), channel_id=1, source_target_pairs={{0,1},{2,0},{4,2},{6,4},{7,6},{5,7},{3,5},{1,3},{8,9},{10,8},{12,1... | collective-permute-start | bytes 196616 | tf_op jit(solution)/shard_map/ppermute | solution.py:59
  81.2 1.6 %collective-permute-start.29 = (f32[32,1024]{1,0:T(8,128)S(1)}, f32[32,1024]{1,0:T(8,128)S(1)}, u32[]{:S(2)}, u32[]{:S(2)}) collective-permute-start(f32[32,1024]{1,0:T(8,128)S(1)} %pad_maximum_fusion), channel_id=1, source_target_pairs={{0,2},{2,4},{4,6},{6,7},{7,5},{5,3},{3,1},{1,0},{8,10},{10,12},{12... | collective-permute-start | bytes 393224 | tf_op jit(solution)/shard_map/ppermute | solution.py:59
  82.8 2.5 %collective-permute-done.32 = f32[16,1024]{1,0:T(8,128)S(1)} collective-permute-done((f32[16,1024]{1,0:T(8,128)S(1)}, f32[16,1024]{1,0:T(8,128)S(1)}, u32[]{:S(2)}, u32[]{:S(2)}) %collective-permute-start.32) | collective-permute-done | bytes 65568 | tf_op jit(solution)/shard_map/ppermute | solution.py:59
  85.8 1.6 %collective-permute-start.41 = (f32[32,1024]{1,0:T(8,128)S(1)}, f32[32,1024]{1,0:T(8,128)S(1)}, u32[]{:S(2)}, u32[]{:S(2)}) collective-permute-start(f32[32,1024]{1,0:T(8,128)S(1)} %add.65), channel_id=1, source_target_pairs={{0,2},{2,4},{4,6},{6,7},{7,5},{5,3},{3,1},{1,0},{8,10},{10,12},{12... | collective-permute-start | bytes 393224 | tf_op jit(solution)/shard_map/ppermute | solution.py:59
  88.0 1.6 %collective-permute-start.30 = (f32[32,1024]{1,0:T(8,128)S(1)}, f32[32,1024]{1,0:T(8,128)S(1)}, u32[]{:S(2)}, u32[]{:S(2)}) collective-permute-start(f32[32,1024]{1,0:T(8,128)S(1)} %add.55), channel_id=1, source_target_pairs={{0,2},{2,4},{4,6},{6,7},{7,5},{5,3},{3,1},{1,0},{8,10},{10,12},{12... | collective-permute-start | bytes 393224 | tf_op jit(solution)/shard_map/ppermute | solution.py:59
  89.6 2.1 %collective-permute-done.33 = f32[32,1024]{1,0:T(8,128)S(1)} collective-permute-done((f32[32,1024]{1,0:T(8,128)S(1)}, f32[32,1024]{1,0:T(8,128)S(1)}, u32[]{:S(2)}, u32[]{:S(2)}) %collective-permute-start.33) | collective-permute-done | bytes 131104 | tf_op jit(solution)/shard_map/ppermute | solution.py:59
  92.3 1.6 %collective-permute-start.42 = (f32[32,1024]{1,0:T(8,128)S(1)}, f32[32,1024]{1,0:T(8,128)S(1)}, u32[]{:S(2)}, u32[]{:S(2)}) collective-permute-start(f32[32,1024]{1,0:T(8,128)S(1)} %add.66), channel_id=1, source_target_pairs={{0,2},{2,4},{4,6},{6,7},{7,5},{5,3},{3,1},{1,0},{8,10},{10,12},{12... | collective-permute-start | bytes 393224 | tf_op jit(solution)/shard_map/ppermute | solution.py:59
  95.0 2.1 %grad_stem.1 = (f32[128,256]{1,0:T(8,128)S(1)}, f32[128,256]{1,0:T(8,128)S(1)}, f32[128,256]{1,0:T(8,128)S(1)}, f32[128,256]{1,0:T(8,128)S(1)}) custom-call(bf16[512,1024]{1,0:T(8,128)(2,1)S(1)} %get-tuple-element.43.back_high, bf16[512,1024]{1,0:T(8,128)(2,1)S(1)} %get-tuple-element.44.back_low, bf16[256,1024]{1,0:T(8,128)(2,1)S(1)} %get-tuple-element.45.branch_high, ...), custom_call_target="tpu_custom_call" | custom-call | flops 805306368 | bytes 3670016 | tf_op jit(solution)/shard_map/grad_stem/pallas_call | solution.py:299
  97.3 1.0 collective-permute-start.26
  98.3 0.9 collective-permute-start.27
  99.2 1.6 %collective-permute-start.31 = (f32[32,1024]{1,0:T(8,128)S(1)}, f32[32,1024]{1,0:T(8,128)S(1)}, u32[]{:S(2)}, u32[]{:S(2)}) collective-permute-start(f32[32,1024]{1,0:T(8,128)S(1)} %add.56), channel_id=1, source_target_pairs={{0,2},{2,4},{4,6},{6,7},{7,5},{5,3},{3,1},{1,0},{8,10},{10,12},{12... | collective-permute-start | bytes 393224 | tf_op jit(solution)/shard_map/ppermute | solution.py:59
  102.0 1.6 %collective-permute-done.26.refs_2_ = f32[128,256]{1,0:T(8,128)S(1)} collective-permute-done((f32[128,256]{1,0:T(8,128)S(1)}, f32[128,256]{1,0:T(8,128)S(1)}, u32[]{:S(2)}, u32[]{:S(2)}) %collective-permute-start.26) | collective-permute-done | bytes 131104 | tf_op jit(solution)/shard_map/ppermute | solution.py:27
  103.6 1.9 %collective-permute-done.27.refs_3_ = f32[128,256]{1,0:T(8,128)S(1)} collective-permute-done((f32[128,256]{1,0:T(8,128)S(1)}, f32[128,256]{1,0:T(8,128)S(1)}, u32[]{:S(2)}, u32[]{:S(2)}) %collective-permute-start.27) | collective-permute-done | bytes 131104 | tf_op jit(solution)/shard_map/ppermute | solution.py:27
  105.5 2.4 %place.1 = f32[128,1024]{1,0:T(8,128)} custom-call(s32[1,1024]{1,0:T(1,128)S(1)} %bitcast.12, f32[128,256]{1,0:T(8,128)S(1)} %get-tuple-element.47.refs_0_, f32[128,256]{1,0:T(8,128)S(1)} %collective-permute-done.25.refs_1_, f32[128,256]{1,0:T(8,128)S(1)} %collective-permute-done.26.refs_2_, f32[128,256]{1,0:T(8,128)S(1)} %collective-permute-done.27.refs_3_), custom_call_target="tpu_custom_call" | custom-call | flops 536870912 | bytes 1052672 | tf_op jit(solution)/shard_map/place/pallas_call | solution.py:299
  (93 shorter events, 11.6 us)
Async XLA Ops:
  0.6 6.8 %collective-permute-start.17 = (f32[32,1024]{1,0:T(8,128)}, f32[32,1024]{1,0:T(8,128)S(1)}, u32[]{:S(2)}, u32[]{:S(2)}) collective-permute-start(f32[32,1024]{1,0:T(8,128)} %refs_4_.3), channel_id=1, source_target_pairs={{0,1},{2,0},{4,2},{6,4},{7,6},{5,7},{3,5},{1,3},{8,9},{10,8},{12,1... | collective-permute-start | bytes 393224 | tf_op jit(solution)/shard_map/ppermute | solution.py:59
  3.6 5.5 %collective-permute-start.21 = (f32[32,1024]{1,0:T(8,128)}, f32[32,1024]{1,0:T(8,128)S(1)}, u32[]{:S(2)}, u32[]{:S(2)}) collective-permute-start(f32[32,1024]{1,0:T(8,128)} %refs_4_.3), channel_id=1, source_target_pairs={{0,2},{2,4},{4,6},{6,7},{7,5},{5,3},{3,1},{1,0},{8,10},{10,12},{12... | collective-permute-start | bytes 393224 | tf_op jit(solution)/shard_map/ppermute | solution.py:59
  7.4 5.0 %collective-permute-start.18 = (f32[32,1024]{1,0:T(8,128)S(1)}, f32[32,1024]{1,0:T(8,128)S(1)}, u32[]{:S(2)}, u32[]{:S(2)}) collective-permute-start(f32[32,1024]{1,0:T(8,128)S(1)} %collective-permute-done.17.refs_5_), channel_id=1, source_target_pairs={{0,1},{2,0},{4,2},{6,4},{7,6},{5,7},{3,5},{1,3},{8,9},{10,8},{12,1... | collective-permute-start | bytes 393224 | tf_op jit(solution)/shard_map/ppermute | solution.py:59
  9.1 5.0 %collective-permute-start.22 = (f32[32,1024]{1,0:T(8,128)S(1)}, f32[32,1024]{1,0:T(8,128)S(1)}, u32[]{:S(2)}, u32[]{:S(2)}) collective-permute-start(f32[32,1024]{1,0:T(8,128)S(1)} %collective-permute-done.21.refs_12_), channel_id=1, source_target_pairs={{0,2},{2,4},{4,6},{6,7},{7,5},{5,3},{3,1},{1,0},{8,10},{10,12},{12... | collective-permute-start | bytes 393224 | tf_op jit(solution)/shard_map/ppermute | solution.py:59
  12.4 6.7 %collective-permute-start.19 = (f32[32,1024]{1,0:T(8,128)S(1)}, f32[32,1024]{1,0:T(8,128)S(1)}, u32[]{:S(2)}, u32[]{:S(2)}) collective-permute-start(f32[32,1024]{1,0:T(8,128)S(1)} %collective-permute-done.18.refs_6_), channel_id=1, source_target_pairs={{0,1},{2,0},{4,2},{6,4},{7,6},{5,7},{3,5},{1,3},{8,9},{10,8},{12,1... | collective-permute-start | bytes 393224 | tf_op jit(solution)/shard_map/ppermute | solution.py:59
  14.1 6.8 %collective-permute-start.23 = (f32[32,1024]{1,0:T(8,128)S(1)}, f32[32,1024]{1,0:T(8,128)S(1)}, u32[]{:S(2)}, u32[]{:S(2)}) collective-permute-start(f32[32,1024]{1,0:T(8,128)S(1)} %collective-permute-done.22.refs_11_), channel_id=1, source_target_pairs={{0,2},{2,4},{4,6},{6,7},{7,5},{5,3},{3,1},{1,0},{8,10},{10,12},{12... | collective-permute-start | bytes 393224 | tf_op jit(solution)/shard_map/ppermute | solution.py:59
  17.2 4.1 %collective-permute-start.14 = (f32[128,256]{1,0:T(8,128)S(1)}, f32[128,256]{1,0:T(8,128)S(1)}, u32[]{:S(2)}, u32[]{:S(2)}) collective-permute-start(f32[128,256]{1,0:T(8,128)S(1)} %get-tuple-element.40), channel_id=1, source_target_pairs={{0,8},{8,0},{16,24},{24,16},{1,9},{9,1},{17,25},{25,17},{2,10},{10... | collective-permute-start | bytes 393224 | tf_op jit(solution)/shard_map/ppermute | solution.py:27
  17.3 6.4 %collective-permute-start.15 = (f32[128,256]{1,0:T(8,128)S(1)}, f32[128,256]{1,0:T(8,128)S(1)}, u32[]{:S(2)}, u32[]{:S(2)}) collective-permute-start(f32[128,256]{1,0:T(8,128)S(1)} %get-tuple-element.41), channel_id=1, source_target_pairs={{0,16},{8,24},{16,0},{24,8},{1,17},{9,25},{17,1},{25,9},{2,18},{10... | collective-permute-start | bytes 393224 | tf_op jit(solution)/shard_map/ppermute | solution.py:27
  19.0 6.6 %copy-start.3 = (f32[32,1024]{1,0:T(8,128)S(1)}, f32[32,1024]{1,0:T(8,128)}, u32[]{:S(2)}) copy-start(f32[32,1024]{1,0:T(8,128)} %refs_4_.3) | copy-start | bytes 393220
  19.0 6.6 %collective-permute-start.16 = (f32[128,256]{1,0:T(8,128)S(1)}, f32[128,256]{1,0:T(8,128)S(1)}, u32[]{:S(2)}, u32[]{:S(2)}) collective-permute-start(f32[128,256]{1,0:T(8,128)S(1)} %get-tuple-element.42), channel_id=1, source_target_pairs={{0,24},{8,16},{16,8},{24,0},{1,25},{9,17},{17,9},{25,1},{2,26},{10... | collective-permute-start | bytes 393224 | tf_op jit(solution)/shard_map/ppermute | solution.py:27
  19.1 6.5 %collective-permute-start.20 = (f32[16,1024]{1,0:T(8,128)S(1)}, f32[16,1024]{1,0:T(8,128)S(1)}, u32[]{:S(2)}, u32[]{:S(2)}) collective-permute-start(f32[16,1024]{1,0:T(8,128)S(1)} %slice.66), channel_id=1, source_target_pairs={{0,1},{2,0},{4,2},{6,4},{7,6},{5,7},{3,5},{1,3},{8,9},{10,8},{12,1... | collective-permute-start | bytes 196616 | tf_op jit(solution)/shard_map/ppermute | solution.py:59
  20.9 4.7 %collective-permute-start.24 = (f32[16,1024]{1,0:T(8,128)S(1)}, f32[16,1024]{1,0:T(8,128)S(1)}, u32[]{:S(2)}, u32[]{:S(2)}) collective-permute-start(f32[16,1024]{1,0:T(8,128)S(1)} %slice.67), channel_id=1, source_target_pairs={{0,2},{2,4},{4,6},{6,7},{7,5},{5,3},{3,1},{1,0},{8,10},{10,12},{12... | collective-permute-start | bytes 196616 | tf_op jit(solution)/shard_map/ppermute | solution.py:59
  21.3 16.0 %collective-permute-start.1 = (f32[128,1024]{1,0:T(8,128)S(1)}, f32[128,1024]{1,0:T(8,128)S(1)}, u32[]{:S(2)}, u32[]{:S(2)}) collective-permute-start(f32[128,1024]{1,0:T(8,128)S(1)} %bitcast.5), channel_id=1, source_target_pairs={{0,16},{8,24},{16,0},{24,8},{1,17},{9,25},{17,1},{25,9},{2,18},{10... | collective-permute-start | bytes 1572872 | tf_op jit(solution)/shard_map/ppermute | solution.py:27
  29.4 12.9 %collective-permute-start.37 = (f32[512,256]{1,0:T(8,128)S(1)}, f32[512,256]{1,0:T(8,128)S(1)}, u32[]{:S(2)}, u32[]{:S(2)}) collective-permute-start(f32[512,256]{1,0:T(8,128)S(1)} %get-tuple-element.62), channel_id=1, source_target_pairs={{0,8},{8,0},{16,24},{24,16},{1,9},{9,1},{17,25},{25,17},{2,10},{10... | collective-permute-start | bytes 1572872 | tf_op jit(solution)/shard_map/ppermute | solution.py:27
  30.1 5.5 %collective-permute-start.7 = (f32[32,1024]{1,0:T(8,128)S(1)}, f32[32,1024]{1,0:T(8,128)S(1)}, u32[]{:S(2)}, u32[]{:S(2)}) collective-permute-start(f32[32,1024]{1,0:T(8,128)S(1)} %copy-done.1), channel_id=1, source_target_pairs={{0,2},{2,4},{4,6},{6,7},{7,5},{5,3},{3,1},{1,0},{8,10},{10,12},{12... | collective-permute-start | bytes 393224 | tf_op jit(solution)/shard_map/ppermute | solution.py:59
  31.8 6.0 %collective-permute-start.3 = (f32[32,1024]{1,0:T(8,128)S(1)}, f32[32,1024]{1,0:T(8,128)S(1)}, u32[]{:S(2)}, u32[]{:S(2)}) collective-permute-start(f32[32,1024]{1,0:T(8,128)S(1)} %copy-done.1), channel_id=1, source_target_pairs={{0,1},{2,0},{4,2},{6,4},{7,6},{5,7},{3,5},{1,3},{8,9},{10,8},{12,1... | collective-permute-start | bytes 393224 | tf_op jit(solution)/shard_map/ppermute | solution.py:59
  35.6 5.0 %collective-permute-start.8 = (f32[32,1024]{1,0:T(8,128)S(1)}, f32[32,1024]{1,0:T(8,128)S(1)}, u32[]{:S(2)}, u32[]{:S(2)}) collective-permute-start(f32[32,1024]{1,0:T(8,128)S(1)} %collective-permute-done.7.refs_12_), channel_id=1, source_target_pairs={{0,2},{2,4},{4,6},{6,7},{7,5},{5,3},{3,1},{1,0},{8,10},{10,12},{12... | collective-permute-start | bytes 393224 | tf_op jit(solution)/shard_map/ppermute | solution.py:59
  37.3 21.7 %collective-permute-start = (f32[128,1024]{1,0:T(8,128)S(1)}, f32[128,1024]{1,0:T(8,128)S(1)}, u32[]{:S(2)}, u32[]{:S(2)}) collective-permute-start(f32[128,1024]{1,0:T(8,128)S(1)} %bitcast.6), channel_id=1, source_target_pairs={{0,8},{8,0},{16,24},{24,16},{1,9},{9,1},{17,25},{25,17},{2,10},{10... | collective-permute-start | bytes 1572872 | tf_op jit(solution)/shard_map/ppermute | solution.py:27
  37.3 21.7 %collective-permute-start.2 = (f32[128,1024]{1,0:T(8,128)S(1)}, f32[128,1024]{1,0:T(8,128)S(1)}, u32[]{:S(2)}, u32[]{:S(2)}) collective-permute-start(f32[128,1024]{1,0:T(8,128)S(1)} %collective-permute-done.1.refs_2_), channel_id=1, source_target_pairs={{0,8},{8,0},{16,24},{24,16},{1,9},{9,1},{17,25},{25,17},{2,10},{10... | collective-permute-start | bytes 1572872 | tf_op jit(solution)/shard_map/ppermute | solution.py:27
  37.8 5.5 %collective-permute-start.4 = (f32[32,1024]{1,0:T(8,128)S(1)}, f32[32,1024]{1,0:T(8,128)S(1)}, u32[]{:S(2)}, u32[]{:S(2)}) collective-permute-start(f32[32,1024]{1,0:T(8,128)S(1)} %collective-permute-done.3.refs_5_), channel_id=1, source_target_pairs={{0,1},{2,0},{4,2},{6,4},{7,6},{5,7},{3,5},{1,3},{8,9},{10,8},{12,1... | collective-permute-start | bytes 393224 | tf_op jit(solution)/shard_map/ppermute | solution.py:59
  40.5 5.0 %collective-permute-start.9 = (f32[32,1024]{1,0:T(8,128)S(1)}, f32[32,1024]{1,0:T(8,128)S(1)}, u32[]{:S(2)}, u32[]{:S(2)}) collective-permute-start(f32[32,1024]{1,0:T(8,128)S(1)} %collective-permute-done.8.refs_11_), channel_id=1, source_target_pairs={{0,2},{2,4},{4,6},{6,7},{7,5},{5,3},{3,1},{1,0},{8,10},{10,12},{12... | collective-permute-start | bytes 393224 | tf_op jit(solution)/shard_map/ppermute | solution.py:59
  42.3 20.9 %collective-permute-start.36 = (f32[512,256]{1,0:T(8,128)S(1)}, f32[512,256]{1,0:T(8,128)S(1)}, u32[]{:S(2)}, u32[]{:S(2)}) collective-permute-start(f32[512,256]{1,0:T(8,128)S(1)} %get-tuple-element.60), channel_id=1, source_target_pairs={{0,8},{8,0},{16,24},{24,16},{1,9},{9,1},{17,25},{25,17},{2,10},{10... | collective-permute-start | bytes 1572872 | tf_op jit(solution)/shard_map/ppermute | solution.py:27
  43.3 19.9 %collective-permute-start.38 = (f32[512,256]{1,0:T(8,128)S(1)}, f32[512,256]{1,0:T(8,128)S(1)}, u32[]{:S(2)}, u32[]{:S(2)}) collective-permute-start(f32[512,256]{1,0:T(8,128)S(1)} %add.63), channel_id=1, source_target_pairs={{0,16},{8,24},{16,0},{24,8},{1,17},{9,25},{17,1},{25,9},{2,18},{10... | collective-permute-start | bytes 1572872 | tf_op jit(solution)/shard_map/ppermute | solution.py:27
  45.5 5.0 %collective-permute-start.5 = (f32[32,1024]{1,0:T(8,128)S(1)}, f32[32,1024]{1,0:T(8,128)S(1)}, u32[]{:S(2)}, u32[]{:S(2)}) collective-permute-start(f32[32,1024]{1,0:T(8,128)S(1)} %collective-permute-done.4.refs_6_), channel_id=1, source_target_pairs={{0,1},{2,0},{4,2},{6,4},{7,6},{5,7},{3,5},{1,3},{8,9},{10,8},{12,1... | collective-permute-start | bytes 393224 | tf_op jit(solution)/shard_map/ppermute | solution.py:59
  50.5 4.3 %collective-permute-start.10 = (f32[16,1024]{1,0:T(8,128)S(1)}, f32[16,1024]{1,0:T(8,128)S(1)}, u32[]{:S(2)}, u32[]{:S(2)}) collective-permute-start(f32[16,1024]{1,0:T(8,128)S(1)} %slice.65), channel_id=1, source_target_pairs={{0,2},{2,4},{4,6},{6,7},{7,5},{5,3},{3,1},{1,0},{8,10},{10,12},{12... | collective-permute-start | bytes 196616 | tf_op jit(solution)/shard_map/ppermute | solution.py:59
  54.8 4.3 %collective-permute-start.6 = (f32[16,1024]{1,0:T(8,128)S(1)}, f32[16,1024]{1,0:T(8,128)S(1)}, u32[]{:S(2)}, u32[]{:S(2)}) collective-permute-start(f32[16,1024]{1,0:T(8,128)S(1)} %slice.64), channel_id=1, source_target_pairs={{0,1},{2,0},{4,2},{6,4},{7,6},{5,7},{3,5},{1,3},{8,9},{10,8},{12,1... | collective-permute-start | bytes 196616 | tf_op jit(solution)/shard_map/ppermute | solution.py:59
  61.4 10.0 %collective-permute-start.12 = (f32[512,256]{1,0:T(8,128)S(1)}, f32[512,256]{1,0:T(8,128)S(1)}, u32[]{:S(2)}, u32[]{:S(2)}) collective-permute-start(f32[512,256]{1,0:T(8,128)S(1)} %get-tuple-element.38.refs_0_), channel_id=1, source_target_pairs={{0,16},{8,24},{16,0},{24,8},{1,17},{9,25},{17,1},{25,9},{2,18},{10... | collective-permute-start | bytes 1572872 | tf_op jit(solution)/shard_map/ppermute | solution.py:27
  64.4 7.1 %collective-permute-start.39 = (f32[16,1024]{1,0:T(8,128)S(1)}, f32[16,1024]{1,0:T(8,128)S(1)}, u32[]{:S(2)}, u32[]{:S(2)}) collective-permute-start(f32[16,1024]{1,0:T(8,128)S(1)} %get-tuple-element.75), channel_id=1, source_target_pairs={{0,2},{2,4},{4,6},{6,7},{7,5},{5,3},{3,1},{1,0},{8,10},{10,12},{12... | collective-permute-start | bytes 196616 | tf_op jit(solution)/shard_map/ppermute | solution.py:59
  66.0 7.3 %collective-permute-start.11 = (f32[512,256]{1,0:T(8,128)S(1)}, f32[512,256]{1,0:T(8,128)S(1)}, u32[]{:S(2)}, u32[]{:S(2)}) collective-permute-start(f32[512,256]{1,0:T(8,128)S(1)} %get-tuple-element.38.refs_0_), channel_id=1, source_target_pairs={{0,8},{8,0},{16,24},{24,16},{1,9},{9,1},{17,25},{25,17},{2,10},{10... | collective-permute-start | bytes 1572872 | tf_op jit(solution)/shard_map/ppermute | solution.py:27
  66.0 7.3 %collective-permute-start.43 = (f32[16,1024]{1,0:T(8,128)S(1)}, f32[16,1024]{1,0:T(8,128)S(1)}, u32[]{:S(2)}, u32[]{:S(2)}) collective-permute-start(f32[16,1024]{1,0:T(8,128)S(1)} %get-tuple-element.76), channel_id=1, source_target_pairs={{0,1},{2,0},{4,2},{6,4},{7,6},{5,7},{3,5},{1,3},{8,9},{10,8},{12,1... | collective-permute-start | bytes 196616 | tf_op jit(solution)/shard_map/ppermute | solution.py:59
  71.4 1.9 %collective-permute-start.13 = (f32[512,256]{1,0:T(8,128)S(1)}, f32[512,256]{1,0:T(8,128)S(1)}, u32[]{:S(2)}, u32[]{:S(2)}) collective-permute-start(f32[512,256]{1,0:T(8,128)S(1)} %collective-permute-done.12.refs_2_), channel_id=1, source_target_pairs={{0,8},{8,0},{16,24},{24,16},{1,9},{9,1},{17,25},{25,17},{2,10},{10... | collective-permute-start | bytes 1572872 | tf_op jit(solution)/shard_map/ppermute | solution.py:27
  71.5 14.3 %collective-permute-start.40 = (f32[32,1024]{1,0:T(8,128)S(1)}, f32[32,1024]{1,0:T(8,128)S(1)}, u32[]{:S(2)}, u32[]{:S(2)}) collective-permute-start(f32[32,1024]{1,0:T(8,128)S(1)} %pad_maximum_fusion.2), channel_id=1, source_target_pairs={{0,2},{2,4},{4,6},{6,7},{7,5},{5,3},{3,1},{1,0},{8,10},{10,12},{12... | collective-permute-start | bytes 393224 | tf_op jit(solution)/shard_map/ppermute | solution.py:59
  76.8 4.3 %collective-permute-start.28 = (f32[16,1024]{1,0:T(8,128)S(1)}, f32[16,1024]{1,0:T(8,128)S(1)}, u32[]{:S(2)}, u32[]{:S(2)}) collective-permute-start(f32[16,1024]{1,0:T(8,128)S(1)} %get-tuple-element.81), channel_id=1, source_target_pairs={{0,2},{2,4},{4,6},{6,7},{7,5},{5,3},{3,1},{1,0},{8,10},{10,12},{12... | collective-permute-start | bytes 196616 | tf_op jit(solution)/shard_map/ppermute | solution.py:59
  78.5 9.0 %collective-permute-start.44 = (f32[32,1024]{1,0:T(8,128)S(1)}, f32[32,1024]{1,0:T(8,128)S(1)}, u32[]{:S(2)}, u32[]{:S(2)}) collective-permute-start(f32[32,1024]{1,0:T(8,128)S(1)} %pad_maximum_fusion.3), channel_id=1, source_target_pairs={{0,1},{2,0},{4,2},{6,4},{7,6},{5,7},{3,5},{1,3},{8,9},{10,8},{12,1... | collective-permute-start | bytes 393224 | tf_op jit(solution)/shard_map/ppermute | solution.py:59
  79.0 6.3 %collective-permute-start.32 = (f32[16,1024]{1,0:T(8,128)S(1)}, f32[16,1024]{1,0:T(8,128)S(1)}, u32[]{:S(2)}, u32[]{:S(2)}) collective-permute-start(f32[16,1024]{1,0:T(8,128)S(1)} %get-tuple-element.82), channel_id=1, source_target_pairs={{0,1},{2,0},{4,2},{6,4},{7,6},{5,7},{3,5},{1,3},{8,9},{10,8},{12,1... | collective-permute-start | bytes 196616 | tf_op jit(solution)/shard_map/ppermute | solution.py:59
  81.2 6.8 %collective-permute-start.29 = (f32[32,1024]{1,0:T(8,128)S(1)}, f32[32,1024]{1,0:T(8,128)S(1)}, u32[]{:S(2)}, u32[]{:S(2)}) collective-permute-start(f32[32,1024]{1,0:T(8,128)S(1)} %pad_maximum_fusion), channel_id=1, source_target_pairs={{0,2},{2,4},{4,6},{6,7},{7,5},{5,3},{3,1},{1,0},{8,10},{10,12},{12... | collective-permute-start | bytes 393224 | tf_op jit(solution)/shard_map/ppermute | solution.py:59
  85.3 6.4 %collective-permute-start.33 = (f32[32,1024]{1,0:T(8,128)S(1)}, f32[32,1024]{1,0:T(8,128)S(1)}, u32[]{:S(2)}, u32[]{:S(2)}) collective-permute-start(f32[32,1024]{1,0:T(8,128)S(1)} %pad_maximum_fusion.1), channel_id=1, source_target_pairs={{0,1},{2,0},{4,2},{6,4},{7,6},{5,7},{3,5},{1,3},{8,9},{10,8},{12,1... | collective-permute-start | bytes 393224 | tf_op jit(solution)/shard_map/ppermute | solution.py:59
  85.8 6.4 %collective-permute-start.41 = (f32[32,1024]{1,0:T(8,128)S(1)}, f32[32,1024]{1,0:T(8,128)S(1)}, u32[]{:S(2)}, u32[]{:S(2)}) collective-permute-start(f32[32,1024]{1,0:T(8,128)S(1)} %add.65), channel_id=1, source_target_pairs={{0,2},{2,4},{4,6},{6,7},{7,5},{5,3},{3,1},{1,0},{8,10},{10,12},{12... | collective-permute-start | bytes 393224 | tf_op jit(solution)/shard_map/ppermute | solution.py:59
  87.5 7.1 %collective-permute-start.45 = (f32[32,1024]{1,0:T(8,128)S(1)}, f32[32,1024]{1,0:T(8,128)S(1)}, u32[]{:S(2)}, u32[]{:S(2)}) collective-permute-start(f32[32,1024]{1,0:T(8,128)S(1)} %add.69), channel_id=1, source_target_pairs={{0,1},{2,0},{4,2},{6,4},{7,6},{5,7},{3,5},{1,3},{8,9},{10,8},{12,1... | collective-permute-start | bytes 393224 | tf_op jit(solution)/shard_map/ppermute | solution.py:59
  88.0 9.3 %collective-permute-start.30 = (f32[32,1024]{1,0:T(8,128)S(1)}, f32[32,1024]{1,0:T(8,128)S(1)}, u32[]{:S(2)}, u32[]{:S(2)}) collective-permute-start(f32[32,1024]{1,0:T(8,128)S(1)} %add.55), channel_id=1, source_target_pairs={{0,2},{2,4},{4,6},{6,7},{7,5},{5,3},{3,1},{1,0},{8,10},{10,12},{12... | collective-permute-start | bytes 393224 | tf_op jit(solution)/shard_map/ppermute | solution.py:59
  91.7 6.5 %collective-permute-start.34 = (f32[32,1024]{1,0:T(8,128)S(1)}, f32[32,1024]{1,0:T(8,128)S(1)}, u32[]{:S(2)}, u32[]{:S(2)}) collective-permute-start(f32[32,1024]{1,0:T(8,128)S(1)} %add.59), channel_id=1, source_target_pairs={{0,1},{2,0},{4,2},{6,4},{7,6},{5,7},{3,5},{1,3},{8,9},{10,8},{12,1... | collective-permute-start | bytes 393224 | tf_op jit(solution)/shard_map/ppermute | solution.py:59
  92.3 7.0 %collective-permute-start.42 = (f32[32,1024]{1,0:T(8,128)S(1)}, f32[32,1024]{1,0:T(8,128)S(1)}, u32[]{:S(2)}, u32[]{:S(2)}) collective-permute-start(f32[32,1024]{1,0:T(8,128)S(1)} %add.66), channel_id=1, source_target_pairs={{0,2},{2,4},{4,6},{6,7},{7,5},{5,3},{3,1},{1,0},{8,10},{10,12},{12... | collective-permute-start | bytes 393224 | tf_op jit(solution)/shard_map/ppermute | solution.py:59
  94.5 6.3 %collective-permute-start.46 = (f32[32,1024]{1,0:T(8,128)S(1)}, f32[32,1024]{1,0:T(8,128)S(1)}, u32[]{:S(2)}, u32[]{:S(2)}) collective-permute-start(f32[32,1024]{1,0:T(8,128)S(1)} %add.70), channel_id=1, source_target_pairs={{0,1},{2,0},{4,2},{6,4},{7,6},{5,7},{3,5},{1,3},{8,9},{10,8},{12,1... | collective-permute-start | bytes 393224 | tf_op jit(solution)/shard_map/ppermute | solution.py:59
  97.2 4.8 %collective-permute-start.25 = (f32[128,256]{1,0:T(8,128)S(1)}, f32[128,256]{1,0:T(8,128)S(1)}, u32[]{:S(2)}, u32[]{:S(2)}) collective-permute-start(f32[128,256]{1,0:T(8,128)S(1)} %get-tuple-element.48), channel_id=1, source_target_pairs={{0,8},{8,0},{16,24},{24,16},{1,9},{9,1},{17,25},{25,17},{2,10},{10... | collective-permute-start | bytes 393224 | tf_op jit(solution)/shard_map/ppermute | solution.py:27
  97.3 6.4 %collective-permute-start.26 = (f32[128,256]{1,0:T(8,128)S(1)}, f32[128,256]{1,0:T(8,128)S(1)}, u32[]{:S(2)}, u32[]{:S(2)}) collective-permute-start(f32[128,256]{1,0:T(8,128)S(1)} %get-tuple-element.49), channel_id=1, source_target_pairs={{0,16},{8,24},{16,0},{24,8},{1,17},{9,25},{17,1},{25,9},{2,18},{10... | collective-permute-start | bytes 393224 | tf_op jit(solution)/shard_map/ppermute | solution.py:27
  98.3 7.2 %collective-permute-start.27 = (f32[128,256]{1,0:T(8,128)S(1)}, f32[128,256]{1,0:T(8,128)S(1)}, u32[]{:S(2)}, u32[]{:S(2)}) collective-permute-start(f32[128,256]{1,0:T(8,128)S(1)} %get-tuple-element.50), channel_id=1, source_target_pairs={{0,24},{8,16},{16,8},{24,0},{1,25},{9,17},{17,9},{25,1},{2,26},{10... | collective-permute-start | bytes 393224 | tf_op jit(solution)/shard_map/ppermute | solution.py:27
  99.2 8.6 %collective-permute-start.31 = (f32[32,1024]{1,0:T(8,128)S(1)}, f32[32,1024]{1,0:T(8,128)S(1)}, u32[]{:S(2)}, u32[]{:S(2)}) collective-permute-start(f32[32,1024]{1,0:T(8,128)S(1)} %add.56), channel_id=1, source_target_pairs={{0,2},{2,4},{4,6},{6,7},{7,5},{5,3},{3,1},{1,0},{8,10},{10,12},{12... | collective-permute-start | bytes 393224 | tf_op jit(solution)/shard_map/ppermute | solution.py:59
  100.9 7.0 %collective-permute-start.35 = (f32[32,1024]{1,0:T(8,128)S(1)}, f32[32,1024]{1,0:T(8,128)S(1)}, u32[]{:S(2)}, u32[]{:S(2)}) collective-permute-start(f32[32,1024]{1,0:T(8,128)S(1)} %add.60), channel_id=1, source_target_pairs={{0,1},{2,0},{4,2},{6,4},{7,6},{5,7},{3,5},{1,3},{8,9},{10,8},{12,1... | collective-permute-start | bytes 393224 | tf_op jit(solution)/shard_map/ppermute | solution.py:59
  (6 other events, 20.3 us)

commit v3 on v1

--- a/solution.py
+++ b/solution.py
@@ -1,6 +1,10 @@
+import functools
+
 import jax
 import jax.numpy as jnp
 from jax import lax
+from jax.experimental import pallas as pl
+from jax.experimental.pallas import tpu as pltpu
 from jax.sharding import PartitionSpec as P
 
 
@@ -45,6 +49,16 @@
     return [block if rel == 0 else swap(block, rel) for rel, block in enumerate(blocks)]
 
 
+def pair_exchange(near, away):
+    away = swap(away, 2)
+    return near, swap(near, 1), away, swap(away, 1)
+
+
+def pair_blocks(refs):
+    half = refs[0].shape[0] // 2
+    return [ref[half:] if rel % 2 else ref[:half] for rel, ref in enumerate(refs)]
+
+
 def ring_order(size):
     return [i for i in range(size) if i % 2 == 0] + [i for i in reversed(range(size)) if i % 2]
 
@@ -55,34 +69,63 @@
     return lax.ppermute(block, "gy", [(order[k], order[(k + step) % size]) for k in range(size)])
 
 
+def ordered(value, *others):
+    return lax.optimization_barrier((value, *others))[0]
+
+
+class Ring:
+    def __init__(self, block):
+        self.size = lax.axis_size("gy")
+        self.ahead = self.behind = block
+        self.taken = 0
+        self.last = []
+        self.pieces = [block] + [None] * (self.size - 1)
+
+    def after(self, *others):
+        self.ahead, self.behind, *others = lax.optimization_barrier((self.ahead, self.behind, *others))
+        return others
+
+    def step(self):
+        self.taken += 1
+        if self.taken < self.size // 2:
+            self.ahead, self.behind = ring_step(self.ahead, -1), ring_step(self.behind, 1)
+            self.pieces[self.taken], self.pieces[self.size - self.taken] = self.ahead, self.behind
+            self.last.append((self.ahead, self.behind))
+            return
+        half = self.ahead.shape[0] // 2
+        halves = [ring_step(self.ahead[:half], -1), ring_step(self.behind[half:], 1)]
+        self.pieces[self.taken : self.taken + 1] = halves
+
+
+def gy_pieces(block):
+    ring = Ring(block)
+    for _ in range(ring.size // 2):
+        ring.step()
+    return ring.pieces
+
+
 def gy_gather(block):
+    return jnp.concatenate(gy_pieces(block), axis=0)
+
+
+def gy_reduce(blocks, waits=()):
     size = lax.axis_size("gy")
-    half = block.shape[0] // 2
-    pieces = [None] * size
-    pieces[0] = block
-    ahead = behind = block
-    for step in range(1, size // 2):
-        ahead, behind = ring_step(ahead, -1), ring_step(behind, 1)
-        pieces[step], pieces[size - step] = ahead, behind
-    pieces[size // 2] = jnp.concatenate([ring_step(ahead[:half], -1), ring_step(behind[half:], 1)], axis=0)
-    return jnp.concatenate(pieces, axis=0)
-
-
-def gy_reduce(blocks):
-    size = lax.axis_size("gy")
+    waits = dict(waits)
     half = blocks[0].shape[0] // 2
     far = blocks[size // 2]
     ahead, behind = ring_step(far[:half], 1), ring_step(far[half:], -1)
     near, back = blocks[size // 2 - 1], blocks[size // 2 + 1]
     ahead = jnp.concatenate([near[:half] + ahead, near[half:]], axis=0)
     behind = jnp.concatenate([back[:half], back[half:] + behind], axis=0)
-    for step in range(size // 2 - 2, 0, -1):
-        ahead = blocks[step] + ring_step(ahead, 1)
-        behind = blocks[size - step] + ring_step(behind, -1)
-    return blocks[0] + ring_step(ahead, 1) + ring_step(behind, -1)
-
-
-def on_device(stem_first, cotangent, branch_first, branch_second, bond_first, bond_second):
+    for step in range(size // 2 - 2, -1, -1):
+        ahead, behind = lax.optimization_barrier((ahead, behind, *waits.get(size // 2 - 1 - step, ())))[:2]
+        ahead, behind = ring_step(ahead, 1), ring_step(behind, -1)
+        if step:
+            ahead, behind = blocks[step] + ahead, blocks[size - step] + behind
+    return blocks[0] + ahead + behind
+
+
+def plain(stem_first, cotangent, branch_first, branch_second, bond_first, bond_second):
     groups, splits = lax.axis_size("gx"), lax.axis_size("gy")
     me_x, me_y = lax.axis_index("gx"), lax.axis_index("gy")
     height, width = stem_first.shape[1:]
@@ -135,6 +178,352 @@
     grad = gx_exchange([grad[rel * height : (rel + 1) * height] for rel in range(groups)])
     grad_stem = jnp.take(jnp.concatenate(grad, axis=1), back_first, axis=1).reshape(1, height, width)
     return (grad_stem, grad_first * factor, grad_second * factor)
+
+
+def split(value):
+    high = value.astype(jnp.bfloat16)
+    return high, (value - high.astype(jnp.float32)).astype(jnp.bfloat16)
+
+
+def dot(left, right, contract):
+    return lax.dot_general(left, right, (contract, ((), ())), preferred_element_type=jnp.float32)
+
+
+def dot_parts(left, right, contract):
+    return dot(left[0], right[0], contract) + dot(left[0], right[1], contract) + dot(left[1], right[0], contract)
+
+
+def ring_owner(offset):
+    size = lax.axis_size("gy")
+    me = lax.axis_index("gy")
+    place = jnp.where(me % 2 == 0, me // 2, size - 1 - me // 2)
+    place = (place + offset) % size
+    return jnp.where(place < size // 2, 2 * place, 2 * (size - 1 - place) + 1)
+
+
+def group(rel):
+    return lax.axis_index("gx") ^ rel
+
+
+def early_offsets(size):
+    near = [k for k in range(size) if min(k, size - k) <= size // 4]
+    return near, [k for k in range(size) if k not in near]
+
+
+def aligned(index, size):
+    return pl.ds(pl.multiple_of(index * size, size), size)
+
+
+def store_split(high_ref, low_ref, where, value):
+    high_ref[where], low_ref[where] = split(value)
+
+
+def branch_rows(ref, own, part):
+    return ref[...] if ref.shape[0] == own else ref[part * own : (part + 1) * own]
+
+
+def chosen(bond_ref, rel, low, width):
+    columns = bond_ref[:, aligned(group(rel), low)]
+    position = lax.broadcasted_iota(jnp.int32, (width, low), 0)
+    return (position == columns).astype(jnp.bfloat16)
+
+
+def put_pairs(blocks, pair_refs):
+    size = pair_refs[0].shape[0] // 2
+    for rel, block in enumerate(blocks):
+        pair_refs[rel // 2][rel % 2 * size : (rel % 2 + 1) * size] = block
+
+
+def pack_kernel(first_ref, second_ref, pair_ref, done):
+    own = first_ref.shape[0]
+    copies = [
+        pltpu.make_async_copy(ref, pair_ref.at[pl.ds(part * own, own)], done.at[part])
+        for part, ref in enumerate((first_ref, second_ref))
+    ]
+    for copy in copies:
+        copy.start()
+    for copy in copies:
+        copy.wait()
+
+
+def pick_kernel(groups, stem_ref, bond_ref, *out_refs):
+    high, low_part = split(stem_ref[...])
+    width = stem_ref.shape[1]
+    selects = [chosen(bond_ref, rel, width // groups, width) for rel in range(groups)]
+    put_pairs([dot(high, one, ((1,), (0,))) + dot(low_part, one, ((1,), (0,))) for one in selects], out_refs)
+
+
+def absorb(picked, branch, mid, groups):
+    height, low = picked[0].shape[0] // 2, picked[0].shape[1]
+    for rel, block in enumerate(pair_blocks(picked)):
+        parts = split(block)
+        columns = aligned(group(rel), low)
+        for h in range(groups):
+            cut = slice(h * low, (h + 1) * low)
+            value = dot_parts(parts, (branch[0][:, cut], branch[1][:, cut]), ((1,), (0,)))
+            store_split(*mid, (slice(h * height, (h + 1) * height), columns), value)
+
+
+def put_picks(bond_ref, mid, out_refs):
+    width = mid[0].shape[1]
+    rows, low = mid[0].shape[0], out_refs[0].shape[1]
+    for rel in range(width // low):
+        select = chosen(bond_ref, rel, low, width)
+        block = dot(mid[0][...], select, ((1,), (0,))) + dot(mid[1][...], select, ((1,), (0,)))
+        out_refs[rel % 2][rel // 2 * rows : (rel // 2 + 1) * rows] = block
+
+
+def mid_kernel(groups, bond_ref, *refs):
+    picked, refs = refs[:groups], refs[groups:]
+    out_refs, branch, mid = refs[-6:-4], refs[-4:-2], refs[-2:]
+    own = branch[0].shape[0] // lax.axis_size("gy")
+    for k, ref in enumerate(refs[:-6]):
+        store_split(*branch, aligned(ring_owner(k), own), branch_rows(ref, own, 0))
+    absorb(picked, branch, mid, groups)
+    put_picks(bond_ref, mid, out_refs)
+
+
+def gather_rows(pieces, rows, own):
+    for k, ref in enumerate(pieces):
+        store_split(*rows, slice(k * own, (k + 1) * own), branch_rows(ref, own, 1))
+
+
+def early_back_kernel(groups, own, *refs):
+    cotan, refs = refs[:groups], refs[groups:]
+    pieces, (out_ref, cotan_high, cotan_low, *rows) = refs[:-5], refs[-5:]
+    height = cotan[0].shape[0]
+    gather_rows(pieces, rows, own)
+    for rel, ref in enumerate(cotan):
+        store_split(cotan_high, cotan_low, aligned(group(rel), height), ref[...])
+    out_ref[...] = dot_parts((rows[0][...], rows[1][...]), (cotan_high[...], cotan_low[...]), ((1,), (1,)))
+
+
+def late_back_kernel(own, cotan_high, cotan_low, *refs):
+    pieces, (out_ref, *rows) = refs[:-3], refs[-3:]
+    gather_rows(pieces, rows, own)
+    out_ref[...] = dot_parts((rows[0][...], rows[1][...]), (cotan_high[...], cotan_low[...]), ((1,), (1,)))
+
+
+def put_blocks(total, out_refs, total_ref):
+    own = out_refs[0].shape[0]
+    total_ref[...] = total
+    for k, out_ref in enumerate(out_refs):
+        out_ref[...] = total_ref[aligned(ring_owner(k), own)]
+
+
+def second_kernel(factor, near_ref, far_ref, cotan_high, cotan_low, *refs):
+    firsts, refs = refs[: (len(refs) - 1) // 2], refs[(len(refs) - 1) // 2 :]
+    out_refs, total_ref = refs[:-1], refs[-1]
+    own = firsts[0].shape[0]
+    parts = split(((near_ref[...] + far_ref[...]) * factor).T)
+    total_ref[...] = dot_parts(parts, (cotan_high[...], cotan_low[...]), ((1,), (0,)))
+    for k, (ref, out_ref) in enumerate(zip(firsts, out_refs, strict=True)):
+        out_ref[:own] = ref[...]
+        out_ref[own:] = total_ref[aligned(ring_owner(k), own)]
+
+
+def first_kernel(groups, factor, bond_ref, *refs):
+    near, far, picked, refs = refs[:groups], refs[groups : 2 * groups], refs[2 * groups : 3 * groups], refs[3 * groups :]
+    out_refs, (turned_high, turned_low, rows_high, rows_low, picked_high, picked_low, total_ref) = refs[:-7], refs[-7:]
+    height, low = picked[0].shape[0] // 2, picked[0].shape[1]
+    width = groups * low
+    size = lax.axis_size("gy")
+    own = low // size
+    for pieces, offsets in zip((near, far), early_offsets(size)):
+        for rel, ref in enumerate(pieces):
+            for number, k in enumerate(offsets):
+                where = aligned(group(rel) * size + ring_owner(k), own)
+                store_split(rows_high, rows_low, where, ref[number * own : (number + 1) * own])
+    position = lax.broadcasted_iota(jnp.int32, (width, width), 0)
+    select = (position == bond_ref[...]).astype(jnp.bfloat16)
+    total = dot(select, rows_high[...], ((1,), (0,))) + dot(select, rows_low[...], ((1,), (0,)))
+    for h in range(groups):
+        for a in range(groups):
+            value = total[a * low : (a + 1) * low, h * height : (h + 1) * height]
+            where = (slice(h * low, (h + 1) * low), slice(a * height, (a + 1) * height))
+            store_split(turned_high, turned_low, where, value)
+    for rel, block in enumerate(pair_blocks(picked)):
+        store_split(picked_high, picked_low, (slice(None), aligned(group(rel), height)), (block * factor).T)
+    parts = picked_high[...], picked_low[...]
+    put_blocks(dot_parts(parts, (turned_high[...], turned_low[...]), ((1,), (1,))), out_refs, total_ref)
+
+
+def stem_kernel(groups, branch_high, branch_low, turned_high, turned_low, *refs):
+    out_refs, total_ref = refs[:-1], refs[-1]
+    height = total_ref.shape[1] // groups
+    branch, turned = (branch_high[...], branch_low[...]), (turned_high[...], turned_low[...])
+    total_ref[...] = dot_parts(branch, turned, ((1,), (0,)))
+    put_pairs([total_ref[:, aligned(group(rel), height)] for rel in range(groups)], out_refs)
+
+
+def place_kernel(bond_ref, *refs):
+    blocks, out_ref = refs[:-1], refs[-1]
+    total = None
+    for rel, block in enumerate(pair_blocks(blocks)):
+        select = chosen(bond_ref, rel, block.shape[0], out_ref.shape[1])
+        high, low_part = split(block.T)
+        term = dot(high, select, ((1,), (1,))) + dot(low_part, select, ((1,), (1,)))
+        total = term if total is None else total + term
+    out_ref[...] = total
+
+
+def call(kernel, name, outs, flops, scratch, *operands):
+    moved = sum(x.size * x.dtype.itemsize for x in (*operands, *outs))
+    whole = pl.BlockSpec(memory_space=pltpu.VMEM)
+    return pl.pallas_call(
+        kernel,
+        name=name,
+        out_shape=outs,
+        in_specs=[whole] * len(operands),
+        out_specs=[whole] * len(outs),
+        scratch_shapes=scratch,
+        compiler_params=pltpu.CompilerParams(vmem_limit_bytes=32 * 1024 * 1024),
+        cost_estimate=pl.CostEstimate(flops=flops, bytes_accessed=moved, transcendentals=0),
+    )(*operands)
+
+
+def f32(*shape):
+    return jax.ShapeDtypeStruct(shape, jnp.float32)
+
+
+def b16(*shape):
+    return jax.ShapeDtypeStruct(shape, jnp.bfloat16)
+
+
+def on_device(stem_first, cotangent, branch_first, branch_second, bond_first, bond_second):
+    groups, splits = lax.axis_size("gx"), lax.axis_size("gy")
+    height, width = stem_first.shape[1:]
+    low = width // groups
+    own = width // (groups * splits)
+    if groups != 4 or splits % 2 or splits < 8 or low % 128 or own % 32 or height % 128:
+        return plain(stem_first, cotangent, branch_first, branch_second, bond_first, bond_second)
+    factor = (height * groups * splits) ** -0.5
+    tall = groups * height
+    unit = 2 * height * width * width
+    first_bond, second_bond = bond_first.reshape(1, width), bond_second.reshape(1, width)
+    stem_rows, cotan_rows = stem_first.reshape(height, width), cotangent.reshape(height, width)
+    blocks = [f32(own, width)] * splits
+
+    early, late = early_offsets(splits)
+
+    def wide(*shape):
+        return [pltpu.VMEM(shape, jnp.bfloat16)] * 2
+
+    inside, anywhere = pl.BlockSpec(memory_space=pltpu.VMEM), pl.BlockSpec(memory_space=pl.ANY)
+    pair = pl.pallas_call(
+        pack_kernel,
+        name="pack",
+        out_shape=f32(2 * own, width),
+        in_specs=[anywhere] * 2,
+        out_specs=inside,
+        scratch_shapes=[pltpu.SemaphoreType.DMA((2,))],
+        compiler_params=pltpu.CompilerParams(vmem_limit_bytes=60 * 1024 * 1024),
+    )(branch_first, branch_second)
+    ring = Ring(pair)
+    ring.step()
+    cotan_far = swap(cotan_rows, 2)
+    near, away = call(
+        functools.partial(pick_kernel, groups),
+        "pick",
+        [f32(2 * height, low)] * 2,
+        2 * unit,
+        [],
+        stem_rows,
+        ordered(first_bond, pair),
+    )
+    near, away = ring.after(near, away)
+    ring.step()
+    pieces = dict(enumerate(ring.pieces))
+    cotan_far, near, away = ring.after(cotan_far, near, away)
+    ring.step()
+    away = swap(away, 2)
+    near_back, cotan_high, cotan_low = call(
+        functools.partial(early_back_kernel, groups, own),
+        "early_back",
+        [f32(len(early) * own, tall)] + [b16(tall, width)] * 2,
+        3 * unit * len(early) // splits,
+        wide(len(early) * own, width),
+        cotan_rows,
+        swap(cotan_rows, 1),
+        cotan_far,
+        swap(cotan_far, 1),
+        *[pieces[k] for k in early],
+    )
+    near_far = swap(near_back, 2)
+    near, away, _ = ring.after(near, away, near_back)
+    for _ in range(ring.size // 2 - 3):
+        ring.step()
+    picked = near, swap(near, 1), away, swap(away, 1)
+    cotan_high, near_far, *picked = lax.optimization_barrier((cotan_high, near_far, *picked))
+    far = splits // 2
+    pieces_first = ring.pieces[: far + 1] + ring.pieces[far + 2 :]
+    pieces_second = ring.pieces[:far] + ring.pieces[far + 1 :]
+    far_back = call(
+        functools.partial(late_back_kernel, own),
+        "late_back",
+        [f32(len(late) * own, tall)],
+        3 * unit * len(late) // splits,
+        wide(len(late) * own, width),
+        cotan_high,
+        cotan_low,
+        *[pieces_second[k] for k in late],
+    )[0]
+    far_far = swap(far_back, 2)
+    *mid, first_high, first_low = call(
+        functools.partial(mid_kernel, groups),
+        "mid",
+        [f32(2 * tall, low)] * 2 + [b16(low, width)] * 2,
+        3 * unit + 2 * groups * unit,
+        wide(tall, width),
+        ordered(second_bond, far_back),
+        *picked,
+        *pieces_first,
+    )
+    mid[1], far_far = lax.optimization_barrier((mid[1], far_far))
+    mid = mid[0] + swap(mid[1], 1)
+    near_mid, away_mid, far_far, near_far = lax.optimization_barrier((mid[:tall], mid[tall:], far_far, near_far))
+    regrouped = [near_mid, swap(away_mid, 2)]
+    gathered = [
+        [near_back, swap(near_back, 1), near_far, swap(near_far, 1)],
+        [far_back, swap(far_back, 1), far_far, swap(far_far, 1)],
+    ]
+    *outer_first, turned_high, turned_low = call(
+        functools.partial(first_kernel, groups, factor),
+        "grad_first",
+        blocks + [b16(width, tall)] * 2,
+        3 * unit + 2 * groups * unit,
+        wide(width, tall) + wide(low, tall) + [pltpu.VMEM((low, width), jnp.float32)],
+        second_bond,
+        *gathered[0],
+        *gathered[1],
+        *picked,
+    )
+    outer = call(
+        functools.partial(second_kernel, factor),
+        "grad_second",
+        [f32(2 * own, width)] * splits,
+        3 * unit,
+        [pltpu.VMEM((low, width), jnp.float32)],
+        *regrouped,
+        cotan_high,
+        cotan_low,
+        *outer_first,
+    )
+    grad = call(
+        functools.partial(stem_kernel, groups),
+        "grad_stem",
+        [f32(2 * low, height)] * 2,
+        3 * unit,
+        [pltpu.VMEM((low, tall), jnp.float32)],
+        ordered(first_high, outer[0]),
+        first_low,
+        turned_high,
+        turned_low,
+    )
+    moved = pair_exchange(*grad)
+    placed = call(place_kernel, "place", [f32(height, width)], 2 * unit, [], first_bond, *moved)[0]
+    grads = gy_reduce(outer, {1: grad, 2: moved, 3: (placed,)})
+    return placed.reshape(1, height, width), grads[:own], grads[own:]
 
 
 def solution(mesh):

time: 206 us -> 94 us (0.46)
  local copies, waits for them, and re-layouts: 71.5 us -> 1.89 us
  waiting for transfers between devices: 67.3 us -> 45.3 us
  Pallas kernels: 0 us -> 17.7 us
  starting transfers between devices: 41.3 us -> 27.7 us
  other arithmetic: 13 us -> 0.39 us
  matrix products: 10.9 us -> 0 us
    ppermute x32 -> x16, waiting for transfers between devices: 57.8 us -> 27.5 us  [ring_step(): lax.ppermute(block, 'gy', [(order[k], order[(k + step) % size]) for k in...]
    gather x11 -> x0, local copies, waits for them, and re-layouts: 28.3 us -> none  [the longest x2 9.06 us: on_device(): bond_first, bond_second = (bond_first[rows], bond_second[rows])]
    pallas_call x0 -> x9, Pallas kernels: none -> 17.7 us  [the longest x8 16 us: call(): pl.pallas_call(kernel, name=name, out_shape=outs, in_specs=[whole] * len(...]
    ppermute x32 -> x16, starting transfers between devices: 35.3 us -> 17.6 us  [ring_step(): lax.ppermute(block, 'gy', [(order[k], order[(k + step) % size]) for k in...]
    dot_general x5 -> x0, matrix products: 10.9 us -> none  [product(): lax.dot_general(left, right, (contract, ((), ())), precision=lax.Precisio...]
    unnamed x57 -> x10, local copies, waits for them, and re-layouts: 11.9 us -> 1.06 us
    scatter x2 -> x0, local copies, waits for them, and re-layouts: 8.62 us -> none  [inverse(): jnp.zeros_like(ordering).at[ordering]]
    ppermute x15 -> x17, waiting for transfers between devices: 9.49 us -> 17.8 us  [swap(): return lax.ppermute(block, 'gx', [(i, i ^ mask) for i in range(size)])]
  transfers between devices with their start and end apart: 47 -> 33, of which waited for: 22 -> 22; matrix products, arithmetic and copies ran while one was open for 44% -> 0% of each run, Pallas kernels for 0% -> 16%
where the time goes in v3:
time: 94 us; the launch traced here: 93.8 us
  waiting for transfers between devices  45.3 us (48%)
  starting transfers between devices  27.7 us (29%)
  Pallas kernels  17.7 us (19%)
  local copies, waits for them, and re-layouts  1.89 us (2%)
    ppermute x16, waiting for transfers between devices, ring_step(): lax.ppermute(block, 'gy', [(order[k], order[(k + step) % size]) for k in...  27.5 us
    ppermute x17, waiting for transfers between devices, swap(): return lax.ppermute(block, 'gx', [(i, i ^ mask) for i in range(size)])  17.8 us
    ppermute x16, starting transfers between devices, ring_step(): lax.ppermute(block, 'gy', [(order[k], order[(k + step) % size]) for k in...  17.6 us
    pallas_call x8, Pallas kernels, call(): pl.pallas_call(kernel, name=name, out_shape=outs, in_specs=[whole] * len(...  16 us
    ppermute x17, starting transfers between devices, swap(): return lax.ppermute(block, 'gx', [(i, i ^ mask) for i in range(size)])  10.1 us
  transfers between devices with their start and end apart: 33, of which 22 were waited for; matrix products, arithmetic and copies ran while one was open for 0% of the time, Pallas kernels for 16%

profile of v3, /device:TPU:0, one launch (start us, length us, event | category | flops | bytes accessed | tf_op | source)
XLA Modules:
  0.0 93.8 jit_solution(2506021905074985111)
XLA Ops:
  0.6 1.7 %pack.1.refs_4_ = f32[64,1024]{1,0:T(8,128)} custom-call(f32[32,1024]{1,0:T(8,128)} %first_ref.1, f32[32,1024]{1,0:T(8,128)} %second_ref.1), custom_call_target="tpu_custom_call" | custom-call | tf_op jit(solution)/shard_map/pack/pallas_call | solution.py:413
  2.4 3.1 %collective-permute-start.2 = (f32[64,1024]{1,0:T(8,128)}, f32[64,1024]{1,0:T(8,128)S(1)}, u32[]{:S(2)}, u32[]{:S(2)}) collective-permute-start(f32[64,1024]{1,0:T(8,128)} %pack.1.refs_4_), channel_id=1, source_target_pairs={{0,2},{2,4},{4,6},{6,7},{7,5},{5,3},{3,1},{1,0},{8,10},{10,12},{12... | collective-permute-start | bytes 786440 | tf_op jit(solution)/shard_map/ppermute | solution.py:69
  5.5 1.9 %collective-permute-start.5 = (f32[128,1024]{1,0:T(8,128)S(1)}, f32[128,1024]{1,0:T(8,128)S(1)}, u32[]{:S(2)}, u32[]{:S(2)}) collective-permute-start(f32[128,1024]{1,0:T(8,128)S(1)} %bitcast.5), channel_id=1, source_target_pairs={{0,16},{8,24},{16,0},{24,8},{1,17},{9,25},{17,1},{25,9},{2,18},{10... | collective-permute-start | bytes 1572872 | tf_op jit(solution)/shard_map/ppermute | solution.py:27
  7.4 1.0 %copy-done.2 = f32[1,128,1024]{2,1,0:T(8,128)S(1)} copy-done((f32[1,128,1024]{2,1,0:T(8,128)S(1)}, f32[1,128,1024]{2,1,0:T(8,128)}, u32[]{:S(2)}) %copy-start.2) | copy-done | bytes 524312
  8.5 1.0 %pick.1 = (f32[256,256]{1,0:T(8,128)S(1)}, f32[256,256]{1,0:T(8,128)S(1)}) custom-call(f32[128,1024]{1,0:T(8,128)S(1)} %bitcast.8, s32[1,1024]{1,0:T(1,128)S(1)} %bitcast.11), custom_call_target="tpu_custom_call" | custom-call | flops 536870912 | bytes 1052672 | tf_op jit(solution)/shard_map/pick/pallas_call | solution.py:373
  9.5 2.4 %collective-permute-done.2.refs_8_.refs_11_ = f32[64,1024]{1,0:T(8,128)S(1)} collective-permute-done((f32[64,1024]{1,0:T(8,128)}, f32[64,1024]{1,0:T(8,128)S(1)}, u32[]{:S(2)}, u32[]{:S(2)}) %collective-permute-start.2) | collective-permute-done | bytes 262176 | tf_op jit(solution)/shard_map/ppermute | solution.py:69
  11.9 1.5 %collective-permute-done.1.refs_5_ = f32[64,1024]{1,0:T(8,128)S(1)} collective-permute-done((f32[64,1024]{1,0:T(8,128)}, f32[64,1024]{1,0:T(8,128)S(1)}, u32[]{:S(2)}, u32[]{:S(2)}) %collective-permute-start.1) | collective-permute-done | bytes 262176 | tf_op jit(solution)/shard_map/ppermute | solution.py:69
  13.8 1.7 %collective-permute-start.4 = (f32[64,1024]{1,0:T(8,128)S(1)}, f32[64,1024]{1,0:T(8,128)S(1)}, u32[]{:S(2)}, u32[]{:S(2)}) collective-permute-start(f32[64,1024]{1,0:T(8,128)S(1)} %collective-permute-done.2.refs_8_.refs_11_), channel_id=1, source_target_pairs={{0,2},{2,4},{4,6},{6,7},{7,5},{5,3},{3,1},{1,0},{8,10},{10,12},{12... | collective-permute-start | bytes 786440 | tf_op jit(solution)/shard_map/ppermute | solution.py:69
  15.5 4.8 %collective-permute-done.3.refs_6_ = f32[64,1024]{1,0:T(8,128)S(1)} collective-permute-done((f32[64,1024]{1,0:T(8,128)S(1)}, f32[64,1024]{1,0:T(8,128)S(1)}, u32[]{:S(2)}, u32[]{:S(2)}) %collective-permute-start.3) | collective-permute-done | bytes 262176 | tf_op jit(solution)/shard_map/ppermute | solution.py:69
  20.7 1.5 %collective-permute-start.8 = (f32[64,1024]{1,0:T(8,128)S(1)}, f32[64,1024]{1,0:T(8,128)S(1)}, u32[]{:S(2)}, u32[]{:S(2)}) collective-permute-start(f32[64,1024]{1,0:T(8,128)S(1)} %collective-permute-done.3.refs_6_), channel_id=1, source_target_pairs={{0,1},{2,0},{4,2},{6,4},{7,6},{5,7},{3,5},{1,3},{8,9},{10,8},{12,1... | collective-permute-start | bytes 786440 | tf_op jit(solution)/shard_map/ppermute | solution.py:69
  22.2 0.5 collective-permute-start.9
  22.7 1.4 %collective-permute-start.10 = (f32[256,256]{1,0:T(8,128)S(1)}, f32[256,256]{1,0:T(8,128)S(1)}, u32[]{:S(2)}, u32[]{:S(2)}) collective-permute-start(f32[256,256]{1,0:T(8,128)S(1)} %get-tuple-element.79), channel_id=1, source_target_pairs={{0,16},{8,24},{16,0},{24,8},{1,17},{9,25},{17,1},{25,9},{2,18},{10... | collective-permute-start | bytes 786440 | tf_op jit(solution)/shard_map/ppermute | solution.py:27
  24.1 1.7 %early_back.1 = (f32[160,512]{1,0:T(8,128)S(1)}, bf16[512,1024]{1,0:T(8,128)(2,1)S(1)}, bf16[512,1024]{1,0:T(8,128)(2,1)S(1)}) custom-call(f32[128,1024]{1,0:T(8,128)S(1)} %bitcast.7, f32[128,1024]{1,0:T(8,128)S(1)} %collective-permute-done.refs_1_, f32[128,1024]{1,0:T(8,128)S(1)} %collective-permute-done.5.refs_2_, ...), custom_call_target="tpu_custom_call" | custom-call | flops 503316480 | bytes 5832704 | tf_op jit(solution)/shard_map/early_back/pallas_call | solution.py:373
  25.8 0.7 collective-permute-start.7
  26.5 2.9 %collective-permute-done.8.refs_0_.refs_7_ = f32[64,1024]{1,0:T(8,128)S(1)} collective-permute-done((f32[64,1024]{1,0:T(8,128)S(1)}, f32[64,1024]{1,0:T(8,128)S(1)}, u32[]{:S(2)}, u32[]{:S(2)}) %collective-permute-start.8) | collective-permute-done | bytes 262176 | tf_op jit(solution)/shard_map/ppermute | solution.py:69
  29.4 1.2 %collective-permute-done.9.refs_2_.refs_9_ = f32[64,1024]{1,0:T(8,128)S(1)} collective-permute-done((f32[64,1024]{1,0:T(8,128)S(1)}, f32[64,1024]{1,0:T(8,128)S(1)}, u32[]{:S(2)}, u32[]{:S(2)}) %collective-permute-start.9) | collective-permute-done | bytes 262176 | tf_op jit(solution)/shard_map/ppermute | solution.py:69
  30.6 1.3 %collective-permute-done.10.refs_2_.refs_10_ = f32[256,256]{1,0:T(8,128)S(1)} collective-permute-done((f32[256,256]{1,0:T(8,128)S(1)}, f32[256,256]{1,0:T(8,128)S(1)}, u32[]{:S(2)}, u32[]{:S(2)}) %collective-permute-start.10) | collective-permute-done | bytes 262176 | tf_op jit(solution)/shard_map/ppermute | solution.py:27
  32.4 1.4 %collective-permute-start.13 = (f32[32,1024]{1,0:T(8,128)S(1)}, f32[32,1024]{1,0:T(8,128)S(1)}, u32[]{:S(2)}, u32[]{:S(2)}) collective-permute-start(f32[32,1024]{1,0:T(8,128)S(1)} %slice.36), channel_id=1, source_target_pairs={{0,2},{2,4},{4,6},{6,7},{7,5},{5,3},{3,1},{1,0},{8,10},{10,12},{12... | collective-permute-start | bytes 393224 | tf_op jit(solution)/shard_map/ppermute | solution.py:69
  33.9 0.7 collective-permute-start.14
  34.6 3.3 %collective-permute-done.7.refs_2_ = f32[160,512]{1,0:T(8,128)S(1)} collective-permute-done((f32[160,512]{1,0:T(8,128)S(1)}, f32[160,512]{1,0:T(8,128)S(1)}, u32[]{:S(2)}, u32[]{:S(2)}) %collective-permute-start.7) | collective-permute-done | bytes 327712 | tf_op jit(solution)/shard_map/ppermute | solution.py:27
  37.9 1.1 %late_back.1.refs_4_ = f32[96,512]{1,0:T(8,128)S(1)} custom-call(bf16[512,1024]{1,0:T(8,128)(2,1)S(1)} %get-tuple-element.82.cotan_high, bf16[512,1024]{1,0:T(8,128)(2,1)S(1)} %get-tuple-element.83.cotan_low, f32[64,1024]{1,0:T(8,128)S(1)} %collective-permute-done.8.refs_0_.refs_7_, f32[32,1024]{1,0:T(8,128)S(1)} %collective-permute-done.13.refs_1_, ...), custom_call_target="tpu_custom_call" | custom-call | flops 301989888 | bytes 2949120 | tf_op jit(solution)/shard_map/late_back/pallas_call | solution.py:373
  39.0 1.5 %collective-permute-start.15 = (f32[96,512]{1,0:T(8,128)S(1)}, f32[96,512]{1,0:T(8,128)S(1)}, u32[]{:S(2)}, u32[]{:S(2)}) collective-permute-start(f32[96,512]{1,0:T(8,128)S(1)} %late_back.1.refs_4_), channel_id=1, source_target_pairs={{0,16},{8,24},{16,0},{24,8},{1,17},{9,25},{17,1},{25,9},{2,18},{10... | collective-permute-start | bytes 589832 | tf_op jit(solution)/shard_map/ppermute | solution.py:27
  40.5 3.8 %mid.1 = (f32[1024,256]{1,0:T(8,128)S(1)}, f32[1024,256]{1,0:T(8,128)S(1)}, bf16[256,1024]{1,0:T(8,128)(2,1)S(1)}, bf16[256,1024]{1,0:T(8,128)(2,1)S(1)}) custom-call(s32[1,1024]{1,0:T(1,128)S(1)} %bitcast.9, f32[256,256]{1,0:T(8,128)S(1)} %get-tuple-element.86.refs_0_.refs_8_, f32[256,256]{1,0:T(8,128)S(1)} %collective-permute-done.11.refs_1_.refs_9_, ...), custom_call_target="tpu_custom_call" | custom-call | flops 2952790016 | bytes 6164480 | tf_op jit(solution)/shard_map/mid/pallas_call | solution.py:373
  44.2 0.7 collective-permute-done.15.refs_6_
  45.5 2.1 %collective-permute-done.16 = f32[1024,256]{1,0:T(8,128)S(1)} collective-permute-done((f32[1024,256]{1,0:T(8,128)S(1)}, f32[1024,256]{1,0:T(8,128)S(1)}, u32[]{:S(2)}, u32[]{:S(2)}) %collective-permute-start.16) | collective-permute-done | bytes 1048608 | tf_op jit(solution)/shard_map/ppermute | solution.py:27
  48.1 1.4 %collective-permute-start.17 = (f32[512,256]{1,0:T(8,128)S(1)}, f32[512,256]{1,0:T(8,128)S(1)}, u32[]{:S(2)}, u32[]{:S(2)}) collective-permute-start(f32[512,256]{1,0:T(8,128)S(1)} %get-tuple-element.98), channel_id=1, source_target_pairs={{0,16},{8,24},{16,0},{24,8},{1,17},{9,25},{17,1},{25,9},{2,18},{10... | collective-permute-start | bytes 1572872 | tf_op jit(solution)/shard_map/ppermute | solution.py:27
  50.0 0.9 collective-permute-done.20.refs_5_
  51.2 3.8 %grad_first.1 = (f32[32,1024]{1,0:T(8,128)S(1)}, f32[32,1024]{1,0:T(8,128)S(1)}, f32[32,1024]{1,0:T(8,128)S(1)}, f32[32,1024]{1,0:T(8,128)S(1)}, f32[32,1024]{1,...) custom-call(s32[1,1024]{1,0:T(1,128)S(1)} %bitcast.10, ...), custom_call_target="tpu_custom_call" | custom-call | flops 2952790016 | bytes 6295552 | tf_op jit(solution)/shard_map/grad_first/pallas_call | solution.py:373
  55.0 7.2 %collective-permute-done.17.far_ref = f32[512,256]{1,0:T(8,128)S(1)} collective-permute-done((f32[512,256]{1,0:T(8,128)S(1)}, f32[512,256]{1,0:T(8,128)S(1)}, u32[]{:S(2)}, u32[]{:S(2)}) %collective-permute-start.17) | collective-permute-done | bytes 524320 | tf_op jit(solution)/shard_map/ppermute | solution.py:27
  62.3 1.2 %grad_second.1 = (f32[64,1024]{1,0:T(8,128)S(1)}, f32[64,1024]{1,0:T(8,128)S(1)}, f32[64,1024]{1,0:T(8,128)S(1)}, f32[64,1024]{1,0:T(8,128)S(1)}, f32[64,1024]{1...) custom-call(f32[512,256]{1,0:T(8,128)S(1)} %get-tuple-element.97.near_ref, ...), custom_call_target="tpu_custom_call" | custom-call | flops 805306368 | bytes 6291456 | tf_op jit(solution)/shard_map/grad_second/pallas_call | solution.py:373
  63.4 1.5 %collective-permute-start.26 = (f32[32,1024]{1,0:T(8,128)S(1)}, f32[32,1024]{1,0:T(8,128)S(1)}, u32[]{:S(2)}, u32[]{:S(2)}) collective-permute-start(f32[32,1024]{1,0:T(8,128)S(1)} %get-tuple-element.135), channel_id=1, source_target_pairs={{0,1},{2,0},{4,2},{6,4},{7,6},{5,7},{3,5},{1,3},{8,9},{10,8},{12,1... | collective-permute-start | bytes 393224 | tf_op jit(solution)/shard_map/ppermute | solution.py:69
  65.0 0.5 collective-permute-start.25
  65.5 1.1 %grad_stem.1 = (f32[512,128]{1,0:T(8,128)S(1)}, f32[512,128]{1,0:T(8,128)S(1)}) custom-call(bf16[256,1024]{1,0:T(8,128)(2,1)S(1)} %get-tuple-element.110.branch_high, bf16[256,1024]{1,0:T(8,128)(2,1)S(1)} %get-tuple-element.111.branch_low, bf16[1024,512]{1,0:T(8,128)(2,1)S(1)} %get-tuple-element.112.turned_high, ...), custom_call_target="tpu_custom_call" | custom-call | flops 805306368 | bytes 3670016 | tf_op jit(solution)/shard_map/grad_stem/pallas_call | solution.py:373
  66.6 1.5 %collective-permute-start.23 = (f32[512,128]{1,0:T(8,128)S(1)}, f32[512,128]{1,0:T(8,128)S(1)}, u32[]{:S(2)}, u32[]{:S(2)}) collective-permute-start(f32[512,128]{1,0:T(8,128)S(1)} %get-tuple-element.115), channel_id=1, source_target_pairs={{0,16},{8,24},{16,0},{24,8},{1,17},{9,25},{17,1},{25,9},{2,18},{10... | collective-permute-start | bytes 786440 | tf_op jit(solution)/shard_map/ppermute | solution.py:27
  68.5 1.5 %collective-permute-done.25 = f32[32,1024]{1,0:T(8,128)S(1)} collective-permute-done((f32[32,1024]{1,0:T(8,128)S(1)}, f32[32,1024]{1,0:T(8,128)S(1)}, u32[]{:S(2)}, u32[]{:S(2)}) %collective-permute-start.25) | collective-permute-done | bytes 131104 | tf_op jit(solution)/shard_map/ppermute | solution.py:69
  70.0 0.6 collective-permute-start.27
  70.6 1.5 %collective-permute-start.28 = (f32[64,1024]{1,0:T(8,128)S(1)}, f32[64,1024]{1,0:T(8,128)S(1)}, u32[]{:S(2)}, u32[]{:S(2)}) collective-permute-start(f32[64,1024]{1,0:T(8,128)S(1)} %get-tuple-element.123), channel_id=1, source_target_pairs={{0,1},{2,0},{4,2},{6,4},{7,6},{5,7},{3,5},{1,3},{8,9},{10,8},{12,1... | collective-permute-start | bytes 786440 | tf_op jit(solution)/shard_map/ppermute | solution.py:69
  72.1 1.8 %collective-permute-done.23.refs_2_ = f32[512,128]{1,0:T(8,128)S(1)} collective-permute-done((f32[512,128]{1,0:T(8,128)S(1)}, f32[512,128]{1,0:T(8,128)S(1)}, u32[]{:S(2)}, u32[]{:S(2)}) %collective-permute-start.23) | collective-permute-done | bytes 262176 | tf_op jit(solution)/shard_map/ppermute | solution.py:27
  73.9 2.8 %collective-permute-done.27 = f32[64,1024]{1,0:T(8,128)S(1)} collective-permute-done((f32[64,1024]{1,0:T(8,128)S(1)}, f32[64,1024]{1,0:T(8,128)S(1)}, u32[]{:S(2)}, u32[]{:S(2)}) %collective-permute-start.27) | collective-permute-done | bytes 262176 | tf_op jit(solution)/shard_map/ppermute | solution.py:69
  77.1 1.5 %collective-permute-start.29 = (f32[64,1024]{1,0:T(8,128)S(1)}, f32[64,1024]{1,0:T(8,128)S(1)}, u32[]{:S(2)}, u32[]{:S(2)}) collective-permute-start(f32[64,1024]{1,0:T(8,128)S(1)} %add.30), channel_id=1, source_target_pairs={{0,2},{2,4},{4,6},{6,7},{7,5},{5,3},{3,1},{1,0},{8,10},{10,12},{12... | collective-permute-start | bytes 786440 | tf_op jit(solution)/shard_map/ppermute | solution.py:69
  78.6 0.6 collective-permute-start.30
  79.1 2.4 %place.1 = f32[128,1024]{1,0:T(8,128)} custom-call(s32[1,1024]{1,0:T(1,128)S(1)} %bitcast.12, f32[512,128]{1,0:T(8,128)S(1)} %get-tuple-element.114.refs_0_, f32[512,128]{1,0:T(8,128)S(1)} %collective-permute-done.22.refs_1_, f32[512,128]{1,0:T(8,128)S(1)} %collective-permute-done.23.refs_2_, f32[512,128]{1,0:T(8,128)S(1)} %collective-permute-done.24.refs_3_), custom_call_target="tpu_custom_call" | custom-call | flops 536870912 | bytes 1576960 | tf_op jit(solution)/shard_map/place/pallas_call | solution.py:373
  81.5 2.3 %collective-permute-done.29 = f32[64,1024]{1,0:T(8,128)S(1)} collective-permute-done((f32[64,1024]{1,0:T(8,128)S(1)}, f32[64,1024]{1,0:T(8,128)S(1)}, u32[]{:S(2)}, u32[]{:S(2)}) %collective-permute-start.29) | collective-permute-done | bytes 262176 | tf_op jit(solution)/shard_map/ppermute | solution.py:69
  83.8 1.2 %collective-permute-done.30 = f32[64,1024]{1,0:T(8,128)S(1)} collective-permute-done((f32[64,1024]{1,0:T(8,128)S(1)}, f32[64,1024]{1,0:T(8,128)S(1)}, u32[]{:S(2)}, u32[]{:S(2)}) %collective-permute-start.30) | collective-permute-done | bytes 262176 | tf_op jit(solution)/shard_map/ppermute | solution.py:69
  85.0 1.6 %collective-permute-start.31 = (f32[64,1024]{1,0:T(8,128)S(1)}, f32[64,1024]{1,0:T(8,128)S(1)}, u32[]{:S(2)}, u32[]{:S(2)}) collective-permute-start(f32[64,1024]{1,0:T(8,128)S(1)} %add.32), channel_id=1, source_target_pairs={{0,2},{2,4},{4,6},{6,7},{7,5},{5,3},{3,1},{1,0},{8,10},{10,12},{12... | collective-permute-start | bytes 786440 | tf_op jit(solution)/shard_map/ppermute | solution.py:69
  87.1 4.3 %collective-permute-done.31 = f32[64,1024]{1,0:T(8,128)S(1)} collective-permute-done((f32[64,1024]{1,0:T(8,128)S(1)}, f32[64,1024]{1,0:T(8,128)S(1)}, u32[]{:S(2)}, u32[]{:S(2)}) %collective-permute-start.31) | collective-permute-done | bytes 262176 | tf_op jit(solution)/shard_map/ppermute | solution.py:69
  91.4 1.6 %collective-permute-done.32 = f32[64,1024]{1,0:T(8,128)S(1)} collective-permute-done((f32[64,1024]{1,0:T(8,128)S(1)}, f32[64,1024]{1,0:T(8,128)S(1)}, u32[]{:S(2)}, u32[]{:S(2)}) %collective-permute-start.32) | collective-permute-done | bytes 262176 | tf_op jit(solution)/shard_map/ppermute | solution.py:69
  93.1 0.7 fusion.1
  (51 shorter events, 4.3 us)
Async XLA Ops:
  0.6 4.9 %copy-start.1 = (f32[1,128,1024]{2,1,0:T(8,128)S(1)}, f32[1,128,1024]{2,1,0:T(8,128)}, u32[]{:S(2)}) copy-start(f32[1,128,1024]{2,1,0:T(8,128)} %param.7) | copy-start | bytes 1572868
  2.4 5.0 %copy-start.4 = (s32[1024]{0:T(1024)S(1)}, s32[1024]{0:T(1024)}, u32[]{:S(2)}) copy-start(s32[1024]{0:T(1024)} %param.10) | copy-start | bytes 12292
  2.4 9.5 %collective-permute-start.2 = (f32[64,1024]{1,0:T(8,128)}, f32[64,1024]{1,0:T(8,128)S(1)}, u32[]{:S(2)}, u32[]{:S(2)}) collective-permute-start(f32[64,1024]{1,0:T(8,128)} %pack.1.refs_4_), channel_id=1, source_target_pairs={{0,2},{2,4},{4,6},{6,7},{7,5},{5,3},{3,1},{1,0},{8,10},{10,12},{12... | collective-permute-start | bytes 786440 | tf_op jit(solution)/shard_map/ppermute | solution.py:69
  5.5 8.0 %collective-permute-start.1 = (f32[64,1024]{1,0:T(8,128)}, f32[64,1024]{1,0:T(8,128)S(1)}, u32[]{:S(2)}, u32[]{:S(2)}) collective-permute-start(f32[64,1024]{1,0:T(8,128)} %pack.1.refs_4_), channel_id=1, source_target_pairs={{0,1},{2,0},{4,2},{6,4},{7,6},{5,7},{3,5},{1,3},{8,9},{10,8},{12,1... | collective-permute-start | bytes 786440 | tf_op jit(solution)/shard_map/ppermute | solution.py:69
  5.5 15.2 %collective-permute-start.5 = (f32[128,1024]{1,0:T(8,128)S(1)}, f32[128,1024]{1,0:T(8,128)S(1)}, u32[]{:S(2)}, u32[]{:S(2)}) collective-permute-start(f32[128,1024]{1,0:T(8,128)S(1)} %bitcast.5), channel_id=1, source_target_pairs={{0,16},{8,24},{16,0},{24,8},{1,17},{9,25},{17,1},{25,9},{2,18},{10... | collective-permute-start | bytes 1572872 | tf_op jit(solution)/shard_map/ppermute | solution.py:27
  7.4 1.0 %copy-start.2 = (f32[1,128,1024]{2,1,0:T(8,128)S(1)}, f32[1,128,1024]{2,1,0:T(8,128)}, u32[]{:S(2)}) copy-start(f32[1,128,1024]{2,1,0:T(8,128)} %param.6) | copy-start | bytes 1572868
  8.5 15.6 %copy-start = (f32[64,1024]{1,0:T(8,128)S(1)}, f32[64,1024]{1,0:T(8,128)}, u32[]{:S(2)}) copy-start(f32[64,1024]{1,0:T(8,128)} %pack.1.refs_4_) | copy-start | bytes 786436
  13.5 6.9 %collective-permute-start.3 = (f32[64,1024]{1,0:T(8,128)S(1)}, f32[64,1024]{1,0:T(8,128)S(1)}, u32[]{:S(2)}, u32[]{:S(2)}) collective-permute-start(f32[64,1024]{1,0:T(8,128)S(1)} %collective-permute-done.1.refs_5_), channel_id=1, source_target_pairs={{0,1},{2,0},{4,2},{6,4},{7,6},{5,7},{3,5},{1,3},{8,9},{10,8},{12,1... | collective-permute-start | bytes 786440 | tf_op jit(solution)/shard_map/ppermute | solution.py:69
  13.8 6.9 %collective-permute-start.4 = (f32[64,1024]{1,0:T(8,128)S(1)}, f32[64,1024]{1,0:T(8,128)S(1)}, u32[]{:S(2)}, u32[]{:S(2)}) collective-permute-start(f32[64,1024]{1,0:T(8,128)S(1)} %collective-permute-done.2.refs_8_.refs_11_), channel_id=1, source_target_pairs={{0,2},{2,4},{4,6},{6,7},{7,5},{5,3},{3,1},{1,0},{8,10},{10,12},{12... | collective-permute-start | bytes 786440 | tf_op jit(solution)/shard_map/ppermute | solution.py:69
  15.5 8.6 %collective-permute-start = (f32[128,1024]{1,0:T(8,128)S(1)}, f32[128,1024]{1,0:T(8,128)S(1)}, u32[]{:S(2)}, u32[]{:S(2)}) collective-permute-start(f32[128,1024]{1,0:T(8,128)S(1)} %bitcast.6), channel_id=1, source_target_pairs={{0,8},{8,0},{16,24},{24,16},{1,9},{9,1},{17,25},{25,17},{2,10},{10... | collective-permute-start | bytes 1572872 | tf_op jit(solution)/shard_map/ppermute | solution.py:27
  20.7 3.4 %collective-permute-start.6 = (f32[128,1024]{1,0:T(8,128)S(1)}, f32[128,1024]{1,0:T(8,128)S(1)}, u32[]{:S(2)}, u32[]{:S(2)}) collective-permute-start(f32[128,1024]{1,0:T(8,128)S(1)} %collective-permute-done.5.refs_2_), channel_id=1, source_target_pairs={{0,8},{8,0},{16,24},{24,16},{1,9},{9,1},{17,25},{25,17},{2,10},{10... | collective-permute-start | bytes 1572872 | tf_op jit(solution)/shard_map/ppermute | solution.py:27
  20.7 8.7 %collective-permute-start.8 = (f32[64,1024]{1,0:T(8,128)S(1)}, f32[64,1024]{1,0:T(8,128)S(1)}, u32[]{:S(2)}, u32[]{:S(2)}) collective-permute-start(f32[64,1024]{1,0:T(8,128)S(1)} %collective-permute-done.3.refs_6_), channel_id=1, source_target_pairs={{0,1},{2,0},{4,2},{6,4},{7,6},{5,7},{3,5},{1,3},{8,9},{10,8},{12,1... | collective-permute-start | bytes 786440 | tf_op jit(solution)/shard_map/ppermute | solution.py:69
  22.2 8.4 %collective-permute-start.9 = (f32[64,1024]{1,0:T(8,128)S(1)}, f32[64,1024]{1,0:T(8,128)S(1)}, u32[]{:S(2)}, u32[]{:S(2)}) collective-permute-start(f32[64,1024]{1,0:T(8,128)S(1)} %collective-permute-done.4.refs_7_.refs_10_), channel_id=1, source_target_pairs={{0,2},{2,4},{4,6},{6,7},{7,5},{5,3},{3,1},{1,0},{8,10},{10,12},{12... | collective-permute-start | bytes 786440 | tf_op jit(solution)/shard_map/ppermute | solution.py:69
  22.7 9.2 %collective-permute-start.10 = (f32[256,256]{1,0:T(8,128)S(1)}, f32[256,256]{1,0:T(8,128)S(1)}, u32[]{:S(2)}, u32[]{:S(2)}) collective-permute-start(f32[256,256]{1,0:T(8,128)S(1)} %get-tuple-element.79), channel_id=1, source_target_pairs={{0,16},{8,24},{16,0},{24,8},{1,17},{9,25},{17,1},{25,9},{2,18},{10... | collective-permute-start | bytes 786440 | tf_op jit(solution)/shard_map/ppermute | solution.py:27
  25.8 12.1 %collective-permute-start.7 = (f32[160,512]{1,0:T(8,128)S(1)}, f32[160,512]{1,0:T(8,128)S(1)}, u32[]{:S(2)}, u32[]{:S(2)}) collective-permute-start(f32[160,512]{1,0:T(8,128)S(1)} %get-tuple-element.75.refs_0_), channel_id=1, source_target_pairs={{0,16},{8,24},{16,0},{24,8},{1,17},{9,25},{17,1},{25,9},{2,18},{10... | collective-permute-start | bytes 983048 | tf_op jit(solution)/shard_map/ppermute | solution.py:27
  31.9 2.7 %collective-permute-start.11 = (f32[256,256]{1,0:T(8,128)S(1)}, f32[256,256]{1,0:T(8,128)S(1)}, u32[]{:S(2)}, u32[]{:S(2)}) collective-permute-start(f32[256,256]{1,0:T(8,128)S(1)} %get-tuple-element.86.refs_0_.refs_8_), channel_id=1, source_target_pairs={{0,8},{8,0},{16,24},{24,16},{1,9},{9,1},{17,25},{25,17},{2,10},{10... | collective-permute-start | bytes 786440 | tf_op jit(solution)/shard_map/ppermute | solution.py:27
  31.9 2.7 %collective-permute-start.12 = (f32[256,256]{1,0:T(8,128)S(1)}, f32[256,256]{1,0:T(8,128)S(1)}, u32[]{:S(2)}, u32[]{:S(2)}) collective-permute-start(f32[256,256]{1,0:T(8,128)S(1)} %collective-permute-done.10.refs_2_.refs_10_), channel_id=1, source_target_pairs={{0,8},{8,0},{16,24},{24,16},{1,9},{9,1},{17,25},{25,17},{2,10},{10... | collective-permute-start | bytes 786440 | tf_op jit(solution)/shard_map/ppermute | solution.py:27
  32.4 5.5 %collective-permute-start.13 = (f32[32,1024]{1,0:T(8,128)S(1)}, f32[32,1024]{1,0:T(8,128)S(1)}, u32[]{:S(2)}, u32[]{:S(2)}) collective-permute-start(f32[32,1024]{1,0:T(8,128)S(1)} %slice.36), channel_id=1, source_target_pairs={{0,2},{2,4},{4,6},{6,7},{7,5},{5,3},{3,1},{1,0},{8,10},{10,12},{12... | collective-permute-start | bytes 393224 | tf_op jit(solution)/shard_map/ppermute | solution.py:69
  33.9 6.6 %collective-permute-start.14 = (f32[32,1024]{1,0:T(8,128)S(1)}, f32[32,1024]{1,0:T(8,128)S(1)}, u32[]{:S(2)}, u32[]{:S(2)}) collective-permute-start(f32[32,1024]{1,0:T(8,128)S(1)} %slice.37), channel_id=1, source_target_pairs={{0,1},{2,0},{4,2},{6,4},{7,6},{5,7},{3,5},{1,3},{8,9},{10,8},{12,1... | collective-permute-start | bytes 393224 | tf_op jit(solution)/shard_map/ppermute | solution.py:69
  37.9 2.6 %copy-start.3 = (s32[1024]{0:T(1024)S(1)}, s32[1024]{0:T(1024)}, u32[]{:S(2)}) copy-start(s32[1024]{0:T(1024)} %param.11) | copy-start | bytes 12292
  39.0 6.0 %collective-permute-start.15 = (f32[96,512]{1,0:T(8,128)S(1)}, f32[96,512]{1,0:T(8,128)S(1)}, u32[]{:S(2)}, u32[]{:S(2)}) collective-permute-start(f32[96,512]{1,0:T(8,128)S(1)} %late_back.1.refs_4_), channel_id=1, source_target_pairs={{0,16},{8,24},{16,0},{24,8},{1,17},{9,25},{17,1},{25,9},{2,18},{10... | collective-permute-start | bytes 589832 | tf_op jit(solution)/shard_map/ppermute | solution.py:27
  45.0 2.7 %collective-permute-start.16 = (f32[1024,256]{1,0:T(8,128)S(1)}, f32[1024,256]{1,0:T(8,128)S(1)}, u32[]{:S(2)}, u32[]{:S(2)}) collective-permute-start(f32[1024,256]{1,0:T(8,128)S(1)} %get-tuple-element.94), channel_id=1, source_target_pairs={{0,8},{8,0},{16,24},{24,16},{1,9},{9,1},{17,25},{25,17},{2,10},{10... | collective-permute-start | bytes 3145736 | tf_op jit(solution)/shard_map/ppermute | solution.py:27
  45.0 5.0 %collective-permute-start.18 = (f32[160,512]{1,0:T(8,128)S(1)}, f32[160,512]{1,0:T(8,128)S(1)}, u32[]{:S(2)}, u32[]{:S(2)}) collective-permute-start(f32[160,512]{1,0:T(8,128)S(1)} %get-tuple-element.75.refs_0_), channel_id=1, source_target_pairs={{0,8},{8,0},{16,24},{24,16},{1,9},{9,1},{17,25},{25,17},{2,10},{10... | collective-permute-start | bytes 983048 | tf_op jit(solution)/shard_map/ppermute | solution.py:27
  47.9 3.3 %collective-permute-start.19 = (f32[160,512]{1,0:T(8,128)S(1)}, f32[160,512]{1,0:T(8,128)S(1)}, u32[]{:S(2)}, u32[]{:S(2)}) collective-permute-start(f32[160,512]{1,0:T(8,128)S(1)} %collective-permute-done.7.refs_2_), channel_id=1, source_target_pairs={{0,8},{8,0},{16,24},{24,16},{1,9},{9,1},{17,25},{25,17},{2,10},{10... | collective-permute-start | bytes 983048 | tf_op jit(solution)/shard_map/ppermute | solution.py:27
  48.1 14.2 %collective-permute-start.17 = (f32[512,256]{1,0:T(8,128)S(1)}, f32[512,256]{1,0:T(8,128)S(1)}, u32[]{:S(2)}, u32[]{:S(2)}) collective-permute-start(f32[512,256]{1,0:T(8,128)S(1)} %get-tuple-element.98), channel_id=1, source_target_pairs={{0,16},{8,24},{16,0},{24,8},{1,17},{9,25},{17,1},{25,9},{2,18},{10... | collective-permute-start | bytes 1572872 | tf_op jit(solution)/shard_map/ppermute | solution.py:27
  49.5 1.4 %collective-permute-start.20 = (f32[96,512]{1,0:T(8,128)S(1)}, f32[96,512]{1,0:T(8,128)S(1)}, u32[]{:S(2)}, u32[]{:S(2)}) collective-permute-start(f32[96,512]{1,0:T(8,128)S(1)} %late_back.1.refs_4_), channel_id=1, source_target_pairs={{0,8},{8,0},{16,24},{24,16},{1,9},{9,1},{17,25},{25,17},{2,10},{10... | collective-permute-start | bytes 589832 | tf_op jit(solution)/shard_map/ppermute | solution.py:27
  49.6 1.6 %collective-permute-start.21 = (f32[96,512]{1,0:T(8,128)S(1)}, f32[96,512]{1,0:T(8,128)S(1)}, u32[]{:S(2)}, u32[]{:S(2)}) collective-permute-start(f32[96,512]{1,0:T(8,128)S(1)} %collective-permute-done.15.refs_6_), channel_id=1, source_target_pairs={{0,8},{8,0},{16,24},{24,16},{1,9},{9,1},{17,25},{25,17},{2,10},{10... | collective-permute-start | bytes 589832 | tf_op jit(solution)/shard_map/ppermute | solution.py:27
  63.4 5.0 %collective-permute-start.26 = (f32[32,1024]{1,0:T(8,128)S(1)}, f32[32,1024]{1,0:T(8,128)S(1)}, u32[]{:S(2)}, u32[]{:S(2)}) collective-permute-start(f32[32,1024]{1,0:T(8,128)S(1)} %get-tuple-element.135), channel_id=1, source_target_pairs={{0,1},{2,0},{4,2},{6,4},{7,6},{5,7},{3,5},{1,3},{8,9},{10,8},{12,1... | collective-permute-start | bytes 393224 | tf_op jit(solution)/shard_map/ppermute | solution.py:69
  65.0 5.0 %collective-permute-start.25 = (f32[32,1024]{1,0:T(8,128)S(1)}, f32[32,1024]{1,0:T(8,128)S(1)}, u32[]{:S(2)}, u32[]{:S(2)}) collective-permute-start(f32[32,1024]{1,0:T(8,128)S(1)} %get-tuple-element.136), channel_id=1, source_target_pairs={{0,2},{2,4},{4,6},{6,7},{7,5},{5,3},{3,1},{1,0},{8,10},{10,12},{12... | collective-permute-start | bytes 393224 | tf_op jit(solution)/shard_map/ppermute | solution.py:69
  66.6 7.3 %collective-permute-start.23 = (f32[512,128]{1,0:T(8,128)S(1)}, f32[512,128]{1,0:T(8,128)S(1)}, u32[]{:S(2)}, u32[]{:S(2)}) collective-permute-start(f32[512,128]{1,0:T(8,128)S(1)} %get-tuple-element.115), channel_id=1, source_target_pairs={{0,16},{8,24},{16,0},{24,8},{1,17},{9,25},{17,1},{25,9},{2,18},{10... | collective-permute-start | bytes 786440 | tf_op jit(solution)/shard_map/ppermute | solution.py:27
  70.0 6.7 %collective-permute-start.27 = (f32[64,1024]{1,0:T(8,128)S(1)}, f32[64,1024]{1,0:T(8,128)S(1)}, u32[]{:S(2)}, u32[]{:S(2)}) collective-permute-start(f32[64,1024]{1,0:T(8,128)S(1)} %get-tuple-element.121), channel_id=1, source_target_pairs={{0,2},{2,4},{4,6},{6,7},{7,5},{5,3},{3,1},{1,0},{8,10},{10,12},{12... | collective-permute-start | bytes 786440 | tf_op jit(solution)/shard_map/ppermute | solution.py:69
  70.6 6.4 %collective-permute-start.28 = (f32[64,1024]{1,0:T(8,128)S(1)}, f32[64,1024]{1,0:T(8,128)S(1)}, u32[]{:S(2)}, u32[]{:S(2)}) collective-permute-start(f32[64,1024]{1,0:T(8,128)S(1)} %get-tuple-element.123), channel_id=1, source_target_pairs={{0,1},{2,0},{4,2},{6,4},{7,6},{5,7},{3,5},{1,3},{8,9},{10,8},{12,1... | collective-permute-start | bytes 786440 | tf_op jit(solution)/shard_map/ppermute | solution.py:69
  72.1 4.9 %collective-permute-start.22 = (f32[512,128]{1,0:T(8,128)S(1)}, f32[512,128]{1,0:T(8,128)S(1)}, u32[]{:S(2)}, u32[]{:S(2)}) collective-permute-start(f32[512,128]{1,0:T(8,128)S(1)} %get-tuple-element.114.refs_0_), channel_id=1, source_target_pairs={{0,8},{8,0},{16,24},{24,16},{1,9},{9,1},{17,25},{25,17},{2,10},{10... | collective-permute-start | bytes 786440 | tf_op jit(solution)/shard_map/ppermute | solution.py:27
  73.9 3.1 %collective-permute-start.24 = (f32[512,128]{1,0:T(8,128)S(1)}, f32[512,128]{1,0:T(8,128)S(1)}, u32[]{:S(2)}, u32[]{:S(2)}) collective-permute-start(f32[512,128]{1,0:T(8,128)S(1)} %collective-permute-done.23.refs_2_), channel_id=1, source_target_pairs={{0,8},{8,0},{16,24},{24,16},{1,9},{9,1},{17,25},{25,17},{2,10},{10... | collective-permute-start | bytes 786440 | tf_op jit(solution)/shard_map/ppermute | solution.py:27
  77.1 6.7 %collective-permute-start.29 = (f32[64,1024]{1,0:T(8,128)S(1)}, f32[64,1024]{1,0:T(8,128)S(1)}, u32[]{:S(2)}, u32[]{:S(2)}) collective-permute-start(f32[64,1024]{1,0:T(8,128)S(1)} %add.30), channel_id=1, source_target_pairs={{0,2},{2,4},{4,6},{6,7},{7,5},{5,3},{3,1},{1,0},{8,10},{10,12},{12... | collective-permute-start | bytes 786440 | tf_op jit(solution)/shard_map/ppermute | solution.py:69
  78.6 6.4 %collective-permute-start.30 = (f32[64,1024]{1,0:T(8,128)S(1)}, f32[64,1024]{1,0:T(8,128)S(1)}, u32[]{:S(2)}, u32[]{:S(2)}) collective-permute-start(f32[64,1024]{1,0:T(8,128)S(1)} %add.31), channel_id=1, source_target_pairs={{0,1},{2,0},{4,2},{6,4},{7,6},{5,7},{3,5},{1,3},{8,9},{10,8},{12,1... | collective-permute-start | bytes 786440 | tf_op jit(solution)/shard_map/ppermute | solution.py:69
  85.0 6.4 %collective-permute-start.31 = (f32[64,1024]{1,0:T(8,128)S(1)}, f32[64,1024]{1,0:T(8,128)S(1)}, u32[]{:S(2)}, u32[]{:S(2)}) collective-permute-start(f32[64,1024]{1,0:T(8,128)S(1)} %add.32), channel_id=1, source_target_pairs={{0,2},{2,4},{4,6},{6,7},{7,5},{5,3},{3,1},{1,0},{8,10},{10,12},{12... | collective-permute-start | bytes 786440 | tf_op jit(solution)/shard_map/ppermute | solution.py:69
  86.6 6.4 %collective-permute-start.32 = (f32[64,1024]{1,0:T(8,128)S(1)}, f32[64,1024]{1,0:T(8,128)S(1)}, u32[]{:S(2)}, u32[]{:S(2)}) collective-permute-start(f32[64,1024]{1,0:T(8,128)S(1)} %add.33), channel_id=1, source_target_pairs={{0,1},{2,0},{4,2},{6,4},{7,6},{5,7},{3,5},{1,3},{8,9},{10,8},{12,1... | collective-permute-start | bytes 786440 | tf_op jit(solution)/shard_map/ppermute | solution.py:69

commit v4 on v3

--- a/solution.py
+++ b/solution.py
@@ -108,21 +108,40 @@
     return jnp.concatenate(gy_pieces(block), axis=0)
 
 
-def gy_reduce(blocks, waits=()):
-    size = lax.axis_size("gy")
-    waits = dict(waits)
-    half = blocks[0].shape[0] // 2
-    far = blocks[size // 2]
-    ahead, behind = ring_step(far[:half], 1), ring_step(far[half:], -1)
-    near, back = blocks[size // 2 - 1], blocks[size // 2 + 1]
-    ahead = jnp.concatenate([near[:half] + ahead, near[half:]], axis=0)
-    behind = jnp.concatenate([back[:half], back[half:] + behind], axis=0)
-    for step in range(size // 2 - 2, -1, -1):
-        ahead, behind = lax.optimization_barrier((ahead, behind, *waits.get(size // 2 - 1 - step, ())))[:2]
-        ahead, behind = ring_step(ahead, 1), ring_step(behind, -1)
-        if step:
-            ahead, behind = blocks[step] + ahead, blocks[size - step] + behind
-    return blocks[0] + ahead + behind
+class RingSum:
+    def __init__(self, blocks):
+        self.size = len(blocks)
+        self.left = self.size // 2
+        self.blocks = blocks
+        self.half = blocks[0].shape[0] // 2
+        far = blocks[self.left]
+        self.ahead, self.behind = far[: self.half], far[self.half :]
+        self.total = None
+
+    def after(self, *others):
+        self.ahead, self.behind, *others = lax.optimization_barrier((self.ahead, self.behind, *others))
+        return others
+
+    def step(self):
+        ahead, behind = ring_step(self.ahead, 1), ring_step(self.behind, -1)
+        self.left -= 1
+        if not self.left:
+            self.total = self.blocks[0] + ahead + behind
+            return
+        near, back = self.blocks[self.left], self.blocks[self.size - self.left]
+        if ahead.shape[0] == self.half:
+            ahead = jnp.concatenate([near[: self.half] + ahead, near[self.half :]], axis=0)
+            behind = jnp.concatenate([back[: self.half], back[self.half :] + behind], axis=0)
+            self.ahead, self.behind = ahead, behind
+        else:
+            self.ahead, self.behind = near + ahead, back + behind
+
+
+def gy_reduce(blocks):
+    ring = RingSum(blocks)
+    for _ in range(ring.size // 2):
+        ring.step()
+    return ring.total
 
 
 def plain(stem_first, cotangent, branch_first, branch_second, bond_first, bond_second):
@@ -206,7 +225,7 @@
 
 
 def early_offsets(size):
-    near = [k for k in range(size) if min(k, size - k) <= size // 4]
+    near = [k for k in range(size) if min(k, size - k) <= min(2, size // 4)]
     return near, [k for k in range(size) if k not in near]
 
 
@@ -234,16 +253,12 @@
         pair_refs[rel // 2][rel % 2 * size : (rel % 2 + 1) * size] = block
 
 
-def pack_kernel(first_ref, second_ref, pair_ref, done):
-    own = first_ref.shape[0]
-    copies = [
-        pltpu.make_async_copy(ref, pair_ref.at[pl.ds(part * own, own)], done.at[part])
-        for part, ref in enumerate((first_ref, second_ref))
-    ]
-    for copy in copies:
-        copy.start()
-    for copy in copies:
-        copy.wait()
+def pack_kernel(*refs):
+    ahead, behind = refs[4:]
+    own = refs[0].shape[0]
+    for part, (ahead_ref, behind_ref) in enumerate((refs[:2], refs[2:4])):
+        ahead[part * own : (part + 1) * own] = ahead_ref[...]
+        behind[part * own : (part + 1) * own] = behind_ref[...]
 
 
 def pick_kernel(groups, stem_ref, bond_ref, *out_refs):
@@ -264,23 +279,27 @@
             store_split(*mid, (slice(h * height, (h + 1) * height), columns), value)
 
 
-def put_picks(bond_ref, mid, out_refs):
-    width = mid[0].shape[1]
-    rows, low = mid[0].shape[0], out_refs[0].shape[1]
-    for rel in range(width // low):
-        select = chosen(bond_ref, rel, low, width)
+def put_picks(bond_ref, mid, out_ref, side):
+    rows, width = mid[0].shape
+    low = out_ref.shape[1]
+    for part in range(2):
+        select = chosen(bond_ref, 2 * part + side, low, width)
         block = dot(mid[0][...], select, ((1,), (0,))) + dot(mid[1][...], select, ((1,), (0,)))
-        out_refs[rel % 2][rel // 2 * rows : (rel // 2 + 1) * rows] = block
+        out_ref[part * rows : (part + 1) * rows] = block
 
 
 def mid_kernel(groups, bond_ref, *refs):
     picked, refs = refs[:groups], refs[groups:]
-    out_refs, branch, mid = refs[-6:-4], refs[-4:-2], refs[-2:]
+    out_ref, branch, mid = refs[-5], refs[-4:-2], refs[-2:]
     own = branch[0].shape[0] // lax.axis_size("gy")
-    for k, ref in enumerate(refs[:-6]):
+    for k, ref in enumerate(refs[:-5]):
         store_split(*branch, aligned(ring_owner(k), own), branch_rows(ref, own, 0))
     absorb(picked, branch, mid, groups)
-    put_picks(bond_ref, mid, out_refs)
+    put_picks(bond_ref, mid, out_ref, 1)
+
+
+def rest_kernel(bond_ref, mid_high, mid_low, out_ref):
+    put_picks(bond_ref, (mid_high, mid_low), out_ref, 0)
 
 
 def gather_rows(pieces, rows, own):
@@ -409,19 +428,10 @@
     def wide(*shape):
         return [pltpu.VMEM(shape, jnp.bfloat16)] * 2
 
-    inside, anywhere = pl.BlockSpec(memory_space=pltpu.VMEM), pl.BlockSpec(memory_space=pl.ANY)
-    pair = pl.pallas_call(
-        pack_kernel,
-        name="pack",
-        out_shape=f32(2 * own, width),
-        in_specs=[anywhere] * 2,
-        out_specs=inside,
-        scratch_shapes=[pltpu.SemaphoreType.DMA((2,))],
-        compiler_params=pltpu.CompilerParams(vmem_limit_bytes=60 * 1024 * 1024),
-    )(branch_first, branch_second)
-    ring = Ring(pair)
-    ring.step()
+    neighbours = [ring_step(branch, step) for branch in (branch_first, branch_second) for step in (-1, 1)]
     cotan_far = swap(cotan_rows, 2)
+    ring = Ring(None)
+    ring.taken = 1
     near, away = call(
         functools.partial(pick_kernel, groups),
         "pick",
@@ -429,14 +439,17 @@
         2 * unit,
         [],
         stem_rows,
-        ordered(first_bond, pair),
-    )
+        first_bond,
+    )
+    ring.ahead, ring.behind = call(pack_kernel, "pack", [f32(2 * own, width)] * 2, 0, [], *neighbours)
+    ring.pieces[1], ring.pieces[-1] = ring.ahead, ring.behind
     near, away = ring.after(near, away)
     ring.step()
+    ring.pieces[0] = branch_second
     pieces = dict(enumerate(ring.pieces))
+    away = swap(away, 2)
     cotan_far, near, away = ring.after(cotan_far, near, away)
     ring.step()
-    away = swap(away, 2)
     near_back, cotan_high, cotan_low = call(
         functools.partial(early_back_kernel, groups, own),
         "early_back",
@@ -450,13 +463,13 @@
         *[pieces[k] for k in early],
     )
     near_far = swap(near_back, 2)
-    near, away, _ = ring.after(near, away, near_back)
+    ring.after(near_back)
     for _ in range(ring.size // 2 - 3):
         ring.step()
     picked = near, swap(near, 1), away, swap(away, 1)
     cotan_high, near_far, *picked = lax.optimization_barrier((cotan_high, near_far, *picked))
     far = splits // 2
-    pieces_first = ring.pieces[: far + 1] + ring.pieces[far + 2 :]
+    pieces_first = [branch_first] + ring.pieces[1 : far + 1] + ring.pieces[far + 2 :]
     pieces_second = ring.pieces[:far] + ring.pieces[far + 1 :]
     far_back = call(
         functools.partial(late_back_kernel, own),
@@ -469,19 +482,19 @@
         *[pieces_second[k] for k in late],
     )[0]
     far_far = swap(far_back, 2)
-    *mid, first_high, first_low = call(
+    across, first_high, first_low, mid_high, mid_low = call(
         functools.partial(mid_kernel, groups),
         "mid",
-        [f32(2 * tall, low)] * 2 + [b16(low, width)] * 2,
-        3 * unit + 2 * groups * unit,
-        wide(tall, width),
+        [f32(2 * tall, low)] + [b16(low, width)] * 2 + [b16(tall, width)] * 2,
+        3 * unit + groups * unit,
+        [],
         ordered(second_bond, far_back),
         *picked,
         *pieces_first,
     )
-    mid[1], far_far = lax.optimization_barrier((mid[1], far_far))
-    mid = mid[0] + swap(mid[1], 1)
-    near_mid, away_mid, far_far, near_far = lax.optimization_barrier((mid[:tall], mid[tall:], far_far, near_far))
+    beside = call(rest_kernel, "rest", [f32(2 * tall, low)], 50 * groups * unit, [], ordered(second_bond, far_far), mid_high, mid_low)[0]
+    mid = beside + swap(across, 1)
+    near_mid, away_mid, near_far = lax.optimization_barrier((mid[:tall], mid[tall:], near_far))
     regrouped = [near_mid, swap(away_mid, 2)]
     gathered = [
         [near_back, swap(near_back, 1), near_far, swap(near_far, 1)],
@@ -498,6 +511,18 @@
         *gathered[1],
         *picked,
     )
+    grad = call(
+        functools.partial(stem_kernel, groups),
+        "grad_stem",
+        [f32(2 * low, height)] * 2,
+        3 * unit,
+        [pltpu.VMEM((low, tall), jnp.float32)],
+        first_high,
+        first_low,
+        turned_high,
+        turned_low,
+    )
+    *grad, regrouped[0] = lax.optimization_barrier((*grad, regrouped[0]))
     outer = call(
         functools.partial(second_kernel, factor),
         "grad_second",
@@ -509,21 +534,16 @@
         cotan_low,
         *outer_first,
     )
-    grad = call(
-        functools.partial(stem_kernel, groups),
-        "grad_stem",
-        [f32(2 * low, height)] * 2,
-        3 * unit,
-        [pltpu.VMEM((low, tall), jnp.float32)],
-        ordered(first_high, outer[0]),
-        first_low,
-        turned_high,
-        turned_low,
-    )
-    moved = pair_exchange(*grad)
+    sums = RingSum(outer)
+    sums.step()
+    grad = sums.after(*grad)
+    sums.step()
+    for _ in range(far - 3):
+        sums.step()
+    moved = sums.after(*pair_exchange(*grad))
+    sums.step()
     placed = call(place_kernel, "place", [f32(height, width)], 2 * unit, [], first_bond, *moved)[0]
-    grads = gy_reduce(outer, {1: grad, 2: moved, 3: (placed,)})
-    return placed.reshape(1, height, width), grads[:own], grads[own:]
+    return placed.reshape(1, height, width), sums.total[:own], sums.total[own:]
 
 
 def solution(mesh):

time: 94 us -> 90.1 us (0.959)
  waiting for transfers between devices: 45.3 us -> 39.7 us
  starting transfers between devices: 27.7 us -> 30.9 us
  Pallas kernels: 17.7 us -> 16.1 us
    ppermute x17, waiting for transfers between devices: 17.8 us -> 10.2 us  [swap(): return lax.ppermute(block, 'gx', [(i, i ^ mask) for i in range(size)])]
    ppermute x16 -> x18, waiting for transfers between devices: 27.5 us -> 29.6 us  [ring_step(): lax.ppermute(block, 'gy', [(order[k], order[(k + step) % size]) for k in...]
    ppermute x17, starting transfers between devices: 10.1 us -> 12.1 us  [swap(): return lax.ppermute(block, 'gx', [(i, i ^ mask) for i in range(size)])]
    pallas_call x1 -> x0, Pallas kernels: 1.74 us -> none  [on_device(): pl.pallas_call(pack_kernel, name='pack', out_shape=f32(2 * own, width), i...]
    ppermute x16 -> x18, starting transfers between devices: 17.6 us -> 18.8 us  [ring_step(): lax.ppermute(block, 'gy', [(order[k], order[(k + step) % size]) for k in...]
    pallas_call x8 -> x10, Pallas kernels: 16 us -> 16.1 us  [call(): pl.pallas_call(kernel, name=name, out_shape=outs, in_specs=[whole] * len(...]
  transfers between devices with their start and end apart: 33 -> 35, of which waited for: 22 -> 21; matrix products, arithmetic and copies ran while one was open for 0% -> 0% of each run, Pallas kernels for 16% -> 17%
where the time goes in v4:
time: 90.1 us; the launch traced here: 89.9 us
  waiting for transfers between devices  39.7 us (44%)
  starting transfers between devices  30.9 us (34%)
  Pallas kernels  16.1 us (18%)
  local copies, waits for them, and re-layouts  1.89 us (2%)
    ppermute x18, waiting for transfers between devices, ring_step(): lax.ppermute(block, 'gy', [(order[k], order[(k + step) % size]) for k in...  29.6 us
    ppermute x18, starting transfers between devices, ring_step(): lax.ppermute(block, 'gy', [(order[k], order[(k + step) % size]) for k in...  18.8 us
    pallas_call x10, Pallas kernels, call(): pl.pallas_call(kernel, name=name, out_shape=outs, in_specs=[whole] * len(...  16.1 us
    ppermute x17, starting transfers between devices, swap(): return lax.ppermute(block, 'gx', [(i, i ^ mask) for i in range(size)])  12.1 us
    ppermute x17, waiting for transfers between devices, swap(): return lax.ppermute(block, 'gx', [(i, i ^ mask) for i in range(size)])  10.2 us
  transfers between devices with their start and end apart: 35, of which 21 were waited for; matrix products, arithmetic and copies ran while one was open for 0% of the time, Pallas kernels for 17%

profile of v4, /device:TPU:0, one launch (start us, length us, event | category | flops | bytes accessed | tf_op | source)
XLA Modules:
  0.0 89.9 jit_solution(11549576627930155192)
XLA Ops:
  0.6 3.0 %collective-permute-start.7 = (f32[128,1024]{1,0:T(8,128)}, f32[128,1024]{1,0:T(8,128)S(1)}, u32[]{:S(2)}, u32[]{:S(2)}) collective-permute-start(f32[128,1024]{1,0:T(8,128)} %bitcast.5), channel_id=1, source_target_pairs={{0,16},{8,24},{16,0},{24,8},{1,17},{9,25},{17,1},{25,9},{2,18},{10... | collective-permute-start | bytes 1572872 | tf_op jit(solution)/shard_map/ppermute | solution.py:27
  3.6 1.5 %collective-permute-start.1 = (f32[32,1024]{1,0:T(8,128)}, f32[32,1024]{1,0:T(8,128)S(1)}, u32[]{:S(2)}, u32[]{:S(2)}) collective-permute-start(f32[32,1024]{1,0:T(8,128)} %refs_4_.3), channel_id=1, source_target_pairs={{0,1},{2,0},{4,2},{6,4},{7,6},{5,7},{3,5},{1,3},{8,9},{10,8},{12,1... | collective-permute-start | bytes 393224 | tf_op jit(solution)/shard_map/ppermute | solution.py:69
  5.2 0.5 collective-permute-start.2
  5.7 1.5 %collective-permute-start.3 = (f32[32,1024]{1,0:T(8,128)}, f32[32,1024]{1,0:T(8,128)S(1)}, u32[]{:S(2)}, u32[]{:S(2)}) collective-permute-start(f32[32,1024]{1,0:T(8,128)} %refs_4_.2), channel_id=1, source_target_pairs={{0,1},{2,0},{4,2},{6,4},{7,6},{5,7},{3,5},{1,3},{8,9},{10,8},{12,1... | collective-permute-start | bytes 393224 | tf_op jit(solution)/shard_map/ppermute | solution.py:69
  7.2 0.5 collective-permute-start.4
  7.7 1.0 %copy-done.2 = f32[1,128,1024]{2,1,0:T(8,128)S(1)} copy-done((f32[1,128,1024]{2,1,0:T(8,128)S(1)}, f32[1,128,1024]{2,1,0:T(8,128)}, u32[]{:S(2)}) %copy-start.2) | copy-done | bytes 524312
  8.7 1.0 %pick.1 = (f32[256,256]{1,0:T(8,128)S(1)}, f32[256,256]{1,0:T(8,128)S(1)}) custom-call(f32[128,1024]{1,0:T(8,128)S(1)} %bitcast.8, s32[1,1024]{1,0:T(1,128)S(1)} %bitcast.12), custom_call_target="tpu_custom_call" | custom-call | flops 536870912 | bytes 1052672 | tf_op jit(solution)/shard_map/pick/pallas_call | solution.py:392
  10.2 1.3 %collective-permute-done.2.refs_1_ = f32[32,1024]{1,0:T(8,128)S(1)} collective-permute-done((f32[32,1024]{1,0:T(8,128)}, f32[32,1024]{1,0:T(8,128)S(1)}, u32[]{:S(2)}, u32[]{:S(2)}) %collective-permute-start.2) | collective-permute-done | bytes 131104 | tf_op jit(solution)/shard_map/ppermute | solution.py:69
  11.6 1.3 %collective-permute-done.4.refs_3_ = f32[32,1024]{1,0:T(8,128)S(1)} collective-permute-done((f32[32,1024]{1,0:T(8,128)}, f32[32,1024]{1,0:T(8,128)S(1)}, u32[]{:S(2)}, u32[]{:S(2)}) %collective-permute-start.4) | collective-permute-done | bytes 131104 | tf_op jit(solution)/shard_map/ppermute | solution.py:69
  13.0 1.6 %collective-permute-start.5 = (f32[64,1024]{1,0:T(8,128)S(1)}, f32[64,1024]{1,0:T(8,128)S(1)}, u32[]{:S(2)}, u32[]{:S(2)}) collective-permute-start(f32[64,1024]{1,0:T(8,128)S(1)} %get-tuple-element.74.refs_5_), channel_id=1, source_target_pairs={{0,1},{2,0},{4,2},{6,4},{7,6},{5,7},{3,5},{1,3},{8,9},{10,8},{12,1... | collective-permute-start | bytes 786440 | tf_op jit(solution)/shard_map/ppermute | solution.py:69
  15.0 0.5 collective-permute-start.8
  15.6 4.1 %collective-permute-done.5.refs_6_ = f32[64,1024]{1,0:T(8,128)S(1)} collective-permute-done((f32[64,1024]{1,0:T(8,128)S(1)}, f32[64,1024]{1,0:T(8,128)S(1)}, u32[]{:S(2)}, u32[]{:S(2)}) %collective-permute-start.5) | collective-permute-done | bytes 262176 | tf_op jit(solution)/shard_map/ppermute | solution.py:69
  19.7 1.3 %collective-permute-done.6.refs_7_.refs_10_ = f32[64,1024]{1,0:T(8,128)S(1)} collective-permute-done((f32[64,1024]{1,0:T(8,128)S(1)}, f32[64,1024]{1,0:T(8,128)S(1)}, u32[]{:S(2)}, u32[]{:S(2)}) %collective-permute-start.6) | collective-permute-done | bytes 262176 | tf_op jit(solution)/shard_map/ppermute | solution.py:69
  21.4 1.8 %collective-permute-start.13 = (f32[64,1024]{1,0:T(8,128)S(1)}, f32[64,1024]{1,0:T(8,128)S(1)}, u32[]{:S(2)}, u32[]{:S(2)}) collective-permute-start(f32[64,1024]{1,0:T(8,128)S(1)} %collective-permute-done.5.refs_6_), channel_id=1, source_target_pairs={{0,1},{2,0},{4,2},{6,4},{7,6},{5,7},{3,5},{1,3},{8,9},{10,8},{12,1... | collective-permute-start | bytes 786440 | tf_op jit(solution)/shard_map/ppermute | solution.py:69
  23.5 1.7 %early_back.1 = (f32[160,512]{1,0:T(8,128)S(1)}, bf16[512,1024]{1,0:T(8,128)(2,1)S(1)}, bf16[512,1024]{1,0:T(8,128)(2,1)S(1)}) custom-call(f32[128,1024]{1,0:T(8,128)S(1)} %bitcast.7, f32[128,1024]{1,0:T(8,128)S(1)} %collective-permute-done.refs_1_, f32[128,1024]{1,0:T(8,128)S(1)} %collective-permute-done.7.refs_2_, ...), custom_call_target="tpu_custom_call" | custom-call | flops 503316480 | bytes 5701632 | tf_op jit(solution)/shard_map/early_back/pallas_call | solution.py:392
  25.1 1.8 %collective-permute-start.10 = (f32[160,512]{1,0:T(8,128)S(1)}, f32[160,512]{1,0:T(8,128)S(1)}, u32[]{:S(2)}, u32[]{:S(2)}) collective-permute-start(f32[160,512]{1,0:T(8,128)S(1)} %get-tuple-element.80.refs_0_), channel_id=1, source_target_pairs={{0,16},{8,24},{16,0},{24,8},{1,17},{9,25},{17,1},{25,9},{2,18},{10... | collective-permute-start | bytes 983048 | tf_op jit(solution)/shard_map/ppermute | solution.py:27
  26.9 0.5 collective-permute-start.12
  27.4 2.8 %collective-permute-done.13.refs_0_.refs_7_ = f32[64,1024]{1,0:T(8,128)S(1)} collective-permute-done((f32[64,1024]{1,0:T(8,128)S(1)}, f32[64,1024]{1,0:T(8,128)S(1)}, u32[]{:S(2)}, u32[]{:S(2)}) %collective-permute-start.13) | collective-permute-done | bytes 262176 | tf_op jit(solution)/shard_map/ppermute | solution.py:69
  30.2 1.4 %collective-permute-done.14.refs_2_.refs_9_ = f32[64,1024]{1,0:T(8,128)S(1)} collective-permute-done((f32[64,1024]{1,0:T(8,128)S(1)}, f32[64,1024]{1,0:T(8,128)S(1)}, u32[]{:S(2)}, u32[]{:S(2)}) %collective-permute-start.14) | collective-permute-done | bytes 262176 | tf_op jit(solution)/shard_map/ppermute | solution.py:69
  32.0 1.9 %collective-permute-start.16 = (f32[32,1024]{1,0:T(8,128)S(1)}, f32[32,1024]{1,0:T(8,128)S(1)}, u32[]{:S(2)}, u32[]{:S(2)}) collective-permute-start(f32[32,1024]{1,0:T(8,128)S(1)} %slice.37), channel_id=1, source_target_pairs={{0,1},{2,0},{4,2},{6,4},{7,6},{5,7},{3,5},{1,3},{8,9},{10,8},{12,1... | collective-permute-start | bytes 393224 | tf_op jit(solution)/shard_map/ppermute | solution.py:69
  34.0 0.9 collective-permute-done.10.refs_2_
  34.8 1.8 %collective-permute-done.15.refs_1_ = f32[32,1024]{1,0:T(8,128)S(1)} collective-permute-done((f32[32,1024]{1,0:T(8,128)S(1)}, f32[32,1024]{1,0:T(8,128)S(1)}, u32[]{:S(2)}, u32[]{:S(2)}) %collective-permute-start.15) | collective-permute-done | bytes 131104 | tf_op jit(solution)/shard_map/ppermute | solution.py:69
  36.6 1.1 %late_back.1.refs_4_ = f32[96,512]{1,0:T(8,128)S(1)} custom-call(bf16[512,1024]{1,0:T(8,128)(2,1)S(1)} %get-tuple-element.83.cotan_high, bf16[512,1024]{1,0:T(8,128)(2,1)S(1)} %get-tuple-element.84.cotan_low, f32[64,1024]{1,0:T(8,128)S(1)} %collective-permute-done.13.refs_0_.refs_7_, f32[32,1024]{1,0:T(8,128)S(1)} %collective-permute-done.15.refs_1_, ...), custom_call_target="tpu_custom_call" | custom-call | flops 301989888 | bytes 2949120 | tf_op jit(solution)/shard_map/late_back/pallas_call | solution.py:392
  37.7 1.6 %collective-permute-start.18 = (f32[96,512]{1,0:T(8,128)S(1)}, f32[96,512]{1,0:T(8,128)S(1)}, u32[]{:S(2)}, u32[]{:S(2)}) collective-permute-start(f32[96,512]{1,0:T(8,128)S(1)} %late_back.1.refs_4_), channel_id=1, source_target_pairs={{0,16},{8,24},{16,0},{24,8},{1,17},{9,25},{17,1},{25,9},{2,18},{10... | collective-permute-start | bytes 589832 | tf_op jit(solution)/shard_map/ppermute | solution.py:27
  39.3 2.6 %mid.1 = (f32[1024,256]{1,0:T(8,128)S(1)}, bf16[256,1024]{1,0:T(8,128)(2,1)S(1)}, bf16[256,1024]{1,0:T(8,128)(2,1)S(1)}, bf16[512,1024]{1,0:T(8,128)(2,1)S(1)}, bf16[512,1024]{1,0:T(8,128)(2,1)S(1)}) custom-call(s32[1,1024]{1,0:T(1,128)S(1)} %bitcast.9, f32[256,256]{1,0:T(8,128)S(1)} %get-tuple-element.89.refs_0_.refs_8_, ...), custom_call_target="tpu_custom_call" | custom-call | flops 1879048192 | bytes 7081984 | tf_op jit(solution)/shard_map/mid/pallas_call | solution.py:392
  41.9 0.6 collective-permute-start.19
  42.5 1.0 %collective-permute-done.18.refs_6_ = f32[96,512]{1,0:T(8,128)S(1)} collective-permute-done((f32[96,512]{1,0:T(8,128)S(1)}, f32[96,512]{1,0:T(8,128)S(1)}, u32[]{:S(2)}, u32[]{:S(2)}) %collective-permute-start.18) | collective-permute-done | bytes 196640 | tf_op jit(solution)/shard_map/ppermute | solution.py:27
  43.5 1.3 %rest.1 = f32[1024,256]{1,0:T(8,128)S(1)} custom-call(s32[1,1024]{1,0:T(1,128)S(1)} %bitcast.10, bf16[512,1024]{1,0:T(8,128)(2,1)S(1)} %get-tuple-element.97.mid_high, bf16[512,1024]{1,0:T(8,128)(2,1)S(1)} %get-tuple-element.98.mid_low), custom_call_target="tpu_custom_call" | custom-call | flops 53687091200 | bytes 3149824 | tf_op jit(solution)/shard_map/rest/pallas_call | solution.py:392
  45.9 1.2 %collective-permute-start.23 = (f32[512,256]{1,0:T(8,128)S(1)}, f32[512,256]{1,0:T(8,128)S(1)}, u32[]{:S(2)}, u32[]{:S(2)}) collective-permute-start(f32[512,256]{1,0:T(8,128)S(1)} %get-tuple-element.108), channel_id=1, source_target_pairs={{0,16},{8,24},{16,0},{24,8},{1,17},{9,25},{17,1},{25,9},{2,18},{10... | collective-permute-start | bytes 1572872 | tf_op jit(solution)/shard_map/ppermute | solution.py:27
  47.3 3.8 %grad_first.1 = (f32[32,1024]{1,0:T(8,128)S(1)}, f32[32,1024]{1,0:T(8,128)S(1)}, f32[32,1024]{1,0:T(8,128)S(1)}, f32[32,1024]{1,0:T(8,128)S(1)}, f32[32,1024]{1,...) custom-call(s32[1,1024]{1,0:T(1,128)S(1)} %bitcast.11, ...), custom_call_target="tpu_custom_call" | custom-call | flops 2952790016 | bytes 6295552 | tf_op jit(solution)/shard_map/grad_first/pallas_call | solution.py:392
  51.1 1.1 %grad_stem.1 = (f32[512,128]{1,0:T(8,128)S(1)}, f32[512,128]{1,0:T(8,128)S(1)}) custom-call(bf16[256,1024]{1,0:T(8,128)(2,1)S(1)} %get-tuple-element.94.branch_high, bf16[256,1024]{1,0:T(8,128)(2,1)S(1)} %get-tuple-element.95.branch_low, bf16[1024,512]{1,0:T(8,128)(2,1)S(1)} %get-tuple-element.102.turned_high, ...), custom_call_target="tpu_custom_call" | custom-call | flops 805306368 | bytes 3670016 | tf_op jit(solution)/shard_map/grad_stem/pallas_call | solution.py:392
  52.2 7.8 %collective-permute-done.23.far_ref = f32[512,256]{1,0:T(8,128)S(1)} collective-permute-done((f32[512,256]{1,0:T(8,128)S(1)}, f32[512,256]{1,0:T(8,128)S(1)}, u32[]{:S(2)}, u32[]{:S(2)}) %collective-permute-start.23) | collective-permute-done | bytes 524320 | tf_op jit(solution)/shard_map/ppermute | solution.py:27
  59.9 1.1 %grad_second.1 = (f32[64,1024]{1,0:T(8,128)S(1)}, f32[64,1024]{1,0:T(8,128)S(1)}, f32[64,1024]{1,0:T(8,128)S(1)}, f32[64,1024]{1,0:T(8,128)S(1)}, f32[64,1024]{1...) custom-call(f32[512,256]{1,0:T(8,128)S(1)} %get-tuple-element.107.near_ref, ...), custom_call_target="tpu_custom_call" | custom-call | flops 805306368 | bytes 6291456 | tf_op jit(solution)/shard_map/grad_second/pallas_call | solution.py:392
  61.1 0.6 collective-permute-start.24
  61.7 1.5 %collective-permute-start.25 = (f32[32,1024]{1,0:T(8,128)S(1)}, f32[32,1024]{1,0:T(8,128)S(1)}, u32[]{:S(2)}, u32[]{:S(2)}) collective-permute-start(f32[32,1024]{1,0:T(8,128)S(1)} %get-tuple-element.143), channel_id=1, source_target_pairs={{0,1},{2,0},{4,2},{6,4},{7,6},{5,7},{3,5},{1,3},{8,9},{10,8},{12,1... | collective-permute-start | bytes 393224 | tf_op jit(solution)/shard_map/ppermute | solution.py:69
  63.2 2.9 %collective-permute-done.24 = f32[32,1024]{1,0:T(8,128)S(1)} collective-permute-done((f32[32,1024]{1,0:T(8,128)S(1)}, f32[32,1024]{1,0:T(8,128)S(1)}, u32[]{:S(2)}, u32[]{:S(2)}) %collective-permute-start.24) | collective-permute-done | bytes 131104 | tf_op jit(solution)/shard_map/ppermute | solution.py:69
  66.7 1.6 %collective-permute-start.26 = (f32[64,1024]{1,0:T(8,128)S(1)}, f32[64,1024]{1,0:T(8,128)S(1)}, u32[]{:S(2)}, u32[]{:S(2)}) collective-permute-start(f32[64,1024]{1,0:T(8,128)S(1)} %get-tuple-element.124), channel_id=1, source_target_pairs={{0,2},{2,4},{4,6},{6,7},{7,5},{5,3},{3,1},{1,0},{8,10},{10,12},{12... | collective-permute-start | bytes 786440 | tf_op jit(solution)/shard_map/ppermute | solution.py:69
  68.8 1.5 %collective-permute-start.31 = (f32[512,128]{1,0:T(8,128)S(1)}, f32[512,128]{1,0:T(8,128)S(1)}, u32[]{:S(2)}, u32[]{:S(2)}) collective-permute-start(f32[512,128]{1,0:T(8,128)S(1)} %get-tuple-element.129), channel_id=1, source_target_pairs={{0,16},{8,24},{16,0},{24,8},{1,17},{9,25},{17,1},{25,9},{2,18},{10... | collective-permute-start | bytes 786440 | tf_op jit(solution)/shard_map/ppermute | solution.py:27
  70.3 3.3 %collective-permute-done.26 = f32[64,1024]{1,0:T(8,128)S(1)} collective-permute-done((f32[64,1024]{1,0:T(8,128)S(1)}, f32[64,1024]{1,0:T(8,128)S(1)}, u32[]{:S(2)}, u32[]{:S(2)}) %collective-permute-start.26) | collective-permute-done | bytes 262176 | tf_op jit(solution)/shard_map/ppermute | solution.py:69
  73.7 1.4 %collective-permute-start.27 = (f32[64,1024]{1,0:T(8,128)S(1)}, f32[64,1024]{1,0:T(8,128)S(1)}, u32[]{:S(2)}, u32[]{:S(2)}) collective-permute-start(f32[64,1024]{1,0:T(8,128)S(1)} %add.30), channel_id=1, source_target_pairs={{0,2},{2,4},{4,6},{6,7},{7,5},{5,3},{3,1},{1,0},{8,10},{10,12},{12... | collective-permute-start | bytes 786440 | tf_op jit(solution)/shard_map/ppermute | solution.py:69
  75.1 0.7 collective-permute-start.29
  75.8 0.5 collective-permute-start.32
  76.3 3.7 %collective-permute-done.27 = f32[64,1024]{1,0:T(8,128)S(1)} collective-permute-done((f32[64,1024]{1,0:T(8,128)S(1)}, f32[64,1024]{1,0:T(8,128)S(1)}, u32[]{:S(2)}, u32[]{:S(2)}) %collective-permute-start.27) | collective-permute-done | bytes 262176 | tf_op jit(solution)/shard_map/ppermute | solution.py:69
  80.1 2.5 %collective-permute-done.29 = f32[64,1024]{1,0:T(8,128)S(1)} collective-permute-done((f32[64,1024]{1,0:T(8,128)S(1)}, f32[64,1024]{1,0:T(8,128)S(1)}, u32[]{:S(2)}, u32[]{:S(2)}) %collective-permute-start.29) | collective-permute-done | bytes 262176 | tf_op jit(solution)/shard_map/ppermute | solution.py:69
  82.7 2.0 %collective-permute-start.33 = (f32[64,1024]{1,0:T(8,128)S(1)}, f32[64,1024]{1,0:T(8,128)S(1)}, u32[]{:S(2)}, u32[]{:S(2)}) collective-permute-start(f32[64,1024]{1,0:T(8,128)S(1)} %add.31), channel_id=1, source_target_pairs={{0,2},{2,4},{4,6},{6,7},{7,5},{5,3},{3,1},{1,0},{8,10},{10,12},{12... | collective-permute-start | bytes 786440 | tf_op jit(solution)/shard_map/ppermute | solution.py:69
  84.7 2.4 %place.1 = f32[128,1024]{1,0:T(8,128)} custom-call(s32[1,1024]{1,0:T(1,128)S(1)} %bitcast.13, f32[512,128]{1,0:T(8,128)S(1)} %get-tuple-element.130.refs_0_, f32[512,128]{1,0:T(8,128)S(1)} %collective-permute-done.30.refs_1_, f32[512,128]{1,0:T(8,128)S(1)} %collective-permute-done.31.refs_2_, f32[512,128]{1,0:T(8,128)S(1)} %collective-permute-done.32.refs_3_), custom_call_target="tpu_custom_call" | custom-call | flops 536870912 | bytes 1576960 | tf_op jit(solution)/shard_map/place/pallas_call | solution.py:392
  87.1 2.0 %collective-permute-done.34 = f32[64,1024]{1,0:T(8,128)S(1)} collective-permute-done((f32[64,1024]{1,0:T(8,128)S(1)}, f32[64,1024]{1,0:T(8,128)S(1)}, u32[]{:S(2)}, u32[]{:S(2)}) %collective-permute-start.34) | collective-permute-done | bytes 262176 | tf_op jit(solution)/shard_map/ppermute | solution.py:69
  89.2 0.7 fusion.1
  (58 shorter events, 4.7 us)
Async XLA Ops:
  0.6 7.1 %copy-start.5 = (s32[1024]{0:T(1024)S(1)}, s32[1024]{0:T(1024)}, u32[]{:S(2)}) copy-start(s32[1024]{0:T(1024)} %param.10) | copy-start | bytes 12292
  0.6 20.8 %collective-permute-start.7 = (f32[128,1024]{1,0:T(8,128)}, f32[128,1024]{1,0:T(8,128)S(1)}, u32[]{:S(2)}, u32[]{:S(2)}) collective-permute-start(f32[128,1024]{1,0:T(8,128)} %bitcast.5), channel_id=1, source_target_pairs={{0,16},{8,24},{16,0},{24,8},{1,17},{9,25},{17,1},{25,9},{2,18},{10... | collective-permute-start | bytes 1572872 | tf_op jit(solution)/shard_map/ppermute | solution.py:27
  3.6 6.5 %collective-permute-start.1 = (f32[32,1024]{1,0:T(8,128)}, f32[32,1024]{1,0:T(8,128)S(1)}, u32[]{:S(2)}, u32[]{:S(2)}) collective-permute-start(f32[32,1024]{1,0:T(8,128)} %refs_4_.3), channel_id=1, source_target_pairs={{0,1},{2,0},{4,2},{6,4},{7,6},{5,7},{3,5},{1,3},{8,9},{10,8},{12,1... | collective-permute-start | bytes 393224 | tf_op jit(solution)/shard_map/ppermute | solution.py:69
  5.2 6.4 %collective-permute-start.2 = (f32[32,1024]{1,0:T(8,128)}, f32[32,1024]{1,0:T(8,128)S(1)}, u32[]{:S(2)}, u32[]{:S(2)}) collective-permute-start(f32[32,1024]{1,0:T(8,128)} %refs_4_.3), channel_id=1, source_target_pairs={{0,2},{2,4},{4,6},{6,7},{7,5},{5,3},{3,1},{1,0},{8,10},{10,12},{12... | collective-permute-start | bytes 393224 | tf_op jit(solution)/shard_map/ppermute | solution.py:69
  5.7 6.0 %collective-permute-start.3 = (f32[32,1024]{1,0:T(8,128)}, f32[32,1024]{1,0:T(8,128)S(1)}, u32[]{:S(2)}, u32[]{:S(2)}) collective-permute-start(f32[32,1024]{1,0:T(8,128)} %refs_4_.2), channel_id=1, source_target_pairs={{0,1},{2,0},{4,2},{6,4},{7,6},{5,7},{3,5},{1,3},{8,9},{10,8},{12,1... | collective-permute-start | bytes 393224 | tf_op jit(solution)/shard_map/ppermute | solution.py:69
  7.2 5.7 %collective-permute-start.4 = (f32[32,1024]{1,0:T(8,128)}, f32[32,1024]{1,0:T(8,128)S(1)}, u32[]{:S(2)}, u32[]{:S(2)}) collective-permute-start(f32[32,1024]{1,0:T(8,128)} %refs_4_.2), channel_id=1, source_target_pairs={{0,2},{2,4},{4,6},{6,7},{7,5},{5,3},{3,1},{1,0},{8,10},{10,12},{12... | collective-permute-start | bytes 393224 | tf_op jit(solution)/shard_map/ppermute | solution.py:69
  7.7 1.0 %copy-start.2 = (f32[1,128,1024]{2,1,0:T(8,128)S(1)}, f32[1,128,1024]{2,1,0:T(8,128)}, u32[]{:S(2)}) copy-start(f32[1,128,1024]{2,1,0:T(8,128)} %param.6) | copy-start | bytes 1572868
  8.7 14.7 %copy-start.1 = (f32[32,1024]{1,0:T(8,128)S(1)}, f32[32,1024]{1,0:T(8,128)}, u32[]{:S(2)}) copy-start(f32[32,1024]{1,0:T(8,128)} %refs_4_.2) | copy-start | bytes 393220
  9.8 5.8 %copy-start = (f32[1,128,1024]{2,1,0:T(8,128)S(1)}, f32[1,128,1024]{2,1,0:T(8,128)}, u32[]{:S(2)}) copy-start(f32[1,128,1024]{2,1,0:T(8,128)} %param.7) | copy-start | bytes 1572868
  13.0 6.7 %collective-permute-start.5 = (f32[64,1024]{1,0:T(8,128)S(1)}, f32[64,1024]{1,0:T(8,128)S(1)}, u32[]{:S(2)}, u32[]{:S(2)}) collective-permute-start(f32[64,1024]{1,0:T(8,128)S(1)} %get-tuple-element.74.refs_5_), channel_id=1, source_target_pairs={{0,1},{2,0},{4,2},{6,4},{7,6},{5,7},{3,5},{1,3},{8,9},{10,8},{12,1... | collective-permute-start | bytes 786440 | tf_op jit(solution)/shard_map/ppermute | solution.py:69
  14.6 6.4 %collective-permute-start.6 = (f32[64,1024]{1,0:T(8,128)S(1)}, f32[64,1024]{1,0:T(8,128)S(1)}, u32[]{:S(2)}, u32[]{:S(2)}) collective-permute-start(f32[64,1024]{1,0:T(8,128)S(1)} %get-tuple-element.75.refs_8_.refs_11_), channel_id=1, source_target_pairs={{0,2},{2,4},{4,6},{6,7},{7,5},{5,3},{3,1},{1,0},{8,10},{10,12},{12... | collective-permute-start | bytes 786440 | tf_op jit(solution)/shard_map/ppermute | solution.py:69
  15.0 6.4 %collective-permute-start.8 = (f32[256,256]{1,0:T(8,128)S(1)}, f32[256,256]{1,0:T(8,128)S(1)}, u32[]{:S(2)}, u32[]{:S(2)}) collective-permute-start(f32[256,256]{1,0:T(8,128)S(1)} %get-tuple-element.77), channel_id=1, source_target_pairs={{0,16},{8,24},{16,0},{24,8},{1,17},{9,25},{17,1},{25,9},{2,18},{10... | collective-permute-start | bytes 786440 | tf_op jit(solution)/shard_map/ppermute | solution.py:27
  15.6 7.9 %collective-permute-start = (f32[128,1024]{1,0:T(8,128)S(1)}, f32[128,1024]{1,0:T(8,128)S(1)}, u32[]{:S(2)}, u32[]{:S(2)}) collective-permute-start(f32[128,1024]{1,0:T(8,128)S(1)} %bitcast.6), channel_id=1, source_target_pairs={{0,8},{8,0},{16,24},{24,16},{1,9},{9,1},{17,25},{25,17},{2,10},{10... | collective-permute-start | bytes 1572872 | tf_op jit(solution)/shard_map/ppermute | solution.py:27
  21.4 2.0 %collective-permute-start.9 = (f32[128,1024]{1,0:T(8,128)S(1)}, f32[128,1024]{1,0:T(8,128)S(1)}, u32[]{:S(2)}, u32[]{:S(2)}) collective-permute-start(f32[128,1024]{1,0:T(8,128)S(1)} %collective-permute-done.7.refs_2_), channel_id=1, source_target_pairs={{0,8},{8,0},{16,24},{24,16},{1,9},{9,1},{17,25},{25,17},{2,10},{10... | collective-permute-start | bytes 1572872 | tf_op jit(solution)/shard_map/ppermute | solution.py:27
  21.4 8.8 %collective-permute-start.13 = (f32[64,1024]{1,0:T(8,128)S(1)}, f32[64,1024]{1,0:T(8,128)S(1)}, u32[]{:S(2)}, u32[]{:S(2)}) collective-permute-start(f32[64,1024]{1,0:T(8,128)S(1)} %collective-permute-done.5.refs_6_), channel_id=1, source_target_pairs={{0,1},{2,0},{4,2},{6,4},{7,6},{5,7},{3,5},{1,3},{8,9},{10,8},{12,1... | collective-permute-start | bytes 786440 | tf_op jit(solution)/shard_map/ppermute | solution.py:69
  23.2 8.4 %collective-permute-start.14 = (f32[64,1024]{1,0:T(8,128)S(1)}, f32[64,1024]{1,0:T(8,128)S(1)}, u32[]{:S(2)}, u32[]{:S(2)}) collective-permute-start(f32[64,1024]{1,0:T(8,128)S(1)} %collective-permute-done.6.refs_7_.refs_10_), channel_id=1, source_target_pairs={{0,2},{2,4},{4,6},{6,7},{7,5},{5,3},{3,1},{1,0},{8,10},{10,12},{12... | collective-permute-start | bytes 786440 | tf_op jit(solution)/shard_map/ppermute | solution.py:69
  25.1 9.7 %collective-permute-start.10 = (f32[160,512]{1,0:T(8,128)S(1)}, f32[160,512]{1,0:T(8,128)S(1)}, u32[]{:S(2)}, u32[]{:S(2)}) collective-permute-start(f32[160,512]{1,0:T(8,128)S(1)} %get-tuple-element.80.refs_0_), channel_id=1, source_target_pairs={{0,16},{8,24},{16,0},{24,8},{1,17},{9,25},{17,1},{25,9},{2,18},{10... | collective-permute-start | bytes 983048 | tf_op jit(solution)/shard_map/ppermute | solution.py:27
  26.9 7.0 %collective-permute-start.11 = (f32[256,256]{1,0:T(8,128)S(1)}, f32[256,256]{1,0:T(8,128)S(1)}, u32[]{:S(2)}, u32[]{:S(2)}) collective-permute-start(f32[256,256]{1,0:T(8,128)S(1)} %get-tuple-element.89.refs_0_.refs_8_), channel_id=1, source_target_pairs={{0,8},{8,0},{16,24},{24,16},{1,9},{9,1},{17,25},{25,17},{2,10},{10... | collective-permute-start | bytes 786440 | tf_op jit(solution)/shard_map/ppermute | solution.py:27
  26.9 7.0 %collective-permute-start.12 = (f32[256,256]{1,0:T(8,128)S(1)}, f32[256,256]{1,0:T(8,128)S(1)}, u32[]{:S(2)}, u32[]{:S(2)}) collective-permute-start(f32[256,256]{1,0:T(8,128)S(1)} %collective-permute-done.8.refs_2_.refs_10_), channel_id=1, source_target_pairs={{0,8},{8,0},{16,24},{24,16},{1,9},{9,1},{17,25},{25,17},{2,10},{10... | collective-permute-start | bytes 786440 | tf_op jit(solution)/shard_map/ppermute | solution.py:27
  31.6 5.0 %collective-permute-start.15 = (f32[32,1024]{1,0:T(8,128)S(1)}, f32[32,1024]{1,0:T(8,128)S(1)}, u32[]{:S(2)}, u32[]{:S(2)}) collective-permute-start(f32[32,1024]{1,0:T(8,128)S(1)} %slice.36), channel_id=1, source_target_pairs={{0,2},{2,4},{4,6},{6,7},{7,5},{5,3},{3,1},{1,0},{8,10},{10,12},{12... | collective-permute-start | bytes 393224 | tf_op jit(solution)/shard_map/ppermute | solution.py:69
  32.0 7.3 %collective-permute-start.16 = (f32[32,1024]{1,0:T(8,128)S(1)}, f32[32,1024]{1,0:T(8,128)S(1)}, u32[]{:S(2)}, u32[]{:S(2)}) collective-permute-start(f32[32,1024]{1,0:T(8,128)S(1)} %slice.37), channel_id=1, source_target_pairs={{0,1},{2,0},{4,2},{6,4},{7,6},{5,7},{3,5},{1,3},{8,9},{10,8},{12,1... | collective-permute-start | bytes 393224 | tf_op jit(solution)/shard_map/ppermute | solution.py:69
  36.6 2.7 %copy-start.3 = (f32[32,1024]{1,0:T(8,128)S(1)}, f32[32,1024]{1,0:T(8,128)}, u32[]{:S(2)}) copy-start(f32[32,1024]{1,0:T(8,128)} %refs_4_.3) | copy-start | bytes 393220
  36.6 2.7 %copy-start.4 = (s32[1024]{0:T(1024)S(1)}, s32[1024]{0:T(1024)}, u32[]{:S(2)}) copy-start(s32[1024]{0:T(1024)} %param.11) | copy-start | bytes 12292
  37.7 5.7 %collective-permute-start.18 = (f32[96,512]{1,0:T(8,128)S(1)}, f32[96,512]{1,0:T(8,128)S(1)}, u32[]{:S(2)}, u32[]{:S(2)}) collective-permute-start(f32[96,512]{1,0:T(8,128)S(1)} %late_back.1.refs_4_), channel_id=1, source_target_pairs={{0,16},{8,24},{16,0},{24,8},{1,17},{9,25},{17,1},{25,9},{2,18},{10... | collective-permute-start | bytes 589832 | tf_op jit(solution)/shard_map/ppermute | solution.py:27
  39.3 7.9 %collective-permute-start.17 = (f32[160,512]{1,0:T(8,128)S(1)}, f32[160,512]{1,0:T(8,128)S(1)}, u32[]{:S(2)}, u32[]{:S(2)}) collective-permute-start(f32[160,512]{1,0:T(8,128)S(1)} %get-tuple-element.80.refs_0_), channel_id=1, source_target_pairs={{0,8},{8,0},{16,24},{24,16},{1,9},{9,1},{17,25},{25,17},{2,10},{10... | collective-permute-start | bytes 983048 | tf_op jit(solution)/shard_map/ppermute | solution.py:27
  41.9 2.9 %collective-permute-start.19 = (f32[1024,256]{1,0:T(8,128)S(1)}, f32[1024,256]{1,0:T(8,128)S(1)}, u32[]{:S(2)}, u32[]{:S(2)}) collective-permute-start(f32[1024,256]{1,0:T(8,128)S(1)} %get-tuple-element.99), channel_id=1, source_target_pairs={{0,8},{8,0},{16,24},{24,16},{1,9},{9,1},{17,25},{25,17},{2,10},{10... | collective-permute-start | bytes 3145736 | tf_op jit(solution)/shard_map/ppermute | solution.py:27
  45.0 2.3 %collective-permute-start.20 = (f32[160,512]{1,0:T(8,128)S(1)}, f32[160,512]{1,0:T(8,128)S(1)}, u32[]{:S(2)}, u32[]{:S(2)}) collective-permute-start(f32[160,512]{1,0:T(8,128)S(1)} %collective-permute-done.10.refs_2_), channel_id=1, source_target_pairs={{0,8},{8,0},{16,24},{24,16},{1,9},{9,1},{17,25},{25,17},{2,10},{10... | collective-permute-start | bytes 983048 | tf_op jit(solution)/shard_map/ppermute | solution.py:27
  45.4 1.8 %collective-permute-start.21 = (f32[96,512]{1,0:T(8,128)S(1)}, f32[96,512]{1,0:T(8,128)S(1)}, u32[]{:S(2)}, u32[]{:S(2)}) collective-permute-start(f32[96,512]{1,0:T(8,128)S(1)} %late_back.1.refs_4_), channel_id=1, source_target_pairs={{0,8},{8,0},{16,24},{24,16},{1,9},{9,1},{17,25},{25,17},{2,10},{10... | collective-permute-start | bytes 589832 | tf_op jit(solution)/shard_map/ppermute | solution.py:27
  45.6 1.7 %collective-permute-start.22 = (f32[96,512]{1,0:T(8,128)S(1)}, f32[96,512]{1,0:T(8,128)S(1)}, u32[]{:S(2)}, u32[]{:S(2)}) collective-permute-start(f32[96,512]{1,0:T(8,128)S(1)} %collective-permute-done.18.refs_6_), channel_id=1, source_target_pairs={{0,8},{8,0},{16,24},{24,16},{1,9},{9,1},{17,25},{25,17},{2,10},{10... | collective-permute-start | bytes 589832 | tf_op jit(solution)/shard_map/ppermute | solution.py:27
  45.9 14.0 %collective-permute-start.23 = (f32[512,256]{1,0:T(8,128)S(1)}, f32[512,256]{1,0:T(8,128)S(1)}, u32[]{:S(2)}, u32[]{:S(2)}) collective-permute-start(f32[512,256]{1,0:T(8,128)S(1)} %get-tuple-element.108), channel_id=1, source_target_pairs={{0,16},{8,24},{16,0},{24,8},{1,17},{9,25},{17,1},{25,9},{2,18},{10... | collective-permute-start | bytes 1572872 | tf_op jit(solution)/shard_map/ppermute | solution.py:27
  61.1 5.0 %collective-permute-start.24 = (f32[32,1024]{1,0:T(8,128)S(1)}, f32[32,1024]{1,0:T(8,128)S(1)}, u32[]{:S(2)}, u32[]{:S(2)}) collective-permute-start(f32[32,1024]{1,0:T(8,128)S(1)} %get-tuple-element.144), channel_id=1, source_target_pairs={{0,2},{2,4},{4,6},{6,7},{7,5},{5,3},{3,1},{1,0},{8,10},{10,12},{12... | collective-permute-start | bytes 393224 | tf_op jit(solution)/shard_map/ppermute | solution.py:69
  61.7 5.0 %collective-permute-start.25 = (f32[32,1024]{1,0:T(8,128)S(1)}, f32[32,1024]{1,0:T(8,128)S(1)}, u32[]{:S(2)}, u32[]{:S(2)}) collective-permute-start(f32[32,1024]{1,0:T(8,128)S(1)} %get-tuple-element.143), channel_id=1, source_target_pairs={{0,1},{2,0},{4,2},{6,4},{7,6},{5,7},{3,5},{1,3},{8,9},{10,8},{12,1... | collective-permute-start | bytes 393224 | tf_op jit(solution)/shard_map/ppermute | solution.py:69
  66.7 6.9 %collective-permute-start.26 = (f32[64,1024]{1,0:T(8,128)S(1)}, f32[64,1024]{1,0:T(8,128)S(1)}, u32[]{:S(2)}, u32[]{:S(2)}) collective-permute-start(f32[64,1024]{1,0:T(8,128)S(1)} %get-tuple-element.124), channel_id=1, source_target_pairs={{0,2},{2,4},{4,6},{6,7},{7,5},{5,3},{3,1},{1,0},{8,10},{10,12},{12... | collective-permute-start | bytes 786440 | tf_op jit(solution)/shard_map/ppermute | solution.py:69
  68.3 6.8 %collective-permute-start.28 = (f32[64,1024]{1,0:T(8,128)S(1)}, f32[64,1024]{1,0:T(8,128)S(1)}, u32[]{:S(2)}, u32[]{:S(2)}) collective-permute-start(f32[64,1024]{1,0:T(8,128)S(1)} %get-tuple-element.127), channel_id=1, source_target_pairs={{0,1},{2,0},{4,2},{6,4},{7,6},{5,7},{3,5},{1,3},{8,9},{10,8},{12,1... | collective-permute-start | bytes 786440 | tf_op jit(solution)/shard_map/ppermute | solution.py:69
  68.8 7.0 %collective-permute-start.31 = (f32[512,128]{1,0:T(8,128)S(1)}, f32[512,128]{1,0:T(8,128)S(1)}, u32[]{:S(2)}, u32[]{:S(2)}) collective-permute-start(f32[512,128]{1,0:T(8,128)S(1)} %get-tuple-element.129), channel_id=1, source_target_pairs={{0,16},{8,24},{16,0},{24,8},{1,17},{9,25},{17,1},{25,9},{2,18},{10... | collective-permute-start | bytes 786440 | tf_op jit(solution)/shard_map/ppermute | solution.py:27
  73.7 6.4 %collective-permute-start.27 = (f32[64,1024]{1,0:T(8,128)S(1)}, f32[64,1024]{1,0:T(8,128)S(1)}, u32[]{:S(2)}, u32[]{:S(2)}) collective-permute-start(f32[64,1024]{1,0:T(8,128)S(1)} %add.30), channel_id=1, source_target_pairs={{0,2},{2,4},{4,6},{6,7},{7,5},{5,3},{3,1},{1,0},{8,10},{10,12},{12... | collective-permute-start | bytes 786440 | tf_op jit(solution)/shard_map/ppermute | solution.py:69
  75.1 7.5 %collective-permute-start.29 = (f32[64,1024]{1,0:T(8,128)S(1)}, f32[64,1024]{1,0:T(8,128)S(1)}, u32[]{:S(2)}, u32[]{:S(2)}) collective-permute-start(f32[64,1024]{1,0:T(8,128)S(1)} %add.32), channel_id=1, source_target_pairs={{0,1},{2,0},{4,2},{6,4},{7,6},{5,7},{3,5},{1,3},{8,9},{10,8},{12,1... | collective-permute-start | bytes 786440 | tf_op jit(solution)/shard_map/ppermute | solution.py:69
  75.8 6.8 %collective-permute-start.30 = (f32[512,128]{1,0:T(8,128)S(1)}, f32[512,128]{1,0:T(8,128)S(1)}, u32[]{:S(2)}, u32[]{:S(2)}) collective-permute-start(f32[512,128]{1,0:T(8,128)S(1)} %get-tuple-element.130.refs_0_), channel_id=1, source_target_pairs={{0,8},{8,0},{16,24},{24,16},{1,9},{9,1},{17,25},{25,17},{2,10},{10... | collective-permute-start | bytes 786440 | tf_op jit(solution)/shard_map/ppermute | solution.py:27
  75.8 6.8 %collective-permute-start.32 = (f32[512,128]{1,0:T(8,128)S(1)}, f32[512,128]{1,0:T(8,128)S(1)}, u32[]{:S(2)}, u32[]{:S(2)}) collective-permute-start(f32[512,128]{1,0:T(8,128)S(1)} %collective-permute-done.31.refs_2_), channel_id=1, source_target_pairs={{0,8},{8,0},{16,24},{24,16},{1,9},{9,1},{17,25},{25,17},{2,10},{10... | collective-permute-start | bytes 786440 | tf_op jit(solution)/shard_map/ppermute | solution.py:27
  82.6 6.4 %collective-permute-start.34 = (f32[64,1024]{1,0:T(8,128)S(1)}, f32[64,1024]{1,0:T(8,128)S(1)}, u32[]{:S(2)}, u32[]{:S(2)}) collective-permute-start(f32[64,1024]{1,0:T(8,128)S(1)} %add.33), channel_id=1, source_target_pairs={{0,1},{2,0},{4,2},{6,4},{7,6},{5,7},{3,5},{1,3},{8,9},{10,8},{12,1... | collective-permute-start | bytes 786440 | tf_op jit(solution)/shard_map/ppermute | solution.py:69
  82.7 6.4 %collective-permute-start.33 = (f32[64,1024]{1,0:T(8,128)S(1)}, f32[64,1024]{1,0:T(8,128)S(1)}, u32[]{:S(2)}, u32[]{:S(2)}) collective-permute-start(f32[64,1024]{1,0:T(8,128)S(1)} %add.31), channel_id=1, source_target_pairs={{0,2},{2,4},{4,6},{6,7},{7,5},{5,3},{3,1},{1,0},{8,10},{10,12},{12... | collective-permute-start | bytes 786440 | tf_op jit(solution)/shard_map/ppermute | solution.py:69

commit v5 on v4

--- a/solution.py
+++ b/solution.py
@@ -279,13 +279,9 @@
             store_split(*mid, (slice(h * height, (h + 1) * height), columns), value)
 
 
-def put_picks(bond_ref, mid, out_ref, side):
-    rows, width = mid[0].shape
-    low = out_ref.shape[1]
-    for part in range(2):
-        select = chosen(bond_ref, 2 * part + side, low, width)
-        block = dot(mid[0][...], select, ((1,), (0,))) + dot(mid[1][...], select, ((1,), (0,)))
-        out_ref[part * rows : (part + 1) * rows] = block
+def picks(bond_ref, mid, rel, low):
+    select = chosen(bond_ref, rel, low, mid[0].shape[1])
+    return dot(mid[0][...], select, ((1,), (0,))) + dot(mid[1][...], select, ((1,), (0,)))
 
 
 def mid_kernel(groups, bond_ref, *refs):
@@ -295,11 +291,12 @@
     for k, ref in enumerate(refs[:-5]):
         store_split(*branch, aligned(ring_owner(k), own), branch_rows(ref, own, 0))
     absorb(picked, branch, mid, groups)
-    put_picks(bond_ref, mid, out_ref, 1)
-
-
-def rest_kernel(bond_ref, mid_high, mid_low, out_ref):
-    put_picks(bond_ref, (mid_high, mid_low), out_ref, 0)
+    out_ref[...] = picks(bond_ref, mid, groups - 1, out_ref.shape[1])
+
+
+def rest_kernel(partners, bond_ref, mid_high, mid_low, *out_refs):
+    for rel, out_ref in zip(partners, out_refs, strict=True):
+        out_ref[...] = picks(bond_ref, (mid_high, mid_low), rel, out_ref.shape[1])
 
 
 def gather_rows(pieces, rows, own):
@@ -330,11 +327,11 @@
         out_ref[...] = total_ref[aligned(ring_owner(k), own)]
 
 
-def second_kernel(factor, near_ref, far_ref, cotan_high, cotan_low, *refs):
+def second_kernel(factor, near_ref, beside_ref, far_ref, cotan_high, cotan_low, *refs):
     firsts, refs = refs[: (len(refs) - 1) // 2], refs[(len(refs) - 1) // 2 :]
     out_refs, total_ref = refs[:-1], refs[-1]
     own = firsts[0].shape[0]
-    parts = split(((near_ref[...] + far_ref[...]) * factor).T)
+    parts = split(((near_ref[...] + beside_ref[...] + far_ref[...]) * factor).T)
     total_ref[...] = dot_parts(parts, (cotan_high[...], cotan_low[...]), ((1,), (0,)))
     for k, (ref, out_ref) in enumerate(zip(firsts, out_refs, strict=True)):
         out_ref[:own] = ref[...]
@@ -485,17 +482,24 @@
     across, first_high, first_low, mid_high, mid_low = call(
         functools.partial(mid_kernel, groups),
         "mid",
-        [f32(2 * tall, low)] + [b16(low, width)] * 2 + [b16(tall, width)] * 2,
-        3 * unit + groups * unit,
+        [f32(tall, low)] + [b16(low, width)] * 2 + [b16(tall, width)] * 2,
+        3 * unit + unit,
         [],
         ordered(second_bond, far_back),
         *picked,
         *pieces_first,
     )
-    beside = call(rest_kernel, "rest", [f32(2 * tall, low)], 50 * groups * unit, [], ordered(second_bond, far_far), mid_high, mid_low)[0]
-    mid = beside + swap(across, 1)
-    near_mid, away_mid, near_far = lax.optimization_barrier((mid[:tall], mid[tall:], near_far))
-    regrouped = [near_mid, swap(away_mid, 2)]
+    away_mid = call(
+        functools.partial(rest_kernel, (2,)),
+        "across",
+        [f32(tall, low)],
+        50 * groups * unit,
+        [],
+        ordered(second_bond, far_far),
+        mid_high,
+        mid_low,
+    )[0]
+    away_mid, near_far = lax.optimization_barrier((away_mid + swap(across, 1), near_far))
     gathered = [
         [near_back, swap(near_back, 1), near_far, swap(near_far, 1)],
         [far_back, swap(far_back, 1), far_far, swap(far_far, 1)],
@@ -511,6 +515,17 @@
         *gathered[1],
         *picked,
     )
+    near_mid = call(
+        functools.partial(rest_kernel, (0, 1)),
+        "rest",
+        [f32(tall, low)] * 2,
+        2 * unit,
+        [],
+        ordered(second_bond, outer_first[0]),
+        mid_high,
+        mid_low,
+    )
+    regrouped = [near_mid[0], swap(near_mid[1], 1), swap(away_mid, 2)]
     grad = call(
         functools.partial(stem_kernel, groups),
         "grad_stem",

time: 90.1 us -> 88.8 us (0.986)
  waiting for transfers between devices: 39.7 us -> 38.3 us
    ppermute x17 -> x18, waiting for transfers between devices: 10.2 us -> 9.26 us  [swap(): return lax.ppermute(block, 'gx', [(i, i ^ mask) for i in range(size)])]
    ppermute x17 -> x18, starting transfers between devices: 12.1 us -> 12.3 us  [swap(): return lax.ppermute(block, 'gx', [(i, i ^ mask) for i in range(size)])]
    pallas_call x10 -> x11, Pallas kernels: 16.1 us -> 16.2 us  [call(): pl.pallas_call(kernel, name=name, out_shape=outs, in_specs=[whole] * len(...]
  transfers between devices with their start and end apart: 35 -> 36, of which waited for: 21 -> 21; matrix products, arithmetic and copies ran while one was open for 0% -> 0% of each run, Pallas kernels for 17% -> 17%
where the time goes in v5:
time: 88.8 us; the launch traced here: 88.6 us
  waiting for transfers between devices  38.3 us (43%)
  starting transfers between devices  31.1 us (35%)
  Pallas kernels  16.2 us (18%)
  local copies, waits for them, and re-layouts  1.82 us (2%)
    ppermute x18, waiting for transfers between devices, ring_step(): lax.ppermute(block, 'gy', [(order[k], order[(k + step) % size]) for k in...  29 us
    ppermute x18, starting transfers between devices, ring_step(): lax.ppermute(block, 'gy', [(order[k], order[(k + step) % size]) for k in...  18.8 us
    pallas_call x11, Pallas kernels, call(): pl.pallas_call(kernel, name=name, out_shape=outs, in_specs=[whole] * len(...  16.2 us
    ppermute x18, starting transfers between devices, swap(): return lax.ppermute(block, 'gx', [(i, i ^ mask) for i in range(size)])  12.3 us
    ppermute x18, waiting for transfers between devices, swap(): return lax.ppermute(block, 'gx', [(i, i ^ mask) for i in range(size)])  9.26 us
  transfers between devices with their start and end apart: 36, of which 21 were waited for; matrix products, arithmetic and copies ran while one was open for 0% of the time, Pallas kernels for 17%

profile of v5, /device:TPU:0, one launch (start us, length us, event | category | flops | bytes accessed | tf_op | source)
XLA Modules:
  0.0 88.6 jit_solution(12396914286175949252)
XLA Ops:
  0.6 3.0 %collective-permute-start.7 = (f32[128,1024]{1,0:T(8,128)}, f32[128,1024]{1,0:T(8,128)S(1)}, u32[]{:S(2)}, u32[]{:S(2)}) collective-permute-start(f32[128,1024]{1,0:T(8,128)} %bitcast.5), channel_id=1, source_target_pairs={{0,16},{8,24},{16,0},{24,8},{1,17},{9,25},{17,1},{25,9},{2,18},{10... | collective-permute-start | bytes 1572872 | tf_op jit(solution)/shard_map/ppermute | solution.py:27
  3.6 1.5 %collective-permute-start.1 = (f32[32,1024]{1,0:T(8,128)}, f32[32,1024]{1,0:T(8,128)S(1)}, u32[]{:S(2)}, u32[]{:S(2)}) collective-permute-start(f32[32,1024]{1,0:T(8,128)} %refs_4_.3), channel_id=1, source_target_pairs={{0,1},{2,0},{4,2},{6,4},{7,6},{5,7},{3,5},{1,3},{8,9},{10,8},{12,1... | collective-permute-start | bytes 393224 | tf_op jit(solution)/shard_map/ppermute | solution.py:69
  5.2 0.5 collective-permute-start.2
  5.7 1.5 %collective-permute-start.3 = (f32[32,1024]{1,0:T(8,128)}, f32[32,1024]{1,0:T(8,128)S(1)}, u32[]{:S(2)}, u32[]{:S(2)}) collective-permute-start(f32[32,1024]{1,0:T(8,128)} %refs_4_.2), channel_id=1, source_target_pairs={{0,1},{2,0},{4,2},{6,4},{7,6},{5,7},{3,5},{1,3},{8,9},{10,8},{12,1... | collective-permute-start | bytes 393224 | tf_op jit(solution)/shard_map/ppermute | solution.py:69
  7.2 0.5 collective-permute-start.4
  7.7 1.0 %copy-done.3 = f32[1,128,1024]{2,1,0:T(8,128)S(1)} copy-done((f32[1,128,1024]{2,1,0:T(8,128)S(1)}, f32[1,128,1024]{2,1,0:T(8,128)}, u32[]{:S(2)}) %copy-start.3) | copy-done | bytes 524312
  8.7 1.0 %pick.1 = (f32[256,256]{1,0:T(8,128)S(1)}, f32[256,256]{1,0:T(8,128)S(1)}) custom-call(f32[128,1024]{1,0:T(8,128)S(1)} %bitcast.12, s32[1,1024]{1,0:T(1,128)S(1)} %bitcast.13), custom_call_target="tpu_custom_call" | custom-call | flops 536870912 | bytes 1052672 | tf_op jit(solution)/shard_map/pick/pallas_call | solution.py:389
  10.2 1.3 %collective-permute-done.2.refs_1_ = f32[32,1024]{1,0:T(8,128)S(1)} collective-permute-done((f32[32,1024]{1,0:T(8,128)}, f32[32,1024]{1,0:T(8,128)S(1)}, u32[]{:S(2)}, u32[]{:S(2)}) %collective-permute-start.2) | collective-permute-done | bytes 131104 | tf_op jit(solution)/shard_map/ppermute | solution.py:69
  11.6 1.3 %collective-permute-done.4.refs_3_ = f32[32,1024]{1,0:T(8,128)S(1)} collective-permute-done((f32[32,1024]{1,0:T(8,128)}, f32[32,1024]{1,0:T(8,128)S(1)}, u32[]{:S(2)}, u32[]{:S(2)}) %collective-permute-start.4) | collective-permute-done | bytes 131104 | tf_op jit(solution)/shard_map/ppermute | solution.py:69
  13.0 1.6 %collective-permute-start.5 = (f32[64,1024]{1,0:T(8,128)S(1)}, f32[64,1024]{1,0:T(8,128)S(1)}, u32[]{:S(2)}, u32[]{:S(2)}) collective-permute-start(f32[64,1024]{1,0:T(8,128)S(1)} %get-tuple-element.76.refs_5_), channel_id=1, source_target_pairs={{0,1},{2,0},{4,2},{6,4},{7,6},{5,7},{3,5},{1,3},{8,9},{10,8},{12,1... | collective-permute-start | bytes 786440 | tf_op jit(solution)/shard_map/ppermute | solution.py:69
  15.0 0.5 collective-permute-start.8
  15.6 4.1 %collective-permute-done.5.refs_6_ = f32[64,1024]{1,0:T(8,128)S(1)} collective-permute-done((f32[64,1024]{1,0:T(8,128)S(1)}, f32[64,1024]{1,0:T(8,128)S(1)}, u32[]{:S(2)}, u32[]{:S(2)}) %collective-permute-start.5) | collective-permute-done | bytes 262176 | tf_op jit(solution)/shard_map/ppermute | solution.py:69
  19.7 1.3 %collective-permute-done.6.refs_7_.refs_10_ = f32[64,1024]{1,0:T(8,128)S(1)} collective-permute-done((f32[64,1024]{1,0:T(8,128)S(1)}, f32[64,1024]{1,0:T(8,128)S(1)}, u32[]{:S(2)}, u32[]{:S(2)}) %collective-permute-start.6) | collective-permute-done | bytes 262176 | tf_op jit(solution)/shard_map/ppermute | solution.py:69
  21.4 1.8 %collective-permute-start.13 = (f32[64,1024]{1,0:T(8,128)S(1)}, f32[64,1024]{1,0:T(8,128)S(1)}, u32[]{:S(2)}, u32[]{:S(2)}) collective-permute-start(f32[64,1024]{1,0:T(8,128)S(1)} %collective-permute-done.5.refs_6_), channel_id=1, source_target_pairs={{0,1},{2,0},{4,2},{6,4},{7,6},{5,7},{3,5},{1,3},{8,9},{10,8},{12,1... | collective-permute-start | bytes 786440 | tf_op jit(solution)/shard_map/ppermute | solution.py:69
  23.5 1.7 %early_back.1 = (f32[160,512]{1,0:T(8,128)S(1)}, bf16[512,1024]{1,0:T(8,128)(2,1)S(1)}, bf16[512,1024]{1,0:T(8,128)(2,1)S(1)}) custom-call(f32[128,1024]{1,0:T(8,128)S(1)} %bitcast.7, f32[128,1024]{1,0:T(8,128)S(1)} %collective-permute-done.refs_1_, f32[128,1024]{1,0:T(8,128)S(1)} %collective-permute-done.7.refs_2_, ...), custom_call_target="tpu_custom_call" | custom-call | flops 503316480 | bytes 5701632 | tf_op jit(solution)/shard_map/early_back/pallas_call | solution.py:389
  25.1 1.8 %collective-permute-start.10 = (f32[160,512]{1,0:T(8,128)S(1)}, f32[160,512]{1,0:T(8,128)S(1)}, u32[]{:S(2)}, u32[]{:S(2)}) collective-permute-start(f32[160,512]{1,0:T(8,128)S(1)} %get-tuple-element.82.refs_0_), channel_id=1, source_target_pairs={{0,16},{8,24},{16,0},{24,8},{1,17},{9,25},{17,1},{25,9},{2,18},{10... | collective-permute-start | bytes 983048 | tf_op jit(solution)/shard_map/ppermute | solution.py:27
  26.9 0.5 collective-permute-start.12
  27.4 2.8 %collective-permute-done.13.refs_0_.refs_7_ = f32[64,1024]{1,0:T(8,128)S(1)} collective-permute-done((f32[64,1024]{1,0:T(8,128)S(1)}, f32[64,1024]{1,0:T(8,128)S(1)}, u32[]{:S(2)}, u32[]{:S(2)}) %collective-permute-start.13) | collective-permute-done | bytes 262176 | tf_op jit(solution)/shard_map/ppermute | solution.py:69
  30.2 1.4 %collective-permute-done.14.refs_2_.refs_9_ = f32[64,1024]{1,0:T(8,128)S(1)} collective-permute-done((f32[64,1024]{1,0:T(8,128)S(1)}, f32[64,1024]{1,0:T(8,128)S(1)}, u32[]{:S(2)}, u32[]{:S(2)}) %collective-permute-start.14) | collective-permute-done | bytes 262176 | tf_op jit(solution)/shard_map/ppermute | solution.py:69
  32.0 1.9 %collective-permute-start.16 = (f32[32,1024]{1,0:T(8,128)S(1)}, f32[32,1024]{1,0:T(8,128)S(1)}, u32[]{:S(2)}, u32[]{:S(2)}) collective-permute-start(f32[32,1024]{1,0:T(8,128)S(1)} %slice.31), channel_id=1, source_target_pairs={{0,1},{2,0},{4,2},{6,4},{7,6},{5,7},{3,5},{1,3},{8,9},{10,8},{12,1... | collective-permute-start | bytes 393224 | tf_op jit(solution)/shard_map/ppermute | solution.py:69
  34.0 0.9 collective-permute-done.10.refs_2_
  34.8 1.8 %collective-permute-done.15.refs_1_ = f32[32,1024]{1,0:T(8,128)S(1)} collective-permute-done((f32[32,1024]{1,0:T(8,128)S(1)}, f32[32,1024]{1,0:T(8,128)S(1)}, u32[]{:S(2)}, u32[]{:S(2)}) %collective-permute-start.15) | collective-permute-done | bytes 131104 | tf_op jit(solution)/shard_map/ppermute | solution.py:69
  36.6 1.1 %late_back.1.refs_4_ = f32[96,512]{1,0:T(8,128)S(1)} custom-call(bf16[512,1024]{1,0:T(8,128)(2,1)S(1)} %get-tuple-element.85.cotan_high, bf16[512,1024]{1,0:T(8,128)(2,1)S(1)} %get-tuple-element.86.cotan_low, f32[64,1024]{1,0:T(8,128)S(1)} %collective-permute-done.13.refs_0_.refs_7_, f32[32,1024]{1,0:T(8,128)S(1)} %collective-permute-done.15.refs_1_, ...), custom_call_target="tpu_custom_call" | custom-call | flops 301989888 | bytes 2949120 | tf_op jit(solution)/shard_map/late_back/pallas_call | solution.py:389
  37.7 1.6 %collective-permute-start.18 = (f32[96,512]{1,0:T(8,128)S(1)}, f32[96,512]{1,0:T(8,128)S(1)}, u32[]{:S(2)}, u32[]{:S(2)}) collective-permute-start(f32[96,512]{1,0:T(8,128)S(1)} %late_back.1.refs_4_), channel_id=1, source_target_pairs={{0,16},{8,24},{16,0},{24,8},{1,17},{9,25},{17,1},{25,9},{2,18},{10... | collective-permute-start | bytes 589832 | tf_op jit(solution)/shard_map/ppermute | solution.py:27
  39.3 2.0 %mid.1 = (f32[512,256]{1,0:T(8,128)S(1)}, bf16[256,1024]{1,0:T(8,128)(2,1)S(1)}, bf16[256,1024]{1,0:T(8,128)(2,1)S(1)}, bf16[512,1024]{1,0:T(8,128)(2,1)S(1)}, bf16[512,1024]{1,0:T(8,128)(2,1)S(1)}) custom-call(s32[1,1024]{1,0:T(1,128)S(1)} %bitcast.8, f32[256,256]{1,0:T(8,128)S(1)} %get-tuple-element.91.refs_0_.refs_8_, ...), custom_call_target="tpu_custom_call" | custom-call | flops 1073741824 | bytes 6557696 | tf_op jit(solution)/shard_map/mid/pallas_call | solution.py:389
  41.3 0.6 collective-permute-start.19
  41.9 1.6 %collective-permute-done.18.refs_6_ = f32[96,512]{1,0:T(8,128)S(1)} collective-permute-done((f32[96,512]{1,0:T(8,128)S(1)}, f32[96,512]{1,0:T(8,128)S(1)}, u32[]{:S(2)}, u32[]{:S(2)}) %collective-permute-start.18) | collective-permute-done | bytes 196640 | tf_op jit(solution)/shard_map/ppermute | solution.py:27
  43.5 0.7 across.1
  44.9 1.5 %collective-permute-start.24 = (f32[512,256]{1,0:T(8,128)S(1)}, f32[512,256]{1,0:T(8,128)S(1)}, u32[]{:S(2)}, u32[]{:S(2)}) collective-permute-start(f32[512,256]{1,0:T(8,128)S(1)} %add.27), channel_id=1, source_target_pairs={{0,16},{8,24},{16,0},{24,8},{1,17},{9,25},{17,1},{25,9},{2,18},{10... | collective-permute-start | bytes 1572872 | tf_op jit(solution)/shard_map/ppermute | solution.py:27
  46.6 3.8 %grad_first.1 = (f32[32,1024]{1,0:T(8,128)S(1)}, f32[32,1024]{1,0:T(8,128)S(1)}, f32[32,1024]{1,0:T(8,128)S(1)}, f32[32,1024]{1,0:T(8,128)S(1)}, f32[32,1024]{1,...) custom-call(s32[1,1024]{1,0:T(1,128)S(1)} %bitcast.10, ...), custom_call_target="tpu_custom_call" | custom-call | flops 2952790016 | bytes 6295552 | tf_op jit(solution)/shard_map/grad_first/pallas_call | solution.py:389
  50.4 1.3 %rest.1 = (f32[512,256]{1,0:T(8,128)S(1)}, f32[512,256]{1,0:T(8,128)S(1)}) custom-call(s32[1,1024]{1,0:T(1,128)S(1)} %bitcast.11, bf16[512,1024]{1,0:T(8,128)(2,1)S(1)} %get-tuple-element.99.mid_high, bf16[512,1024]{1,0:T(8,128)(2,1)S(1)} %get-tuple-element.100.mid_low), custom_call_target="tpu_custom_call" | custom-call | flops 536870912 | bytes 3149824 | tf_op jit(solution)/shard_map/rest/pallas_call | solution.py:389
  51.9 1.1 %grad_stem.1 = (f32[512,128]{1,0:T(8,128)S(1)}, f32[512,128]{1,0:T(8,128)S(1)}) custom-call(bf16[256,1024]{1,0:T(8,128)(2,1)S(1)} %get-tuple-element.96.branch_high, bf16[256,1024]{1,0:T(8,128)(2,1)S(1)} %get-tuple-element.97.branch_low, bf16[1024,512]{1,0:T(8,128)(2,1)S(1)} %get-tuple-element.104.turned_high, ...), custom_call_target="tpu_custom_call" | custom-call | flops 805306368 | bytes 3670016 | tf_op jit(solution)/shard_map/grad_stem/pallas_call | solution.py:389
  53.0 6.2 %collective-permute-done.24.far_ref = f32[512,256]{1,0:T(8,128)S(1)} collective-permute-done((f32[512,256]{1,0:T(8,128)S(1)}, f32[512,256]{1,0:T(8,128)S(1)}, u32[]{:S(2)}, u32[]{:S(2)}) %collective-permute-start.24) | collective-permute-done | bytes 524320 | tf_op jit(solution)/shard_map/ppermute | solution.py:27
  59.2 1.1 %grad_second.1 = (f32[64,1024]{1,0:T(8,128)S(1)}, f32[64,1024]{1,0:T(8,128)S(1)}, f32[64,1024]{1,0:T(8,128)S(1)}, f32[64,1024]{1,0:T(8,128)S(1)}, f32[64,1024]{1...) custom-call(f32[512,256]{1,0:T(8,128)S(1)} %get-tuple-element.111.near_ref, ...), custom_call_target="tpu_custom_call" | custom-call | flops 805306368 | bytes 6815744 | tf_op jit(solution)/shard_map/grad_second/pallas_call | solution.py:389
  60.4 1.6 %collective-permute-start.26 = (f32[32,1024]{1,0:T(8,128)S(1)}, f32[32,1024]{1,0:T(8,128)S(1)}, u32[]{:S(2)}, u32[]{:S(2)}) collective-permute-start(f32[32,1024]{1,0:T(8,128)S(1)} %get-tuple-element.145), channel_id=1, source_target_pairs={{0,1},{2,0},{4,2},{6,4},{7,6},{5,7},{3,5},{1,3},{8,9},{10,8},{12,1... | collective-permute-start | bytes 393224 | tf_op jit(solution)/shard_map/ppermute | solution.py:69
  62.5 3.0 %collective-permute-done.26 = f32[32,1024]{1,0:T(8,128)S(1)} collective-permute-done((f32[32,1024]{1,0:T(8,128)S(1)}, f32[32,1024]{1,0:T(8,128)S(1)}, u32[]{:S(2)}, u32[]{:S(2)}) %collective-permute-start.26) | collective-permute-done | bytes 131104 | tf_op jit(solution)/shard_map/ppermute | solution.py:69
  65.5 1.5 %collective-permute-done.25 = f32[32,1024]{1,0:T(8,128)S(1)} collective-permute-done((f32[32,1024]{1,0:T(8,128)S(1)}, f32[32,1024]{1,0:T(8,128)S(1)}, u32[]{:S(2)}, u32[]{:S(2)}) %collective-permute-start.25) | collective-permute-done | bytes 131104 | tf_op jit(solution)/shard_map/ppermute | solution.py:69
  67.6 1.6 %collective-permute-start.29 = (f32[64,1024]{1,0:T(8,128)S(1)}, f32[64,1024]{1,0:T(8,128)S(1)}, u32[]{:S(2)}, u32[]{:S(2)}) collective-permute-start(f32[64,1024]{1,0:T(8,128)S(1)} %get-tuple-element.131), channel_id=1, source_target_pairs={{0,1},{2,0},{4,2},{6,4},{7,6},{5,7},{3,5},{1,3},{8,9},{10,8},{12,1... | collective-permute-start | bytes 786440 | tf_op jit(solution)/shard_map/ppermute | solution.py:69
  69.1 1.5 %collective-permute-start.32 = (f32[512,128]{1,0:T(8,128)S(1)}, f32[512,128]{1,0:T(8,128)S(1)}, u32[]{:S(2)}, u32[]{:S(2)}) collective-permute-start(f32[512,128]{1,0:T(8,128)S(1)} %get-tuple-element.133), channel_id=1, source_target_pairs={{0,16},{8,24},{16,0},{24,8},{1,17},{9,25},{17,1},{25,9},{2,18},{10... | collective-permute-start | bytes 786440 | tf_op jit(solution)/shard_map/ppermute | solution.py:27
  70.6 3.2 %collective-permute-done.27 = f32[64,1024]{1,0:T(8,128)S(1)} collective-permute-done((f32[64,1024]{1,0:T(8,128)S(1)}, f32[64,1024]{1,0:T(8,128)S(1)}, u32[]{:S(2)}, u32[]{:S(2)}) %collective-permute-start.27) | collective-permute-done | bytes 262176 | tf_op jit(solution)/shard_map/ppermute | solution.py:69
  74.4 1.6 %collective-permute-start.30 = (f32[64,1024]{1,0:T(8,128)S(1)}, f32[64,1024]{1,0:T(8,128)S(1)}, u32[]{:S(2)}, u32[]{:S(2)}) collective-permute-start(f32[64,1024]{1,0:T(8,128)S(1)} %add.32), channel_id=1, source_target_pairs={{0,1},{2,0},{4,2},{6,4},{7,6},{5,7},{3,5},{1,3},{8,9},{10,8},{12,1... | collective-permute-start | bytes 786440 | tf_op jit(solution)/shard_map/ppermute | solution.py:69
  76.1 0.5 collective-permute-start.33
  76.6 3.7 %collective-permute-done.28 = f32[64,1024]{1,0:T(8,128)S(1)} collective-permute-done((f32[64,1024]{1,0:T(8,128)S(1)}, f32[64,1024]{1,0:T(8,128)S(1)}, u32[]{:S(2)}, u32[]{:S(2)}) %collective-permute-start.28) | collective-permute-done | bytes 262176 | tf_op jit(solution)/shard_map/ppermute | solution.py:69
  80.9 0.6 collective-permute-start.34
  81.5 1.5 %collective-permute-start.35 = (f32[64,1024]{1,0:T(8,128)S(1)}, f32[64,1024]{1,0:T(8,128)S(1)}, u32[]{:S(2)}, u32[]{:S(2)}) collective-permute-start(f32[64,1024]{1,0:T(8,128)S(1)} %add.33), channel_id=1, source_target_pairs={{0,1},{2,0},{4,2},{6,4},{7,6},{5,7},{3,5},{1,3},{8,9},{10,8},{12,1... | collective-permute-start | bytes 786440 | tf_op jit(solution)/shard_map/ppermute | solution.py:69
  83.0 2.4 %place.1 = f32[128,1024]{1,0:T(8,128)} custom-call(s32[1,1024]{1,0:T(1,128)S(1)} %bitcast.14, f32[512,128]{1,0:T(8,128)S(1)} %get-tuple-element.134.refs_0_, f32[512,128]{1,0:T(8,128)S(1)} %collective-permute-done.31.refs_1_, f32[512,128]{1,0:T(8,128)S(1)} %collective-permute-done.32.refs_2_, f32[512,128]{1,0:T(8,128)S(1)} %collective-permute-done.33.refs_3_), custom_call_target="tpu_custom_call" | custom-call | flops 536870912 | bytes 1576960 | tf_op jit(solution)/shard_map/place/pallas_call | solution.py:389
  85.4 2.0 %collective-permute-done.34 = f32[64,1024]{1,0:T(8,128)S(1)} collective-permute-done((f32[64,1024]{1,0:T(8,128)S(1)}, f32[64,1024]{1,0:T(8,128)S(1)}, u32[]{:S(2)}, u32[]{:S(2)}) %collective-permute-start.34) | collective-permute-done | bytes 262176 | tf_op jit(solution)/shard_map/ppermute | solution.py:69
  87.9 0.7 fusion
  (60 shorter events, 5.9 us)
Async XLA Ops:
  0.6 7.1 %copy-start.5 = (s32[1024]{0:T(1024)S(1)}, s32[1024]{0:T(1024)}, u32[]{:S(2)}) copy-start(s32[1024]{0:T(1024)} %param.10) | copy-start | bytes 12292
  0.6 20.8 %collective-permute-start.7 = (f32[128,1024]{1,0:T(8,128)}, f32[128,1024]{1,0:T(8,128)S(1)}, u32[]{:S(2)}, u32[]{:S(2)}) collective-permute-start(f32[128,1024]{1,0:T(8,128)} %bitcast.5), channel_id=1, source_target_pairs={{0,16},{8,24},{16,0},{24,8},{1,17},{9,25},{17,1},{25,9},{2,18},{10... | collective-permute-start | bytes 1572872 | tf_op jit(solution)/shard_map/ppermute | solution.py:27
  3.6 6.5 %collective-permute-start.1 = (f32[32,1024]{1,0:T(8,128)}, f32[32,1024]{1,0:T(8,128)S(1)}, u32[]{:S(2)}, u32[]{:S(2)}) collective-permute-start(f32[32,1024]{1,0:T(8,128)} %refs_4_.3), channel_id=1, source_target_pairs={{0,1},{2,0},{4,2},{6,4},{7,6},{5,7},{3,5},{1,3},{8,9},{10,8},{12,1... | collective-permute-start | bytes 393224 | tf_op jit(solution)/shard_map/ppermute | solution.py:69
  5.2 6.4 %collective-permute-start.2 = (f32[32,1024]{1,0:T(8,128)}, f32[32,1024]{1,0:T(8,128)S(1)}, u32[]{:S(2)}, u32[]{:S(2)}) collective-permute-start(f32[32,1024]{1,0:T(8,128)} %refs_4_.3), channel_id=1, source_target_pairs={{0,2},{2,4},{4,6},{6,7},{7,5},{5,3},{3,1},{1,0},{8,10},{10,12},{12... | collective-permute-start | bytes 393224 | tf_op jit(solution)/shard_map/ppermute | solution.py:69
  5.7 6.0 %collective-permute-start.3 = (f32[32,1024]{1,0:T(8,128)}, f32[32,1024]{1,0:T(8,128)S(1)}, u32[]{:S(2)}, u32[]{:S(2)}) collective-permute-start(f32[32,1024]{1,0:T(8,128)} %refs_4_.2), channel_id=1, source_target_pairs={{0,1},{2,0},{4,2},{6,4},{7,6},{5,7},{3,5},{1,3},{8,9},{10,8},{12,1... | collective-permute-start | bytes 393224 | tf_op jit(solution)/shard_map/ppermute | solution.py:69
  7.2 5.7 %collective-permute-start.4 = (f32[32,1024]{1,0:T(8,128)}, f32[32,1024]{1,0:T(8,128)S(1)}, u32[]{:S(2)}, u32[]{:S(2)}) collective-permute-start(f32[32,1024]{1,0:T(8,128)} %refs_4_.2), channel_id=1, source_target_pairs={{0,2},{2,4},{4,6},{6,7},{7,5},{5,3},{3,1},{1,0},{8,10},{10,12},{12... | collective-permute-start | bytes 393224 | tf_op jit(solution)/shard_map/ppermute | solution.py:69
  7.7 1.0 %copy-start.3 = (f32[1,128,1024]{2,1,0:T(8,128)S(1)}, f32[1,128,1024]{2,1,0:T(8,128)}, u32[]{:S(2)}) copy-start(f32[1,128,1024]{2,1,0:T(8,128)} %param.6) | copy-start | bytes 1572868
  8.7 14.7 %copy-start.1 = (f32[32,1024]{1,0:T(8,128)S(1)}, f32[32,1024]{1,0:T(8,128)}, u32[]{:S(2)}) copy-start(f32[32,1024]{1,0:T(8,128)} %refs_4_.2) | copy-start | bytes 393220
  9.8 5.8 %copy-start = (f32[1,128,1024]{2,1,0:T(8,128)S(1)}, f32[1,128,1024]{2,1,0:T(8,128)}, u32[]{:S(2)}) copy-start(f32[1,128,1024]{2,1,0:T(8,128)} %param.7) | copy-start | bytes 1572868
  13.0 6.7 %collective-permute-start.5 = (f32[64,1024]{1,0:T(8,128)S(1)}, f32[64,1024]{1,0:T(8,128)S(1)}, u32[]{:S(2)}, u32[]{:S(2)}) collective-permute-start(f32[64,1024]{1,0:T(8,128)S(1)} %get-tuple-element.76.refs_5_), channel_id=1, source_target_pairs={{0,1},{2,0},{4,2},{6,4},{7,6},{5,7},{3,5},{1,3},{8,9},{10,8},{12,1... | collective-permute-start | bytes 786440 | tf_op jit(solution)/shard_map/ppermute | solution.py:69
  14.6 6.4 %collective-permute-start.6 = (f32[64,1024]{1,0:T(8,128)S(1)}, f32[64,1024]{1,0:T(8,128)S(1)}, u32[]{:S(2)}, u32[]{:S(2)}) collective-permute-start(f32[64,1024]{1,0:T(8,128)S(1)} %get-tuple-element.77.refs_8_.refs_11_), channel_id=1, source_target_pairs={{0,2},{2,4},{4,6},{6,7},{7,5},{5,3},{3,1},{1,0},{8,10},{10,12},{12... | collective-permute-start | bytes 786440 | tf_op jit(solution)/shard_map/ppermute | solution.py:69
  15.0 6.4 %collective-permute-start.8 = (f32[256,256]{1,0:T(8,128)S(1)}, f32[256,256]{1,0:T(8,128)S(1)}, u32[]{:S(2)}, u32[]{:S(2)}) collective-permute-start(f32[256,256]{1,0:T(8,128)S(1)} %get-tuple-element.79), channel_id=1, source_target_pairs={{0,16},{8,24},{16,0},{24,8},{1,17},{9,25},{17,1},{25,9},{2,18},{10... | collective-permute-start | bytes 786440 | tf_op jit(solution)/shard_map/ppermute | solution.py:27
  15.6 7.9 %collective-permute-start = (f32[128,1024]{1,0:T(8,128)S(1)}, f32[128,1024]{1,0:T(8,128)S(1)}, u32[]{:S(2)}, u32[]{:S(2)}) collective-permute-start(f32[128,1024]{1,0:T(8,128)S(1)} %bitcast.6), channel_id=1, source_target_pairs={{0,8},{8,0},{16,24},{24,16},{1,9},{9,1},{17,25},{25,17},{2,10},{10... | collective-permute-start | bytes 1572872 | tf_op jit(solution)/shard_map/ppermute | solution.py:27
  21.4 2.0 %collective-permute-start.9 = (f32[128,1024]{1,0:T(8,128)S(1)}, f32[128,1024]{1,0:T(8,128)S(1)}, u32[]{:S(2)}, u32[]{:S(2)}) collective-permute-start(f32[128,1024]{1,0:T(8,128)S(1)} %collective-permute-done.7.refs_2_), channel_id=1, source_target_pairs={{0,8},{8,0},{16,24},{24,16},{1,9},{9,1},{17,25},{25,17},{2,10},{10... | collective-permute-start | bytes 1572872 | tf_op jit(solution)/shard_map/ppermute | solution.py:27
  21.4 8.8 %collective-permute-start.13 = (f32[64,1024]{1,0:T(8,128)S(1)}, f32[64,1024]{1,0:T(8,128)S(1)}, u32[]{:S(2)}, u32[]{:S(2)}) collective-permute-start(f32[64,1024]{1,0:T(8,128)S(1)} %collective-permute-done.5.refs_6_), channel_id=1, source_target_pairs={{0,1},{2,0},{4,2},{6,4},{7,6},{5,7},{3,5},{1,3},{8,9},{10,8},{12,1... | collective-permute-start | bytes 786440 | tf_op jit(solution)/shard_map/ppermute | solution.py:69
  23.2 8.4 %collective-permute-start.14 = (f32[64,1024]{1,0:T(8,128)S(1)}, f32[64,1024]{1,0:T(8,128)S(1)}, u32[]{:S(2)}, u32[]{:S(2)}) collective-permute-start(f32[64,1024]{1,0:T(8,128)S(1)} %collective-permute-done.6.refs_7_.refs_10_), channel_id=1, source_target_pairs={{0,2},{2,4},{4,6},{6,7},{7,5},{5,3},{3,1},{1,0},{8,10},{10,12},{12... | collective-permute-start | bytes 786440 | tf_op jit(solution)/shard_map/ppermute | solution.py:69
  25.1 9.7 %collective-permute-start.10 = (f32[160,512]{1,0:T(8,128)S(1)}, f32[160,512]{1,0:T(8,128)S(1)}, u32[]{:S(2)}, u32[]{:S(2)}) collective-permute-start(f32[160,512]{1,0:T(8,128)S(1)} %get-tuple-element.82.refs_0_), channel_id=1, source_target_pairs={{0,16},{8,24},{16,0},{24,8},{1,17},{9,25},{17,1},{25,9},{2,18},{10... | collective-permute-start | bytes 983048 | tf_op jit(solution)/shard_map/ppermute | solution.py:27
  26.9 7.0 %collective-permute-start.11 = (f32[256,256]{1,0:T(8,128)S(1)}, f32[256,256]{1,0:T(8,128)S(1)}, u32[]{:S(2)}, u32[]{:S(2)}) collective-permute-start(f32[256,256]{1,0:T(8,128)S(1)} %get-tuple-element.91.refs_0_.refs_8_), channel_id=1, source_target_pairs={{0,8},{8,0},{16,24},{24,16},{1,9},{9,1},{17,25},{25,17},{2,10},{10... | collective-permute-start | bytes 786440 | tf_op jit(solution)/shard_map/ppermute | solution.py:27
  26.9 7.0 %collective-permute-start.12 = (f32[256,256]{1,0:T(8,128)S(1)}, f32[256,256]{1,0:T(8,128)S(1)}, u32[]{:S(2)}, u32[]{:S(2)}) collective-permute-start(f32[256,256]{1,0:T(8,128)S(1)} %collective-permute-done.8.refs_2_.refs_10_), channel_id=1, source_target_pairs={{0,8},{8,0},{16,24},{24,16},{1,9},{9,1},{17,25},{25,17},{2,10},{10... | collective-permute-start | bytes 786440 | tf_op jit(solution)/shard_map/ppermute | solution.py:27
  31.6 5.0 %collective-permute-start.15 = (f32[32,1024]{1,0:T(8,128)S(1)}, f32[32,1024]{1,0:T(8,128)S(1)}, u32[]{:S(2)}, u32[]{:S(2)}) collective-permute-start(f32[32,1024]{1,0:T(8,128)S(1)} %slice.30), channel_id=1, source_target_pairs={{0,2},{2,4},{4,6},{6,7},{7,5},{5,3},{3,1},{1,0},{8,10},{10,12},{12... | collective-permute-start | bytes 393224 | tf_op jit(solution)/shard_map/ppermute | solution.py:69
  32.0 7.3 %collective-permute-start.16 = (f32[32,1024]{1,0:T(8,128)S(1)}, f32[32,1024]{1,0:T(8,128)S(1)}, u32[]{:S(2)}, u32[]{:S(2)}) collective-permute-start(f32[32,1024]{1,0:T(8,128)S(1)} %slice.31), channel_id=1, source_target_pairs={{0,1},{2,0},{4,2},{6,4},{7,6},{5,7},{3,5},{1,3},{8,9},{10,8},{12,1... | collective-permute-start | bytes 393224 | tf_op jit(solution)/shard_map/ppermute | solution.py:69
  36.6 2.7 %copy-start.2 = (s32[1024]{0:T(1024)S(1)}, s32[1024]{0:T(1024)}, u32[]{:S(2)}) copy-start(s32[1024]{0:T(1024)} %param.11) | copy-start | bytes 12292
  36.6 2.7 %copy-start.4 = (f32[32,1024]{1,0:T(8,128)S(1)}, f32[32,1024]{1,0:T(8,128)}, u32[]{:S(2)}) copy-start(f32[32,1024]{1,0:T(8,128)} %refs_4_.3) | copy-start | bytes 393220
  37.7 5.7 %collective-permute-start.18 = (f32[96,512]{1,0:T(8,128)S(1)}, f32[96,512]{1,0:T(8,128)S(1)}, u32[]{:S(2)}, u32[]{:S(2)}) collective-permute-start(f32[96,512]{1,0:T(8,128)S(1)} %late_back.1.refs_4_), channel_id=1, source_target_pairs={{0,16},{8,24},{16,0},{24,8},{1,17},{9,25},{17,1},{25,9},{2,18},{10... | collective-permute-start | bytes 589832 | tf_op jit(solution)/shard_map/ppermute | solution.py:27
  39.3 7.1 %collective-permute-start.17 = (f32[160,512]{1,0:T(8,128)S(1)}, f32[160,512]{1,0:T(8,128)S(1)}, u32[]{:S(2)}, u32[]{:S(2)}) collective-permute-start(f32[160,512]{1,0:T(8,128)S(1)} %get-tuple-element.82.refs_0_), channel_id=1, source_target_pairs={{0,8},{8,0},{16,24},{24,16},{1,9},{9,1},{17,25},{25,17},{2,10},{10... | collective-permute-start | bytes 983048 | tf_op jit(solution)/shard_map/ppermute | solution.py:27
  41.3 2.9 %collective-permute-start.19 = (f32[512,256]{1,0:T(8,128)S(1)}, f32[512,256]{1,0:T(8,128)S(1)}, u32[]{:S(2)}, u32[]{:S(2)}) collective-permute-start(f32[512,256]{1,0:T(8,128)S(1)} %get-tuple-element.101), channel_id=1, source_target_pairs={{0,8},{8,0},{16,24},{24,16},{1,9},{9,1},{17,25},{25,17},{2,10},{10... | collective-permute-start | bytes 1572872 | tf_op jit(solution)/shard_map/ppermute | solution.py:27
  44.3 2.3 %collective-permute-start.20 = (f32[160,512]{1,0:T(8,128)S(1)}, f32[160,512]{1,0:T(8,128)S(1)}, u32[]{:S(2)}, u32[]{:S(2)}) collective-permute-start(f32[160,512]{1,0:T(8,128)S(1)} %collective-permute-done.10.refs_2_), channel_id=1, source_target_pairs={{0,8},{8,0},{16,24},{24,16},{1,9},{9,1},{17,25},{25,17},{2,10},{10... | collective-permute-start | bytes 983048 | tf_op jit(solution)/shard_map/ppermute | solution.py:27
  44.4 2.1 %collective-permute-start.21 = (f32[96,512]{1,0:T(8,128)S(1)}, f32[96,512]{1,0:T(8,128)S(1)}, u32[]{:S(2)}, u32[]{:S(2)}) collective-permute-start(f32[96,512]{1,0:T(8,128)S(1)} %late_back.1.refs_4_), channel_id=1, source_target_pairs={{0,8},{8,0},{16,24},{24,16},{1,9},{9,1},{17,25},{25,17},{2,10},{10... | collective-permute-start | bytes 589832 | tf_op jit(solution)/shard_map/ppermute | solution.py:27
  44.9 1.7 %collective-permute-start.22 = (f32[96,512]{1,0:T(8,128)S(1)}, f32[96,512]{1,0:T(8,128)S(1)}, u32[]{:S(2)}, u32[]{:S(2)}) collective-permute-start(f32[96,512]{1,0:T(8,128)S(1)} %collective-permute-done.18.refs_6_), channel_id=1, source_target_pairs={{0,8},{8,0},{16,24},{24,16},{1,9},{9,1},{17,25},{25,17},{2,10},{10... | collective-permute-start | bytes 589832 | tf_op jit(solution)/shard_map/ppermute | solution.py:27
  44.9 14.3 %collective-permute-start.24 = (f32[512,256]{1,0:T(8,128)S(1)}, f32[512,256]{1,0:T(8,128)S(1)}, u32[]{:S(2)}, u32[]{:S(2)}) collective-permute-start(f32[512,256]{1,0:T(8,128)S(1)} %add.27), channel_id=1, source_target_pairs={{0,16},{8,24},{16,0},{24,8},{1,17},{9,25},{17,1},{25,9},{2,18},{10... | collective-permute-start | bytes 1572872 | tf_op jit(solution)/shard_map/ppermute | solution.py:27
  51.7 7.5 %collective-permute-start.23 = (f32[512,256]{1,0:T(8,128)S(1)}, f32[512,256]{1,0:T(8,128)S(1)}, u32[]{:S(2)}, u32[]{:S(2)}) collective-permute-start(f32[512,256]{1,0:T(8,128)S(1)} %get-tuple-element.112), channel_id=1, source_target_pairs={{0,8},{8,0},{16,24},{24,16},{1,9},{9,1},{17,25},{25,17},{2,10},{10... | collective-permute-start | bytes 1572872 | tf_op jit(solution)/shard_map/ppermute | solution.py:27
  60.4 5.1 %collective-permute-start.26 = (f32[32,1024]{1,0:T(8,128)S(1)}, f32[32,1024]{1,0:T(8,128)S(1)}, u32[]{:S(2)}, u32[]{:S(2)}) collective-permute-start(f32[32,1024]{1,0:T(8,128)S(1)} %get-tuple-element.145), channel_id=1, source_target_pairs={{0,1},{2,0},{4,2},{6,4},{7,6},{5,7},{3,5},{1,3},{8,9},{10,8},{12,1... | collective-permute-start | bytes 393224 | tf_op jit(solution)/shard_map/ppermute | solution.py:69
  62.0 5.0 %collective-permute-start.25 = (f32[32,1024]{1,0:T(8,128)S(1)}, f32[32,1024]{1,0:T(8,128)S(1)}, u32[]{:S(2)}, u32[]{:S(2)}) collective-permute-start(f32[32,1024]{1,0:T(8,128)S(1)} %get-tuple-element.146), channel_id=1, source_target_pairs={{0,2},{2,4},{4,6},{6,7},{7,5},{5,3},{3,1},{1,0},{8,10},{10,12},{12... | collective-permute-start | bytes 393224 | tf_op jit(solution)/shard_map/ppermute | solution.py:69
  67.1 6.8 %collective-permute-start.27 = (f32[64,1024]{1,0:T(8,128)S(1)}, f32[64,1024]{1,0:T(8,128)S(1)}, u32[]{:S(2)}, u32[]{:S(2)}) collective-permute-start(f32[64,1024]{1,0:T(8,128)S(1)} %get-tuple-element.128), channel_id=1, source_target_pairs={{0,2},{2,4},{4,6},{6,7},{7,5},{5,3},{3,1},{1,0},{8,10},{10,12},{12... | collective-permute-start | bytes 786440 | tf_op jit(solution)/shard_map/ppermute | solution.py:69
  67.6 6.8 %collective-permute-start.29 = (f32[64,1024]{1,0:T(8,128)S(1)}, f32[64,1024]{1,0:T(8,128)S(1)}, u32[]{:S(2)}, u32[]{:S(2)}) collective-permute-start(f32[64,1024]{1,0:T(8,128)S(1)} %get-tuple-element.131), channel_id=1, source_target_pairs={{0,1},{2,0},{4,2},{6,4},{7,6},{5,7},{3,5},{1,3},{8,9},{10,8},{12,1... | collective-permute-start | bytes 786440 | tf_op jit(solution)/shard_map/ppermute | solution.py:69
  69.1 6.9 %collective-permute-start.32 = (f32[512,128]{1,0:T(8,128)S(1)}, f32[512,128]{1,0:T(8,128)S(1)}, u32[]{:S(2)}, u32[]{:S(2)}) collective-permute-start(f32[512,128]{1,0:T(8,128)S(1)} %get-tuple-element.133), channel_id=1, source_target_pairs={{0,16},{8,24},{16,0},{24,8},{1,17},{9,25},{17,1},{25,9},{2,18},{10... | collective-permute-start | bytes 786440 | tf_op jit(solution)/shard_map/ppermute | solution.py:27
  73.9 6.4 %collective-permute-start.28 = (f32[64,1024]{1,0:T(8,128)S(1)}, f32[64,1024]{1,0:T(8,128)S(1)}, u32[]{:S(2)}, u32[]{:S(2)}) collective-permute-start(f32[64,1024]{1,0:T(8,128)S(1)} %add.30), channel_id=1, source_target_pairs={{0,2},{2,4},{4,6},{6,7},{7,5},{5,3},{3,1},{1,0},{8,10},{10,12},{12... | collective-permute-start | bytes 786440 | tf_op jit(solution)/shard_map/ppermute | solution.py:69
  74.4 6.4 %collective-permute-start.30 = (f32[64,1024]{1,0:T(8,128)S(1)}, f32[64,1024]{1,0:T(8,128)S(1)}, u32[]{:S(2)}, u32[]{:S(2)}) collective-permute-start(f32[64,1024]{1,0:T(8,128)S(1)} %add.32), channel_id=1, source_target_pairs={{0,1},{2,0},{4,2},{6,4},{7,6},{5,7},{3,5},{1,3},{8,9},{10,8},{12,1... | collective-permute-start | bytes 786440 | tf_op jit(solution)/shard_map/ppermute | solution.py:69
  76.1 4.8 %collective-permute-start.31 = (f32[512,128]{1,0:T(8,128)S(1)}, f32[512,128]{1,0:T(8,128)S(1)}, u32[]{:S(2)}, u32[]{:S(2)}) collective-permute-start(f32[512,128]{1,0:T(8,128)S(1)} %get-tuple-element.134.refs_0_), channel_id=1, source_target_pairs={{0,8},{8,0},{16,24},{24,16},{1,9},{9,1},{17,25},{25,17},{2,10},{10... | collective-permute-start | bytes 786440 | tf_op jit(solution)/shard_map/ppermute | solution.py:27
  76.1 4.8 %collective-permute-start.33 = (f32[512,128]{1,0:T(8,128)S(1)}, f32[512,128]{1,0:T(8,128)S(1)}, u32[]{:S(2)}, u32[]{:S(2)}) collective-permute-start(f32[512,128]{1,0:T(8,128)S(1)} %collective-permute-done.32.refs_2_), channel_id=1, source_target_pairs={{0,8},{8,0},{16,24},{24,16},{1,9},{9,1},{17,25},{25,17},{2,10},{10... | collective-permute-start | bytes 786440 | tf_op jit(solution)/shard_map/ppermute | solution.py:27
  80.9 6.4 %collective-permute-start.34 = (f32[64,1024]{1,0:T(8,128)S(1)}, f32[64,1024]{1,0:T(8,128)S(1)}, u32[]{:S(2)}, u32[]{:S(2)}) collective-permute-start(f32[64,1024]{1,0:T(8,128)S(1)} %add.31), channel_id=1, source_target_pairs={{0,2},{2,4},{4,6},{6,7},{7,5},{5,3},{3,1},{1,0},{8,10},{10,12},{12... | collective-permute-start | bytes 786440 | tf_op jit(solution)/shard_map/ppermute | solution.py:69
  81.5 6.4 %collective-permute-start.35 = (f32[64,1024]{1,0:T(8,128)S(1)}, f32[64,1024]{1,0:T(8,128)S(1)}, u32[]{:S(2)}, u32[]{:S(2)}) collective-permute-start(f32[64,1024]{1,0:T(8,128)S(1)} %add.33), channel_id=1, source_target_pairs={{0,1},{2,0},{4,2},{6,4},{7,6},{5,7},{3,5},{1,3},{8,9},{10,8},{12,1... | collective-permute-start | bytes 786440 | tf_op jit(solution)/shard_map/ppermute | solution.py:69
